TPU v7x, 32 devices: a whole 2x2x4 slice. The times are simulated.
32 devices in a mesh: fs: 8 (over y, x, core), tp: 4 (over z).
Axes of the slice: x: 2, y: 2, z: 4, core: 2. Of those that a mesh axis runs over, the one named last changes fastest.
Arguments:
- tokens: bfloat16 [2048, 2048], P('fs'), may hold values from -6 to 6
- cotangent: bfloat16 [2048, 2048], P('fs'), may hold values from -6 to 6
- qkv_weight: bfloat16 [3, 2048, 2048], P(None, 'fs', 'tp'), may hold values from -0.125 to 0.125
- out_weight: bfloat16 [2048, 2048], P('tp', 'fs'), may hold values from -1.5 to 1.5
- norm_gains: bfloat16 [2, 2048], P(None, 'fs'), may hold values from 0.5 to 1.5
- router_weight: bfloat16 [8, 2048], P(None, 'fs'), may hold values from -0.0625 to 0.0625
- shared_gate: bfloat16 [2048], P('fs'), may hold values from -0.125 to 0.125
- expert_gate_up: bfloat16 [8, 2048, 2, 1408], P(None, 'fs', None, 'tp'), may hold values from -0.125 to 0.125
- expert_down: bfloat16 [8, 1408, 2048], P(None, 'tp', 'fs'), may hold values from -0.625 to 0.625
- shared_gate_up: bfloat16 [2048, 2, 5632], P('fs', None, 'tp'), may hold values from -0.125 to 0.125
- shared_down: bfloat16 [5632, 2048], P('tp', 'fs'), may hold values from -0.15625 to 0.15625
- routes: int32 [2048, 4], P('fs'), may hold values from 0 to 7, all different within a row
- doc_start: int32 [2048], P('fs'), may hold values from 0 to 1023, as said below
Outputs:
- output: bfloat16 [2048, 2048], P('fs', 'tp')
- input_grad: float32 [2048, 2048], P('fs')
- grad_qkv_weight: float32 [3, 2048, 2048], P(None, 'fs', 'tp')
- grad_out_weight: float32 [2048, 2048], P('tp', 'fs')
- grad_norm_gains: float32 [2, 2048], P(None, 'fs')
- grad_router_weight: float32 [8, 2048], P(None, 'fs')
- grad_shared_gate: float32 [2048], P('fs')
- grad_expert_gate_up: float32 [8, 2048, 2, 1408], P(None, 'fs', None, 'tp')
- grad_expert_down: float32 [8, 1408, 2048], P(None, 'tp', 'fs')
- grad_shared_gate_up: float32 [2048, 2, 5632], P('fs', None, 'tp')
- grad_shared_down: float32 [5632, 2048], P('tp', 'fs')
Inputs may be any that keep to these rules, and one draw needn't show every extreme that they name: `routes`: each token names 4 different experts; every expert is named by some token. `doc_start`: every sequence holds three documents; the second begins within the first 128 positions and ends within the last 128.
All inputs are finite; a program needn't handle non-finite values.
Results may differ from a plain program's by a relative error of at most 0.029.
Values may be sent and summed in bfloat16 or wider, within the bound.
A program may use at most 320 MiB of HBM per device.

v0:
```python
import math

import jax
import jax.numpy as jnp
from jax import lax
from jax.sharding import PartitionSpec as P

HD = 128
E = 8
SEQ_DEV = 128


NORM_EPS = 1e-06
NEG_FILL = -1e30
ROPE_BASE = 1000000.0


def rope_tables(positions):
    half_size = HD // 2
    frequency = ROPE_BASE ** (-(jnp.arange(half_size, dtype=jnp.float32) * 2.0 / HD))
    angles = positions.astype(jnp.float32)[:, None] * frequency[None, :]
    return (jnp.cos(angles), jnp.sin(angles))


def rotate(values, cosine, sine_table):
    shaped = values.reshape(values.shape[0], -1, HD)
    half_size = HD // 2
    first_half = shaped[..., :half_size]
    second_half = shaped[..., half_size:]
    cos_part = cosine[:, None, :]
    sin_part = sine_table[:, None, :]
    turned = jnp.concatenate(
        [
            first_half * cos_part - second_half * sin_part,
            second_half * cos_part + first_half * sin_part,
        ],
        axis=-1,
    )
    return turned.reshape(values.shape)


def key_mask(query_pos, query_start, first_dev, group_size):
    key_pos = (first_dev + jnp.arange(group_size, dtype=jnp.int32)[:, None]) * SEQ_DEV + jnp.arange(
        SEQ_DEV, dtype=jnp.int32
    )[None, :]
    key_pos = key_pos[None, None, :, :]
    return (key_pos <= query_pos[None, :, None, None]) & (key_pos >= query_start[:, :, None, None])


def shards(
    tokens,
    cotangent,
    qkv_weight,
    out_weight,
    norm_gains,
    router_weight,
    shared_gate,
    expert_gate_up,
    expert_down,
    shared_gate_up,
    shared_down,
    routes,
    doc_start,
):
    tok_rows = tokens.shape[0]
    seq_count = tok_rows // SEQ_DEV
    local_width = qkv_weight.shape[2]
    head_count = local_width // HD
    out_width = tokens.shape[1] // lax.axis_size("tp")
    score_scale = HD ** (-0.5)
    fs_index = lax.axis_index("fs")
    tp_index = lax.axis_index("tp")
    query_pos = fs_index * SEQ_DEV + jnp.arange(SEQ_DEV, dtype=jnp.int32)
    positions = jnp.tile(query_pos, seq_count)
    query_start = doc_start.reshape(seq_count, SEQ_DEV)
    cosine, sine_table = rope_tables(positions)
    group_limit = max(1, 512 // SEQ_DEV)
    qkv_full, out_full, gains_full, router_full, shared_gate_full = (
        lax.all_gather(qkv_weight, "fs", axis=1, tiled=True),
        lax.all_gather(out_weight, "fs", axis=1, tiled=True),
        lax.all_gather(norm_gains, "fs", axis=1, tiled=True),
        lax.all_gather(router_weight, "fs", axis=1, tiled=True),
        lax.all_gather(shared_gate, "fs", axis=0, tiled=True),
    )
    token_float = tokens.astype(jnp.float32)
    rstd_one = lax.rsqrt(jnp.mean(token_float * token_float, axis=1, keepdims=True) + NORM_EPS)
    normed_one = token_float * rstd_one
    hidden_one = (normed_one * gains_full[0].astype(jnp.float32)[None, :]).astype(jnp.bfloat16)
    projected = jnp.einsum("td,jdf->jtf", hidden_one, qkv_full, preferred_element_type=jnp.float32)
    query_rows = rotate(projected[0], cosine, sine_table).astype(jnp.bfloat16)
    key_own = rotate(projected[1], cosine, sine_table).astype(jnp.bfloat16)
    value_own = projected[2].astype(jnp.bfloat16)
    query_heads = query_rows.reshape(seq_count, SEQ_DEV, head_count, HD)

    def score_block(key_group, first_dev):
        allowed = key_mask(query_pos, query_start, first_dev, key_group.shape[0])[:, None]
        scores = (
            jnp.einsum(
                "pqhd,gpkhd->phqgk", query_heads, key_group, preferred_element_type=jnp.float32
            )
            * score_scale
        )
        return (jnp.where(allowed, scores, NEG_FILL), allowed)

    def forward_update(running, key_group, value_group, first_dev):
        run_max, run_sum, accumulated = running
        scores, allowed = score_block(key_group, first_dev)
        new_max = jnp.maximum(run_max, jnp.max(scores, axis=(3, 4)))
        weights = jnp.where(allowed, jnp.exp(scores - new_max[..., None, None]), 0.0)
        factor = jnp.exp(run_max - new_max)
        new_sum = run_sum * factor + jnp.sum(weights, axis=(3, 4))
        mixed_part = jnp.einsum(
            "phqgk,gpkhd->pqhd",
            weights.astype(jnp.bfloat16),
            value_group,
            preferred_element_type=jnp.float32,
        )
        new_accum = accumulated * jnp.transpose(factor, (0, 2, 1))[..., None] + mixed_part
        return (new_max, new_sum, new_accum)

    initial = (
        jnp.full((seq_count, head_count, SEQ_DEV), NEG_FILL, jnp.float32),
        jnp.zeros((seq_count, head_count, SEQ_DEV), jnp.float32),
        jnp.zeros((seq_count, SEQ_DEV, head_count, HD), jnp.float32),
    )
    running = initial
    key_piece = lax.all_gather(key_own, "fs", axis=0, tiled=True)
    value_piece = lax.all_gather(value_own, "fs", axis=0, tiled=True)
    shard_count = key_piece.shape[0] // tok_rows
    group_size = math.gcd(shard_count, group_limit)
    step_count = shard_count // group_size
    shaped = (step_count, group_size, seq_count, SEQ_DEV, head_count, HD)
    first_dev = jnp.int32(0) // tok_rows

    def one_step(carried, inputs):
        key_group, value_group, group_index = inputs
        start_dev = group_index * group_size
        updated = lax.cond(
            start_dev <= fs_index,
            lambda state_in: forward_update(state_in, key_group, value_group, start_dev),
            lambda state_in: state_in,
            carried,
        )
        return (updated, None)

    running, ignored = lax.scan(
        one_step,
        running,
        (
            key_piece.reshape(shaped),
            value_piece.reshape(shaped),
            jnp.arange(step_count, dtype=jnp.int32),
        ),
    )
    run_max, run_sum, accumulated = running
    attended_heads = (accumulated / jnp.transpose(run_sum, (0, 2, 1))[..., None]).astype(
        jnp.bfloat16
    )
    log_total = run_max + jnp.log(run_sum)
    attended = attended_heads.reshape(tok_rows, local_width)
    branch_part = jnp.dot(attended, out_full, preferred_element_type=jnp.float32)
    branch = lax.psum(branch_part.astype(jnp.bfloat16), "tp").astype(jnp.float32)
    residual = token_float + branch
    rstd_two = lax.rsqrt(jnp.mean(residual * residual, axis=1, keepdims=True) + NORM_EPS)
    normed_two = residual * rstd_two
    hidden_two = (normed_two * gains_full[1].astype(jnp.float32)[None, :]).astype(jnp.bfloat16)
    expert_gate_all, expert_down_all, shared_up_all, shared_down_all = (
        lax.all_gather(expert_gate_up, "fs", axis=1, tiled=True),
        lax.all_gather(expert_down, "fs", axis=2, tiled=True),
        lax.all_gather(shared_gate_up, "fs", axis=0, tiled=True),
        lax.all_gather(shared_down, "fs", axis=1, tiled=True),
    )
    logits = jnp.einsum("td,ed->te", hidden_two, router_full, preferred_element_type=jnp.float32)
    router_probs = jax.nn.softmax(logits, axis=-1)
    chosen = jnp.sum(
        (routes[:, :, None] == jnp.arange(E, dtype=jnp.int32)[None, None, :]).astype(jnp.float32),
        axis=1,
    )
    gate_weights = router_probs * chosen
    gate_up = jnp.einsum(
        "td,edkf->tekf", hidden_two, expert_gate_all, preferred_element_type=jnp.float32
    )
    gate_part = gate_up[:, :, 0]
    up_part = gate_up[:, :, 1]
    gate_sigmoid = jax.nn.sigmoid(gate_part)
    active = gate_part * gate_sigmoid * up_part
    hidden = (gate_weights[:, :, None] * active).astype(jnp.bfloat16)
    shared_in = jnp.einsum(
        "td,dkf->tkf", hidden_two, shared_up_all, preferred_element_type=jnp.float32
    )
    shared_gate_in = shared_in[:, 0]
    shared_up_in = shared_in[:, 1]
    shared_sigmoid = jax.nn.sigmoid(shared_gate_in)
    shared_active = shared_gate_in * shared_sigmoid * shared_up_in
    gate_logit = jnp.einsum(
        "td,d->t", hidden_two, shared_gate_full, preferred_element_type=jnp.float32
    )
    gate_value = jax.nn.sigmoid(gate_logit)
    shared_hidden = (gate_value[:, None] * shared_active).astype(jnp.bfloat16)
    mixture_part = jnp.einsum(
        "tef,efd->td", hidden, expert_down_all, preferred_element_type=jnp.float32
    ) + jnp.dot(shared_hidden, shared_down_all, preferred_element_type=jnp.float32)
    mixture = lax.psum_scatter(
        mixture_part.astype(jnp.bfloat16), "tp", scatter_dimension=1, tiled=True
    ).astype(jnp.float32)
    output = (
        lax.dynamic_slice_in_dim(residual, tp_index * out_width, out_width, 1) + mixture
    ).astype(jnp.bfloat16)
    qkv_back, out_back, gains_back, router_back, shared_gate_back = (
        lax.all_gather(qkv_weight, "fs", axis=1, tiled=True),
        lax.all_gather(out_weight, "fs", axis=1, tiled=True),
        lax.all_gather(norm_gains, "fs", axis=1, tiled=True),
        lax.all_gather(router_weight, "fs", axis=1, tiled=True),
        lax.all_gather(shared_gate, "fs", axis=0, tiled=True),
    )
    expert_gate_back, expert_down_back, shared_up_back, shared_down_back = (
        lax.all_gather(expert_gate_up, "fs", axis=1, tiled=True),
        lax.all_gather(expert_down, "fs", axis=2, tiled=True),
        lax.all_gather(shared_gate_up, "fs", axis=0, tiled=True),
        lax.all_gather(shared_down, "fs", axis=1, tiled=True),
    )
    hidden_grad = jnp.einsum(
        "td,efd->tef", cotangent, expert_down_back, preferred_element_type=jnp.float32
    )
    expert_down_grad = jnp.einsum(
        "tef,td->efd", hidden, cotangent, preferred_element_type=jnp.float32
    )
    shared_grad = jnp.einsum(
        "td,fd->tf", cotangent, shared_down_back, preferred_element_type=jnp.float32
    )
    shared_down_grad = jnp.einsum(
        "tf,td->fd", shared_hidden, cotangent, preferred_element_type=jnp.float32
    )
    gate_dot = jnp.sum(active * hidden_grad, axis=2)
    shared_dot = jnp.sum(shared_active * shared_grad, axis=1)
    active_grad = gate_weights[:, :, None] * hidden_grad
    gate_grad = active_grad * up_part * gate_sigmoid * (1.0 + gate_part * (1.0 - gate_sigmoid))
    up_grad = active_grad * gate_part * gate_sigmoid
    gate_up_grad = jnp.stack([gate_grad, up_grad], axis=2).astype(jnp.bfloat16)
    shared_active_grad = gate_value[:, None] * shared_grad
    shared_gate_grad = (
        shared_active_grad
        * shared_up_in
        * shared_sigmoid
        * (1.0 + shared_gate_in * (1.0 - shared_sigmoid))
    )
    shared_unit_grad = shared_active_grad * shared_gate_in * shared_sigmoid
    shared_up_grad = jnp.stack([shared_gate_grad, shared_unit_grad], axis=1).astype(jnp.bfloat16)
    expert_gate_grad = jnp.einsum(
        "td,tekf->edkf", hidden_two, gate_up_grad, preferred_element_type=jnp.float32
    )
    shared_proj_grad = jnp.einsum(
        "td,tkf->dkf", hidden_two, shared_up_grad, preferred_element_type=jnp.float32
    )
    input_part = jnp.einsum(
        "tekf,edkf->td", gate_up_grad, expert_gate_back, preferred_element_type=jnp.float32
    ) + jnp.einsum(
        "tkf,dkf->td", shared_up_grad, shared_up_back, preferred_element_type=jnp.float32
    )
    input_sum, gate_sum, shared_sum = (
        lax.psum(input_part.astype(jnp.bfloat16), "tp").astype(jnp.float32),
        lax.psum(gate_dot.astype(jnp.bfloat16), "tp").astype(jnp.float32),
        lax.psum(shared_dot.astype(jnp.bfloat16), "tp").astype(jnp.float32),
    )
    chosen_grad = chosen * gate_sum
    logit_grad = (
        router_probs * (chosen_grad - jnp.sum(router_probs * chosen_grad, axis=1, keepdims=True))
    ).astype(jnp.bfloat16)
    gate_logit_grad = (shared_sum * gate_value * (1.0 - gate_value)).astype(jnp.bfloat16)
    router_grad = jnp.einsum(
        "te,td->ed", logit_grad, hidden_two, preferred_element_type=jnp.float32
    )
    shared_vector_grad = jnp.einsum(
        "t,td->d", gate_logit_grad, hidden_two, preferred_element_type=jnp.float32
    )
    two_grad = (
        input_sum
        + jnp.einsum("te,ed->td", logit_grad, router_back, preferred_element_type=jnp.float32)
        + gate_logit_grad.astype(jnp.float32)[:, None]
        * shared_gate_back.astype(jnp.float32)[None, :]
    )
    scaled_two = two_grad * gains_back[1].astype(jnp.float32)[None, :]
    gain_two_grad = jnp.sum(two_grad * normed_two, axis=0)
    residual_grad = cotangent.astype(jnp.float32) + rstd_two * (
        scaled_two - normed_two * jnp.mean(scaled_two * normed_two, axis=1, keepdims=True)
    )
    branch_grad = residual_grad.astype(jnp.bfloat16)
    out_grad = jnp.einsum("tf,td->fd", attended, branch_grad, preferred_element_type=jnp.float32)
    attended_grad = jnp.einsum(
        "td,fd->tf", branch_grad, out_back, preferred_element_type=jnp.float32
    ).astype(jnp.bfloat16)
    grad_heads = attended_grad.reshape(seq_count, SEQ_DEV, head_count, HD)
    delta_rows = jnp.einsum(
        "pqhd,pqhd->phq", grad_heads, attended_heads, preferred_element_type=jnp.float32
    )
    key_all, value_all = (
        lax.all_gather(key_own, "fs", axis=0, tiled=True),
        lax.all_gather(value_own, "fs", axis=0, tiled=True),
    )
    device_count = key_all.shape[0] // tok_rows
    back_group = math.gcd(device_count, group_limit)
    back_steps = device_count // back_group
    back_shape = (back_steps, back_group, seq_count, SEQ_DEV, head_count, HD)

    def backward_update(key_group, value_group, start_dev):
        scores, allowed = score_block(key_group, start_dev)
        probs_block = jnp.where(allowed, jnp.exp(scores - log_total[..., None, None]), 0.0)
        weights_grad = jnp.einsum(
            "pqhd,gpkhd->phqgk", grad_heads, value_group, preferred_element_type=jnp.float32
        )
        score_grad = (probs_block * (weights_grad - delta_rows[..., None, None])).astype(
            jnp.bfloat16
        )
        query_part = (
            jnp.einsum(
                "phqgk,gpkhd->pqhd", score_grad, key_group, preferred_element_type=jnp.float32
            )
            * score_scale
        )
        key_part = (
            jnp.einsum(
                "phqgk,pqhd->gpkhd", score_grad, query_heads, preferred_element_type=jnp.float32
            )
            * score_scale
        )
        value_part = jnp.einsum(
            "phqgk,pqhd->gpkhd",
            probs_block.astype(jnp.bfloat16),
            grad_heads,
            preferred_element_type=jnp.float32,
        )
        return (query_part, key_part, value_part)

    empty_grads = (
        jnp.zeros((seq_count, SEQ_DEV, head_count, HD), jnp.float32),
        jnp.zeros((back_group, seq_count, SEQ_DEV, head_count, HD), jnp.float32),
        jnp.zeros((back_group, seq_count, SEQ_DEV, head_count, HD), jnp.float32),
    )
    scan_inputs = (
        key_all.reshape(back_shape),
        value_all.reshape(back_shape),
        jnp.arange(back_steps, dtype=jnp.int32),
    )

    def back_step(query_acc, inputs):
        key_group, value_group, group_index = inputs
        start_dev = group_index * back_group
        query_part, key_part, value_part = lax.cond(
            start_dev <= fs_index,
            lambda ignored_in: backward_update(key_group, value_group, start_dev),
            lambda ignored_in: empty_grads,
            key_group,
        )
        term_rows = jnp.concatenate(
            [
                key_part.reshape(back_group * tok_rows, local_width),
                value_part.reshape(back_group * tok_rows, local_width),
            ],
            axis=1,
        )
        return (query_acc + query_part, term_rows)

    query_grad, key_value_terms = lax.scan(back_step, empty_grads[0], scan_inputs)
    key_value_sum = lax.psum_scatter(
        key_value_terms.reshape(device_count * tok_rows, 2 * local_width).astype(jnp.bfloat16),
        "fs",
        scatter_dimension=0,
        tiled=True,
    ).astype(jnp.float32)
    key_grad_rows = key_value_sum[:, :local_width]
    value_grad_rows = key_value_sum[:, local_width:]
    projected_grad = jnp.stack(
        [
            rotate(query_grad.reshape(tok_rows, local_width), cosine, -sine_table),
            rotate(key_grad_rows, cosine, -sine_table),
            value_grad_rows,
        ],
        axis=0,
    ).astype(jnp.bfloat16)
    qkv_grad = jnp.einsum(
        "td,jtf->jdf", hidden_one, projected_grad, preferred_element_type=jnp.float32
    )
    one_part = jnp.einsum(
        "jtf,jdf->td", projected_grad, qkv_back, preferred_element_type=jnp.float32
    )
    one_grad = lax.psum(one_part.astype(jnp.bfloat16), "tp").astype(jnp.float32)
    scaled_one = one_grad * gains_back[0].astype(jnp.float32)[None, :]
    gain_one_grad = jnp.sum(one_grad * normed_one, axis=0)
    input_grad = residual_grad + rstd_one * (
        scaled_one - normed_one * jnp.mean(scaled_one * normed_one, axis=1, keepdims=True)
    )
    gains_grad = jnp.stack([gain_one_grad, gain_two_grad], axis=0)
    reduced = (
        lax.psum_scatter(
            qkv_grad.astype(jnp.bfloat16), "fs", scatter_dimension=1, tiled=True
        ).astype(jnp.float32),
        lax.psum_scatter(
            out_grad.astype(jnp.bfloat16), "fs", scatter_dimension=1, tiled=True
        ).astype(jnp.float32),
        lax.psum_scatter(
            gains_grad.astype(jnp.bfloat16), "fs", scatter_dimension=1, tiled=True
        ).astype(jnp.float32),
        lax.psum_scatter(
            router_grad.astype(jnp.bfloat16), "fs", scatter_dimension=1, tiled=True
        ).astype(jnp.float32),
        lax.psum_scatter(
            shared_vector_grad.astype(jnp.bfloat16), "fs", scatter_dimension=0, tiled=True
        ).astype(jnp.float32),
        lax.psum_scatter(
            expert_gate_grad.astype(jnp.bfloat16), "fs", scatter_dimension=1, tiled=True
        ).astype(jnp.float32),
        lax.psum_scatter(
            expert_down_grad.astype(jnp.bfloat16), "fs", scatter_dimension=2, tiled=True
        ).astype(jnp.float32),
        lax.psum_scatter(
            shared_proj_grad.astype(jnp.bfloat16), "fs", scatter_dimension=0, tiled=True
        ).astype(jnp.float32),
        lax.psum_scatter(
            shared_down_grad.astype(jnp.bfloat16), "fs", scatter_dimension=1, tiled=True
        ).astype(jnp.float32),
    )
    return (
        output,
        input_grad,
        reduced[0],
        reduced[1],
        reduced[2],
        reduced[3],
        reduced[4],
        reduced[5],
        reduced[6],
        reduced[7],
        reduced[8],
    )


def solution(mesh):
    return jax.shard_map(
        shards,
        mesh=mesh,
        in_specs=(
            P("fs", None),
            P("fs", None),
            P(None, "fs", "tp"),
            P("tp", "fs"),
            P(None, "fs"),
            P(None, "fs"),
            P("fs"),
            P(None, "fs", None, "tp"),
            P(None, "tp", "fs"),
            P("fs", None, "tp"),
            P("tp", "fs"),
            P("fs", None),
            P("fs"),
        ),
        out_specs=(
            P("fs", "tp"),
            P("fs", None),
            P(None, "fs", "tp"),
            P("tp", "fs"),
            P(None, "fs"),
            P(None, "fs"),
            P("fs"),
            P(None, "fs", None, "tp"),
            P(None, "tp", "fs"),
            P("fs", None, "tp"),
            P("tp", "fs"),
        ),
        check_vma=False,
    )
```

profile of v0, /device:TPU:0, one launch (start us, length us, event | category | flops | bytes accessed | tf_op | source)
XLA Modules:
  0.0 1378.0 jit_solution(2925851654451179741)
XLA Ops:
  8.0 10.5 all_gather.44
  21.1 37.1 %all-gather.11.cloned.1.call-done = bf16[3,2048,512]{2,1,0:T(8,128)(2,1)} async-done(((bf16[3,256,512]{2,1,0:T(8,128)(2,1)}), bf16[3,2048,512]{2,1,0:T(8,128)(2,1)}) %all-gather.11.cloned.1.call-update) | async-done | bytes 6291472 | tf_op jit(solution)/shard_map/all_gather | solution.py:79
  58.2 4.6 convolution_bitcast_fusion.7
  68.0 25.6 %all-gather.13.cloned.1.call-done = bf16[2048,512]{0,1:T(8,128)(2,1)} async-done(((bf16[256,512]{0,1:T(8,128)(2,1)}), bf16[2048,512]{0,1:T(8,128)(2,1)}) %all-gather.13.cloned.1.call-update) | async-done | bytes 2097168 | tf_op jit(solution)/shard_map/all_gather | solution.py:127
  93.6 4.4 reshape.287
  98.1 6.2 copy.146
  104.2 19.8 %all-gather.25.cloned.1.call-done = bf16[1,2048,512]{2,1,0:T(8,128)(2,1)} async-done(((bf16[1,256,512]{2,1,0:T(8,128)(2,1)}), bf16[1,2048,512]{2,1,0:T(8,128)(2,1)}) %all-gather.25.cloned.1.call-update) | async-done | bytes 2097168 | tf_op jit(solution)/shard_map/all_gather | solution.py:128
  124.0 4.0 reshape.253
  131.5 6.5 while.28
  138.4 15.6 %all-gather.15.cloned.1.call-done = bf16[512,2048]{1,0:T(8,128)(2,1)} async-done(((bf16[512,256]{1,0:T(8,128)(2,1)}), bf16[512,2048]{1,0:T(8,128)(2,1)}) %all-gather.15.cloned.1.call-update) | async-done | bytes 2097168 | tf_op jit(solution)/shard_map/all_gather | solution.py:80
  162.3 8.8 all-gather.1
  171.2 8.6 all_gather.49
  179.8 29.4 %all-reduce.6.cloned.1.call-done = bf16[256,2048]{1,0:T(8,128)(2,1)} async-done(((bf16[256,2048]{1,0:T(8,128)(2,1)}), bf16[256,2048]{1,0:T(8,128)(2,1)}) %all-reduce.6.cloned.1.call-update) | async-done | bytes 1048592 | tf_op jit(solution)/shard_map/psum | solution.py:162
  212.9 66.0 %all-gather.21.cloned.1.call-done = bf16[2048,2,1408]{2,0,1:T(8,128)(2,1)} async-done(((bf16[256,2,1408]{2,0,1:T(8,128)(2,1)}), bf16[2048,2,1408]{2,0,1:T(8,128)(2,1)}) %all-gather.21.cloned.1.call-update) | async-done | bytes 11534352 | tf_op jit(solution)/shard_map/all_gather | solution.py:170
  278.9 9.0 fusion.75
  287.9 37.4 %all-gather.23.cloned.1.call-done = bf16[1408,2048]{1,0:T(8,128)(2,1)} async-done(((bf16[1408,256]{1,0:T(8,128)(2,1)}), bf16[1408,2048]{1,0:T(8,128)(2,1)}) %all-gather.23.cloned.1.call-update) | async-done | bytes 5767184 | tf_op jit(solution)/shard_map/all_gather | solution.py:171
  325.3 6.9 multiply_reduce_fusion.4
  332.2 116.1 %all-gather.17.cloned.1.call-done = bf16[8,2048,2,352]{1,3,2,0:T(8,128)(2,1)} async-done(((bf16[8,256,2,352]{1,3,2,0:T(8,128)(2,1)}), bf16[8,2048,2,352]{1,3,2,0:T(8,128)(2,1)}) %all-gather.17.cloned.1.call-update) | async-done | bytes 23068688 | tf_op jit(solution)/shard_map/all_gather | solution.py:168
  448.3 13.4 fusion.69
  461.8 58.5 %all-gather.19.cloned.1.call-done = bf16[8,352,2048]{2,1,0:T(8,128)(2,1)} async-done(((bf16[8,352,256]{2,1,0:T(8,128)(2,1)}), bf16[8,352,2048]{2,1,0:T(8,128)(2,1)}) %all-gather.19.cloned.1.call-update) | async-done | bytes 11534352 | tf_op jit(solution)/shard_map/all_gather | solution.py:169
  520.3 13.2 fusion.66
  533.5 12.6 all-reduce.1
  546.6 3.9 fusion.78
  550.6 12.4 convolution_bitcast_fusion.5
  563.1 5.6 fusion.53
  570.3 47.7 %all-reduce.8.cloned.1.call-done = bf16[256,2048]{1,0:T(8,128)(2,1)} async-done(((bf16[256,2048]{1,0:T(8,128)(2,1)}), bf16[256,2048]{1,0:T(8,128)(2,1)}) %all-reduce.8.cloned.1.call-update) | async-done | bytes 1048592 | tf_op jit(solution)/shard_map/psum | solution.py:261
  626.4 19.7 %while.29 = (s32[]{:T(128)}, f32[2,128,4,128]{3,1,2,0:T(8,128)}, bf16[2,1024,1024]{2,1,0:T(8,128)(2,1)}, s32[2]{0:T(128)S(1)}, s32[]{:T(128)}, /*index=5*/s32[25...) while((s32[]{:T(128)}, f32[2,128,4,128]{3,1,2,0:T(8,128)}, ...), condition=%wide.region_23.24_spmd.clone, body=%wide.region_20.23_spmd.clone.sunk | while | flops 681247360 | bytes 40258464 | solution.py:363
  628.1 8.5 conditional.7
  647.8 56.7 %reduce-scatter.15.cloned.1.call-done = bf16[256,1024]{1,0:T(8,128)(2,1)} async-done(((bf16[2048,1024]{1,0:T(8,128)(2,1)}), bf16[256,1024]{1,0:T(8,128)(2,1)}) %reduce-scatter.15.cloned.1.call-update) | async-done | bytes 524304 | tf_op jit(solution)/shard_map/reduce_scatter | solution.py:364
  706.4 5.7 fusion.55
  713.1 7.1 convolution_bitcast_fusion.6
  720.3 5.6 fusion.54
  729.8 34.2 %all-reduce.10.cloned.1.call-done = bf16[256,2048]{1,0:T(8,128)(2,1)} async-done(((bf16[256,2048]{1,0:T(8,128)(2,1)}), bf16[256,2048]{1,0:T(8,128)(2,1)}) %all-reduce.10.cloned.1.call-update) | async-done | bytes 1048592 | tf_op jit(solution)/shard_map/psum | solution.py:386
  767.3 5.7 convolution_convert_fusion.1
  773.9 5.6 convert_bitcast_fusion.1
  779.6 7.8 convolution_convert_fusion.2
  788.4 7.0 convolution_convert_fusion
  795.6 12.9 convert_bitcast_fusion
  810.6 14.8 %all-reduce = bf16[2048]{0:T(1024)(128)(2,1)S(1)} all-reduce(bf16[2048]{0:T(1024)(128)(2,1)S(1)} %convert_element_type.242), channel_id=9, replica_groups=mesh['fs'=8,'tp'=4] {'fs'}, use_global_device_ids=true, to_apply=%region_33.34.clone | all-reduce | flops 2048 | bytes 8192
  829.3 40.9 %reduce-scatter.19.cloned.1.call-done = bf16[512,256]{1,0:T(8,128)(2,1)} async-done(((bf16[512,2048]{1,0:T(8,128)(2,1)}), bf16[512,256]{1,0:T(8,128)(2,1)}) %reduce-scatter.19.cloned.1.call-update) | async-done | bytes 262160 | tf_op jit(solution)/shard_map/reduce_scatter | solution.py:397
  875.4 32.1 %reduce-scatter.31.cloned.1.call-done = bf16[256,2]{1,0:T(8,128)(2,1)} async-done(((bf16[2048,2]{1,0:T(8,128)(2,1)}), bf16[256,2]{1,0:T(8,128)(2,1)}) %reduce-scatter.31.cloned.1.call-update) | async-done | bytes 1040
  909.1 61.4 %reduce-scatter.29.cloned.1.call-done = bf16[1408,256]{1,0:T(8,128)(2,1)} async-done(((bf16[1408,2048]{1,0:T(8,128)(2,1)}), bf16[1408,256]{1,0:T(8,128)(2,1)}) %reduce-scatter.29.cloned.1.call-update) | async-done | bytes 720912 | tf_op jit(solution)/shard_map/reduce_scatter | solution.py:418
  972.8 63.1 %reduce-scatter.17.cloned.1.call-done = bf16[3,256,512]{1,2,0:T(8,128)(2,1)} async-done(((bf16[3,2048,512]{1,2,0:T(8,128)(2,1)}), bf16[3,256,512]{1,2,0:T(8,128)(2,1)}) %reduce-scatter.17.cloned.1.call-update) | async-done | bytes 786448 | tf_op jit(solution)/shard_map/reduce_scatter | solution.py:394
  1038.4 87.8 %reduce-scatter.25.cloned.1.call-done = bf16[8,352,256]{2,1,0:T(8,128)(2,1)} async-done(((bf16[8,352,2048]{2,1,0:T(8,128)(2,1)}), bf16[8,352,256]{2,1,0:T(8,128)(2,1)}) %reduce-scatter.25.cloned.1.call-update) | async-done | bytes 1441808 | tf_op jit(solution)/shard_map/reduce_scatter | solution.py:412
  1129.4 87.0 %reduce-scatter.27.cloned.1.call-done = bf16[256,2,1408]{2,0,1:T(8,128)(2,1)} async-done(((bf16[2048,2,1408]{2,0,1:T(8,128)(2,1)}), bf16[256,2,1408]{2,0,1:T(8,128)(2,1)}) %reduce-scatter.27.cloned.1.call-update) | async-done | bytes 1441808 | tf_op jit(solution)/shard_map/reduce_scatter | solution.py:415
  1216.4 4.4 copy.168
  1220.8 145.1 %reduce-scatter.23.cloned.1.call-done = bf16[8,256,2,352]{1,3,2,0:T(8,128)(2,1)} async-done(((bf16[8,2048,2,352]{1,3,2,0:T(8,128)(2,1)}), bf16[8,256,2,352]{1,3,2,0:T(8,128)(2,1)}) %reduce-scatter.23.cloned.1.call-update) | async-done | bytes 2883600 | tf_op jit(solution)/shard_map/reduce_scatter | solution.py:409
  1365.9 5.0 convert_element_type.246
  (273 shorter events, 96.3 us)
Async XLA Ops:
  7.2 51.0 %copy-start = (bf16[256,2048]{1,0:T(8,128)(2,1)S(1)}, bf16[256,2048]{1,0:T(8,128)(2,1)}, u32[]{:S(2)}) copy-start(bf16[256,2048]{1,0:T(8,128)(2,1)} %param.21) | copy-start | bytes 3145732
  7.2 51.0 %all-gather.11.cloned.1.call-start = ((), (), s32[]{:S(2)}) async-start(), calls=%async_computation.10 | async-start | bytes 7077888 | tf_op jit(solution)/shard_map/all_gather | solution.py:79
  7.9 85.7 %all-gather.13.cloned.1.call-start = ((), (), s32[]{:S(2)}) async-start(), calls=%async_computation.11 | async-start | bytes 2359296 | tf_op jit(solution)/shard_map/all_gather | solution.py:127
  20.1 42.7 %copy-start.39 = (f32[256]{0:T(256)}, f32[256]{0:T(256)S(1)}, u32[]{:S(2)}) copy-start(f32[256]{0:T(256)S(1)} %add_rsqrt_fusion.1) | copy-start | bytes 3076
  21.0 43.3 %copy-start.23 = (f32[256,64]{0,1:T(8,128)}, f32[256,64]{0,1:T(8,128)S(1)}, u32[]{:S(2)}) copy-start(f32[256,64]{0,1:T(8,128)S(1)} %get-tuple-element.673) | copy-start | bytes 196612
  21.1 41.8 %copy-start.32 = (f32[1,2048]{1,0:T(1,128)}, f32[1,2048]{1,0:T(1,128)S(1)}, u32[]{:S(2)}) copy-start(f32[1,2048]{1,0:T(1,128)S(1)} %get-tuple-element.669) | copy-start | bytes 24580
  21.1 190.0 %copy-start.34 = (f32[1,2048]{1,0:T(1,128)}, f32[1,2048]{1,0:T(1,128)S(1)}, u32[]{:S(2)}) copy-start(f32[1,2048]{1,0:T(1,128)S(1)} %get-tuple-element.670) | copy-start | bytes 24580
  65.3 58.7 %all-gather.25.cloned.1.call-start = ((), (), s32[]{:S(2)}) async-start(), calls=%async_computation.29 | async-start | bytes 2359296 | tf_op jit(solution)/shard_map/all_gather | solution.py:128
  67.1 86.8 %all-gather.15.cloned.1.call-start = ((), (), s32[]{:S(2)}) async-start(), calls=%async_computation.12 | async-start | bytes 2359296 | tf_op jit(solution)/shard_map/all_gather | solution.py:80
  67.7 141.5 %all-reduce.6.cloned.1.call-start = ((), (), s32[]{:S(2)}) async-start(), calls=%async_computation.13 | async-start | bytes 2097152 | tf_op jit(solution)/shard_map/psum | solution.py:162
  138.0 19.3 %copy-start.13 = (f32[2,128,4,128]{3,1,2,0:T(8,128)}, f32[2,128,4,128]{3,1,2,0:T(8,128)S(1)}, u32[]{:S(2)}) copy-start(f32[2,128,4,128]{3,1,2,0:T(8,128)S(1)} %get-tuple-element.314) | copy-start | bytes 1572868
  138.4 18.9 %copy-start.19 = (bf16[2,128,4,128]{3,2,1,0:T(4,128)(2,1)}, bf16[2,128,4,128]{3,2,1,0:T(4,128)(2,1)S(1)}, u32[]{:S(2)}) copy-start(bf16[2,128,4,128]{3,2,1,0:T(4,128)(2,1)S(1)} %copy.149) | copy-start | bytes 786436
  157.3 121.6 %all-gather.21.cloned.1.call-start = ((), (), s32[]{:S(2)}) async-start(), calls=%async_computation.16 | async-start | bytes 12976128 | tf_op jit(solution)/shard_map/all_gather | solution.py:170
  160.0 165.3 %all-gather.23.cloned.1.call-start = ((), (), s32[]{:S(2)}) async-start(), calls=%async_computation.17 | async-start | bytes 6488064 | tf_op jit(solution)/shard_map/all_gather | solution.py:171
  160.8 10.4 copy-start.43
  160.8 19.0 %copy-start.44 = (s32[256,4]{0,1:T(4,128)S(1)}, s32[256,4]{0,1:T(4,128)}, u32[]{:S(2)}) copy-start(s32[256,4]{0,1:T(4,128)} %param.32) | copy-start | bytes 12292
  160.8 287.6 %all-gather.17.cloned.1.call-start = ((), (), s32[]{:S(2)}) async-start(), calls=%async_computation.14 | async-start | bytes 25952256 | tf_op jit(solution)/shard_map/all_gather | solution.py:168
  161.5 358.8 %all-gather.19.cloned.1.call-start = ((), (), s32[]{:S(2)}) async-start(), calls=%async_computation.15 | async-start | bytes 12976128 | tf_op jit(solution)/shard_map/all_gather | solution.py:169
  162.3 455.7 %all-reduce.8.cloned.1.call-start = ((), (), s32[]{:S(2)}) async-start(), calls=%async_computation.19 | async-start | bytes 2097152 | tf_op jit(solution)/shard_map/psum | solution.py:261
  179.8 31.7 %copy-start.30 = (bf16[8,2048]{1,0:T(8,128)(2,1)}, bf16[8,2048]{1,0:T(8,128)(2,1)S(1)}, u32[]{:S(2)}) copy-start(bf16[8,2048]{1,0:T(8,128)(2,1)S(1)} %all_gather.49) | copy-start | bytes 98308
  212.9 112.4 %copy-start.7 = (bf16[256,2048]{1,0:T(8,128)(2,1)S(1)}, bf16[256,2048]{1,0:T(8,128)(2,1)}, u32[]{:S(2)}) copy-start(bf16[256,2048]{1,0:T(8,128)(2,1)} %param.22) | copy-start | bytes 3145732
  546.6 16.4 %slice-start = ((s8[11534336]{0:T(1024)(128)(4,1)}), s8[4194304]{0:T(1024)(128)(4,1)S(1)}, s32[]{:S(2)}) async-start(s8[11534336]{0:T(1024)(128)(4,1)} %bitcast.277), calls=%async_computation.31 | async-start | bytes 8388608
  550.6 12.4 copy-start.17
  550.6 12.4 slice-start.1
  550.6 12.4 slice-start.2
  568.7 135.8 %reduce-scatter.15.cloned.1.call-start = ((), (), s32[]{:S(2)}) async-start(), calls=%async_computation.20 | async-start | bytes 4718592 | tf_op jit(solution)/shard_map/reduce_scatter | solution.py:364
  646.2 117.9 %all-reduce.10.cloned.1.call-start = ((), (), s32[]{:S(2)}) async-start(), calls=%async_computation.21 | async-start | bytes 2097152 | tf_op jit(solution)/shard_map/psum | solution.py:386
  647.4 58.4 %copy-start.24 = (f32[256,64]{0,1:T(8,128)S(1)}, f32[256,64]{0,1:T(8,128)}, u32[]{:S(2)}) copy-start(f32[256,64]{0,1:T(8,128)} %copy-done.23) | copy-start | bytes 196612
  647.4 58.4 %copy-start.29 = (f32[256,64]{0,1:T(8,128)S(1)}, f32[256,64]{0,1:T(8,128)}, u32[]{:S(2)}) copy-start(f32[256,64]{0,1:T(8,128)} %get-tuple-element.671) | copy-start | bytes 196612
  706.2 5.9 copy-start.27
  706.3 5.7 copy-start.28
  712.1 114.0 %reduce-scatter.21.cloned.1.call-start = ((), (), s32[]{:S(2)}) async-start(), calls=%async_computation.24 | async-start | bytes 36864 | tf_op jit(solution)/shard_map/reduce_scatter | solution.py:403
  713.0 114.4 %reduce-scatter.13.cloned.1.call-start = ((), (), s32[]{:S(2)}) async-start(), calls=%async_computation.18 | async-start | bytes 1310720 | tf_op jit(solution)/shard_map/reduce_scatter | solution.py:203
  713.1 7.2 copy-start.16
  713.1 7.2 copy-start.37
  720.2 5.6 copy-start.20
  725.8 144.3 %reduce-scatter.19.cloned.1.call-start = ((), (), s32[]{:S(2)}) async-start(), calls=%async_computation.23 | async-start | bytes 2359296 | tf_op jit(solution)/shard_map/reduce_scatter | solution.py:397
  729.5 34.5 %copy-start.1 = (bf16[256,2048]{1,0:T(8,128)(2,1)S(1)}, bf16[256,2048]{1,0:T(8,128)(2,1)}, u32[]{:S(2)}) copy-start(bf16[256,2048]{1,0:T(8,128)(2,1)} %param.21) | copy-start | bytes 3145732
  729.5 34.5 %copy-start.33 = (f32[1,2048]{1,0:T(1,128)S(1)}, f32[1,2048]{1,0:T(1,128)}, u32[]{:S(2)}) copy-start(f32[1,2048]{1,0:T(1,128)} %copy-done.32) | copy-start | bytes 24580
  729.5 34.5 %copy-start.40 = (f32[256]{0:T(256)S(1)}, f32[256]{0:T(256)}, u32[]{:S(2)}) copy-start(f32[256]{0:T(256)} %copy-done.39) | copy-start | bytes 3076
  729.6 37.7 %copy-start.9 = (bf16[256,2048]{1,0:T(8,128)(2,1)S(1)}, bf16[256,2048]{1,0:T(8,128)(2,1)}, u32[]{:S(2)}) copy-start(bf16[256,2048]{1,0:T(8,128)(2,1)} %param.22) | copy-start | bytes 3145732
  729.6 178.0 %reduce-scatter.31.cloned.1.call-start = ((), (), s32[]{:S(2)}) async-start(), calls=%async_computation.30 | async-start | bytes 589824
  767.2 203.3 %reduce-scatter.29.cloned.1.call-start = ((), (), s32[]{:S(2)}) async-start(), calls=%async_computation.28 | async-start | bytes 6488064 | tf_op jit(solution)/shard_map/reduce_scatter | solution.py:418
  773.0 262.9 %reduce-scatter.17.cloned.1.call-start = ((), (), s32[]{:S(2)}) async-start(), calls=%async_computation.22 | async-start | bytes 7077888 | tf_op jit(solution)/shard_map/reduce_scatter | solution.py:394
  779.5 346.7 %reduce-scatter.25.cloned.1.call-start = ((), (), s32[]{:S(2)}) async-start(), calls=%async_computation.26 | async-start | bytes 12976128 | tf_op jit(solution)/shard_map/reduce_scatter | solution.py:412
  787.4 429.0 %reduce-scatter.27.cloned.1.call-start = ((), (), s32[]{:S(2)}) async-start(), calls=%async_computation.27 | async-start | bytes 12976128 | tf_op jit(solution)/shard_map/reduce_scatter | solution.py:415
  795.5 570.4 %reduce-scatter.23.cloned.1.call-start = ((), (), s32[]{:S(2)}) async-start(), calls=%async_computation.25 | async-start | bytes 25952256 | tf_op jit(solution)/shard_map/reduce_scatter | solution.py:409
  808.5 63.5 %copy-start.15 = (bf16[256,2048]{1,0:T(8,128)(2,1)S(1)}, bf16[256,2048]{1,0:T(8,128)(2,1)}, u32[]{:S(2)}) copy-start(bf16[256,2048]{1,0:T(8,128)(2,1)} %all-reduce.10.cloned.1.call-done) | copy-start | bytes 3145732
  (24 other events, 48.6 us)
Sparse Core Ops, SparseCore 0:
  9.9 48.2 all-gather.10
  65.4 28.1 all-gather.12
  96.1 27.8 all-gather.24
  125.8 28.1 all-gather.14
  157.4 51.8 all-reduce.5
  211.8 67.0 all-gather.20
  280.9 44.3 all-gather.22
  327.3 120.9 all-gather.16
  450.4 69.8 all-gather.18
  568.8 49.0 all-reduce.7
  646.3 58.1 reduce-scatter.14
  712.2 51.8 all-reduce.9
  767.0 30.6 reduce-scatter.20
  799.9 27.1 reduce-scatter.12
  830.2 39.8 reduce-scatter.18
  873.4 34.1 reduce-scatter.30
  911.4 59.0 reduce-scatter.28
  974.1 61.7 reduce-scatter.16
  1039.4 86.7 reduce-scatter.24
  1129.5 86.7 reduce-scatter.26
  1220.0 145.8 reduce-scatter.22
where the time goes:
time: 1390 us; the launch traced here: 1380 us
  waiting for transfers between devices  1070 us (77%)
  matrix products  144 us (10%)
  blocking collectives  55.4 us (4%)
  local copies, waits for them, and re-layouts  46.7 us (3%)
  other arithmetic  46.7 us (3%)
  between operations  16 us (1%)
    reduce_scatter x1, waiting for transfers between devices, shards(): lax.psum_scatter(expert_gate_grad.astype(jnp.bfloat16), 'fs', scatter_dim...  145 us
    all_gather x1, waiting for transfers between devices, shards(): lax.all_gather(expert_gate_up, 'fs', axis=1, tiled=True)  116 us
    reduce_scatter x1, waiting for transfers between devices, shards(): lax.psum_scatter(expert_down_grad.astype(jnp.bfloat16), 'fs', scatter_dim...  87.8 us
    reduce_scatter x1, waiting for transfers between devices, shards(): lax.psum_scatter(shared_proj_grad.astype(jnp.bfloat16), 'fs', scatter_dim...  87 us
    all_gather x1, waiting for transfers between devices, shards(): lax.all_gather(shared_gate_up, 'fs', axis=0, tiled=True)  66 us
    reduce_scatter x1, waiting for transfers between devices, shards(): lax.psum_scatter(qkv_grad.astype(jnp.bfloat16), 'fs', scatter_dimension=1...  63.1 us
    reduce_scatter x1, waiting for transfers between devices, shards(): lax.psum_scatter(shared_down_grad.astype(jnp.bfloat16), 'fs', scatter_dim...  61.4 us
    all_gather x1, waiting for transfers between devices, shards(): lax.all_gather(expert_down, 'fs', axis=2, tiled=True)  58.5 us
  transfers between devices with their start and end apart: 21, of which 19 were waited for; matrix products, arithmetic and copies ran while one was open for 11% of the time, Pallas kernels for 0%

commit v1 on v0

--- a/solution.py
+++ b/solution.py
@@ -8,6 +8,7 @@
 HD = 128
 E = 8
 SEQ_DEV = 128
+SIDE = 128
 
 
 NORM_EPS = 1e-06
@@ -47,7 +48,7 @@
     return (key_pos <= query_pos[None, :, None, None]) & (key_pos >= query_start[:, :, None, None])
 
 
-def shards(
+def shards_gathered(
     tokens,
     cotangent,
     qkv_weight,
@@ -434,9 +435,396 @@
     )
 
 
+def shards_units(
+    tokens,
+    cotangent,
+    qkv_weight,
+    out_weight,
+    norm_gains,
+    router_weight,
+    shared_gate,
+    expert_gate_up,
+    expert_down,
+    shared_gate_up,
+    shared_down,
+    routes,
+    doc_start,
+):
+    tok_rows = tokens.shape[0]
+    seq_count = tok_rows // SEQ_DEV
+    local_width = qkv_weight.shape[2]
+    head_count = local_width // HD
+    out_width = tokens.shape[1] // lax.axis_size("tp")
+    score_scale = HD ** (-0.5)
+    fs_index = lax.axis_index("fs")
+    tp_index = lax.axis_index("tp")
+    query_pos = fs_index * SEQ_DEV + jnp.arange(SEQ_DEV, dtype=jnp.int32)
+    positions = jnp.tile(query_pos, seq_count)
+    query_start = doc_start.reshape(seq_count, SEQ_DEV)
+    cosine, sine_table = rope_tables(positions)
+    group_limit = max(1, 512 // SEQ_DEV)
+    fs_size = lax.axis_size("fs")
+    width = tokens.shape[1]
+    small = jnp.concatenate([norm_gains, router_weight, shared_gate[None]], axis=0)
+    small_full = lax.all_gather(small, "fs", axis=1, tiled=True)
+    gains_full = small_full[:2]
+    router_full = small_full[2 : 2 + E]
+    shared_gate_full = small_full[2 + E]
+    qkv_full = lax.all_gather(qkv_weight, "fs", axis=1, tiled=True)
+    out_full = lax.all_gather(out_weight, "fs", axis=1, tiled=True)
+    routed_units = expert_down.shape[1]
+    shared_units = shared_down.shape[0] // fs_size
+    units = routed_units + shared_units
+    block = expert_down.shape[2]
+    expert_up_slabs = jnp.transpose(expert_gate_up, (0, 2, 3, 1))
+    shared_up_slabs = jnp.transpose(
+        shared_gate_up.reshape(block, 2, fs_size, shared_units), (2, 1, 3, 0)
+    )
+    up_slabs = jnp.concatenate([expert_up_slabs, shared_up_slabs], axis=2)
+    down_slabs = jnp.concatenate(
+        [expert_down, shared_down.reshape(fs_size, shared_units, block)], axis=1
+    )
+    slabs = jnp.concatenate([up_slabs, down_slabs[:, None]], axis=1)
+    slabs = lax.all_to_all(slabs, "fs", 0, 0, tiled=True)
+    cotangent_all = lax.all_gather(cotangent, "fs", axis=0, tiled=True)
+    token_float = tokens.astype(jnp.float32)
+    rstd_one = lax.rsqrt(jnp.mean(token_float * token_float, axis=1, keepdims=True) + NORM_EPS)
+    normed_one = token_float * rstd_one
+    hidden_one = (normed_one * gains_full[0].astype(jnp.float32)[None, :]).astype(jnp.bfloat16)
+    projected = jnp.einsum("td,jdf->jtf", hidden_one, qkv_full, preferred_element_type=jnp.float32)
+    query_rows = rotate(projected[0], cosine, sine_table).astype(jnp.bfloat16)
+    key_own = rotate(projected[1], cosine, sine_table).astype(jnp.bfloat16)
+    value_own = projected[2].astype(jnp.bfloat16)
+    query_heads = query_rows.reshape(seq_count, SEQ_DEV, head_count, HD)
+
+    def score_block(key_group, first_dev):
+        allowed = key_mask(query_pos, query_start, first_dev, key_group.shape[0])[:, None]
+        scores = (
+            jnp.einsum(
+                "pqhd,gpkhd->phqgk", query_heads, key_group, preferred_element_type=jnp.float32
+            )
+            * score_scale
+        )
+        return (jnp.where(allowed, scores, NEG_FILL), allowed)
+
+    def forward_update(running, key_group, value_group, first_dev):
+        run_max, run_sum, accumulated = running
+        scores, allowed = score_block(key_group, first_dev)
+        new_max = jnp.maximum(run_max, jnp.max(scores, axis=(3, 4)))
+        weights = jnp.where(allowed, jnp.exp(scores - new_max[..., None, None]), 0.0)
+        factor = jnp.exp(run_max - new_max)
+        new_sum = run_sum * factor + jnp.sum(weights, axis=(3, 4))
+        mixed_part = jnp.einsum(
+            "phqgk,gpkhd->pqhd",
+            weights.astype(jnp.bfloat16),
+            value_group,
+            preferred_element_type=jnp.float32,
+        )
+        new_accum = accumulated * jnp.transpose(factor, (0, 2, 1))[..., None] + mixed_part
+        return (new_max, new_sum, new_accum)
+
+    initial = (
+        jnp.full((seq_count, head_count, SEQ_DEV), NEG_FILL, jnp.float32),
+        jnp.zeros((seq_count, head_count, SEQ_DEV), jnp.float32),
+        jnp.zeros((seq_count, SEQ_DEV, head_count, HD), jnp.float32),
+    )
+    running = initial
+    key_piece = lax.all_gather(key_own, "fs", axis=0, tiled=True)
+    value_piece = lax.all_gather(value_own, "fs", axis=0, tiled=True)
+    shard_count = key_piece.shape[0] // tok_rows
+    group_size = math.gcd(shard_count, group_limit)
+    step_count = shard_count // group_size
+    shaped = (step_count, group_size, seq_count, SEQ_DEV, head_count, HD)
+    first_dev = jnp.int32(0) // tok_rows
+
+    def one_step(carried, inputs):
+        key_group, value_group, group_index = inputs
+        start_dev = group_index * group_size
+        updated = lax.cond(
+            start_dev <= fs_index,
+            lambda state_in: forward_update(state_in, key_group, value_group, start_dev),
+            lambda state_in: state_in,
+            carried,
+        )
+        return (updated, None)
+
+    running, ignored = lax.scan(
+        one_step,
+        running,
+        (
+            key_piece.reshape(shaped),
+            value_piece.reshape(shaped),
+            jnp.arange(step_count, dtype=jnp.int32),
+        ),
+    )
+    run_max, run_sum, accumulated = running
+    attended_heads = (accumulated / jnp.transpose(run_sum, (0, 2, 1))[..., None]).astype(
+        jnp.bfloat16
+    )
+    log_total = run_max + jnp.log(run_sum)
+    attended = attended_heads.reshape(tok_rows, local_width)
+    branch_part = jnp.dot(attended, out_full, preferred_element_type=jnp.float32)
+    branch = lax.psum(branch_part.astype(jnp.bfloat16), "tp").astype(jnp.float32)
+    residual = token_float + branch
+    rstd_two = lax.rsqrt(jnp.mean(residual * residual, axis=1, keepdims=True) + NORM_EPS)
+    normed_two = residual * rstd_two
+    hidden_two = (normed_two * gains_full[1].astype(jnp.float32)[None, :]).astype(jnp.bfloat16)
+    logits = jnp.einsum("td,ed->te", hidden_two, router_full, preferred_element_type=jnp.float32)
+    router_probs = jax.nn.softmax(logits, axis=-1)
+    chosen = jnp.sum(
+        (routes[:, :, None] == jnp.arange(E, dtype=jnp.int32)[None, None, :]).astype(jnp.float32),
+        axis=1,
+    )
+    gate_weights = router_probs * chosen
+    gate_logit = jnp.einsum(
+        "td,d->t", hidden_two, shared_gate_full, preferred_element_type=jnp.float32
+    )
+    gate_value = jax.nn.sigmoid(gate_logit)
+    scales = jnp.concatenate([gate_weights, gate_value[:, None]], axis=1)
+    scales_high = scales.astype(jnp.bfloat16)
+    scales_low = (scales - scales_high.astype(jnp.float32)).astype(jnp.bfloat16)
+    sent = jnp.concatenate(
+        [
+            hidden_two,
+            scales_high,
+            scales_low,
+            jnp.zeros((tok_rows, SIDE - 2 * (E + 1)), jnp.bfloat16),
+        ],
+        axis=1,
+    )
+    hidden_all = lax.all_gather(sent, "fs", axis=0, tiled=True)
+    side_all = hidden_all[:, width : width + 2 * (E + 1)].astype(jnp.float32)
+    scales_all = side_all[:, : E + 1] + side_all[:, E + 1 :]
+    two_all = hidden_all[:, :width]
+    mine = (jnp.arange(E, dtype=jnp.int32) == fs_index).astype(jnp.float32)
+    routed_scale = jnp.sum(scales_all[:, :E] * mine[None, :], axis=1, keepdims=True)
+    is_routed = jnp.arange(units, dtype=jnp.int32)[None, :] < routed_units
+    scale = jnp.where(is_routed, routed_scale, scales_all[:, E:])
+    weights_by_unit = jnp.transpose(slabs, (1, 2, 0, 3)).reshape(3, units, width)
+    gate_part = jnp.einsum(
+        "td,ud->tu", two_all, weights_by_unit[0], preferred_element_type=jnp.float32
+    )
+    up_part = jnp.einsum(
+        "td,ud->tu", two_all, weights_by_unit[1], preferred_element_type=jnp.float32
+    )
+    hidden_grad = jnp.einsum(
+        "td,ud->tu", cotangent_all, weights_by_unit[2], preferred_element_type=jnp.float32
+    )
+    gate_sigmoid = jax.nn.sigmoid(gate_part)
+    silu = gate_part * gate_sigmoid
+    active = silu * up_part
+    hidden = (scale * active).astype(jnp.bfloat16)
+    dots = active * hidden_grad
+    routed_dot = jnp.sum(jnp.where(is_routed, dots, 0.0), axis=1, keepdims=True)
+    shared_dot = jnp.sum(jnp.where(is_routed, 0.0, dots), axis=1, keepdims=True)
+    active_grad = scale * hidden_grad
+    gate_grad = (
+        active_grad * up_part * gate_sigmoid * (1.0 + gate_part * (1.0 - gate_sigmoid))
+    ).astype(jnp.bfloat16)
+    up_grad = (active_grad * silu).astype(jnp.bfloat16)
+    mixture_part = jnp.einsum(
+        "tu,ud->td", hidden, weights_by_unit[2], preferred_element_type=jnp.float32
+    )
+    mixture_own = lax.psum_scatter(
+        mixture_part.astype(jnp.bfloat16), "fs", scatter_dimension=0, tiled=True
+    )
+    mixture = lax.psum_scatter(
+        mixture_own, "tp", scatter_dimension=1, tiled=True
+    ).astype(jnp.float32)
+    output = (
+        lax.dynamic_slice_in_dim(residual, tp_index * out_width, out_width, 1) + mixture
+    ).astype(jnp.bfloat16)
+    input_part = jnp.einsum(
+        "tu,ud->td", gate_grad, weights_by_unit[0], preferred_element_type=jnp.float32
+    ) + jnp.einsum(
+        "tu,ud->td", up_grad, weights_by_unit[1], preferred_element_type=jnp.float32
+    )
+    side_part = jnp.concatenate(
+        [
+            routed_dot * mine[None, :],
+            shared_dot,
+            jnp.zeros((input_part.shape[0], SIDE - E - 1), jnp.float32),
+        ],
+        axis=1,
+    )
+    back_part = jnp.concatenate([input_part, side_part], axis=1).astype(jnp.bfloat16)
+    back_own = lax.psum_scatter(back_part, "fs", scatter_dimension=0, tiled=True)
+    back_sum = lax.psum(back_own, "tp").astype(jnp.float32)
+    input_sum = back_sum[:, :width]
+    gate_sum = back_sum[:, width : width + E]
+    shared_sum = back_sum[:, width + E]
+    grad_by_unit = jnp.stack(
+        [
+            jnp.einsum("tu,td->ud", gate_grad, two_all, preferred_element_type=jnp.float32),
+            jnp.einsum("tu,td->ud", up_grad, two_all, preferred_element_type=jnp.float32),
+            jnp.einsum("tu,td->ud", hidden, cotangent_all, preferred_element_type=jnp.float32),
+        ],
+        axis=0,
+    ).astype(jnp.bfloat16)
+    grad_slabs = jnp.transpose(grad_by_unit.reshape(3, units, fs_size, block), (2, 0, 1, 3))
+    grad_slabs = lax.all_to_all(grad_slabs, "fs", 0, 0, tiled=True)
+    chosen_grad = chosen * gate_sum
+    logit_grad = (
+        router_probs * (chosen_grad - jnp.sum(router_probs * chosen_grad, axis=1, keepdims=True))
+    ).astype(jnp.bfloat16)
+    gate_logit_grad = (shared_sum * gate_value * (1.0 - gate_value)).astype(jnp.bfloat16)
+    router_grad = jnp.einsum(
+        "te,td->ed", logit_grad, hidden_two, preferred_element_type=jnp.float32
+    )
+    shared_vector_grad = jnp.einsum(
+        "t,td->d", gate_logit_grad, hidden_two, preferred_element_type=jnp.float32
+    )
+    two_grad = (
+        input_sum
+        + jnp.einsum("te,ed->td", logit_grad, router_full, preferred_element_type=jnp.float32)
+        + gate_logit_grad.astype(jnp.float32)[:, None]
+        * shared_gate_full.astype(jnp.float32)[None, :]
+    )
+    scaled_two = two_grad * gains_full[1].astype(jnp.float32)[None, :]
+    gain_two_grad = jnp.sum(two_grad * normed_two, axis=0)
+    residual_grad = cotangent.astype(jnp.float32) + rstd_two * (
+        scaled_two - normed_two * jnp.mean(scaled_two * normed_two, axis=1, keepdims=True)
+    )
+    branch_grad = residual_grad.astype(jnp.bfloat16)
+    out_grad = jnp.einsum("tf,td->fd", attended, branch_grad, preferred_element_type=jnp.float32)
+    attended_grad = jnp.einsum(
+        "td,fd->tf", branch_grad, out_full, preferred_element_type=jnp.float32
+    ).astype(jnp.bfloat16)
+    grad_heads = attended_grad.reshape(seq_count, SEQ_DEV, head_count, HD)
+    delta_rows = jnp.einsum(
+        "pqhd,pqhd->phq", grad_heads, attended_heads, preferred_element_type=jnp.float32
+    )
+    key_all, value_all = key_piece, value_piece
+    device_count = key_all.shape[0] // tok_rows
+    back_group = math.gcd(device_count, group_limit)
+    back_steps = device_count // back_group
+    back_shape = (back_steps, back_group, seq_count, SEQ_DEV, head_count, HD)
+
+    def backward_update(key_group, value_group, start_dev):
+        scores, allowed = score_block(key_group, start_dev)
+        probs_block = jnp.where(allowed, jnp.exp(scores - log_total[..., None, None]), 0.0)
+        weights_grad = jnp.einsum(
+            "pqhd,gpkhd->phqgk", grad_heads, value_group, preferred_element_type=jnp.float32
+        )
+        score_grad = (probs_block * (weights_grad - delta_rows[..., None, None])).astype(
+            jnp.bfloat16
+        )
+        query_part = (
+            jnp.einsum(
+                "phqgk,gpkhd->pqhd", score_grad, key_group, preferred_element_type=jnp.float32
+            )
+            * score_scale
+        )
+        key_part = (
+            jnp.einsum(
+                "phqgk,pqhd->gpkhd", score_grad, query_heads, preferred_element_type=jnp.float32
+            )
+            * score_scale
+        )
+        value_part = jnp.einsum(
+            "phqgk,pqhd->gpkhd",
+            probs_block.astype(jnp.bfloat16),
+            grad_heads,
+            preferred_element_type=jnp.float32,
+        )
+        return (query_part, key_part, value_part)
+
+    empty_grads = (
+        jnp.zeros((seq_count, SEQ_DEV, head_count, HD), jnp.float32),
+        jnp.zeros((back_group, seq_count, SEQ_DEV, head_count, HD), jnp.float32),
+        jnp.zeros((back_group, seq_count, SEQ_DEV, head_count, HD), jnp.float32),
+    )
+    scan_inputs = (
+        key_all.reshape(back_shape),
+        value_all.reshape(back_shape),
+        jnp.arange(back_steps, dtype=jnp.int32),
+    )
+
+    def back_step(query_acc, inputs):
+        key_group, value_group, group_index = inputs
+        start_dev = group_index * back_group
+        query_part, key_part, value_part = lax.cond(
+            start_dev <= fs_index,
+            lambda ignored_in: backward_update(key_group, value_group, start_dev),
+            lambda ignored_in: empty_grads,
+            key_group,
+        )
+        term_rows = jnp.concatenate(
+            [
+                key_part.reshape(back_group * tok_rows, local_width),
+                value_part.reshape(back_group * tok_rows, local_width),
+            ],
+            axis=1,
+        )
+        return (query_acc + query_part, term_rows)
+
+    query_grad, key_value_terms = lax.scan(back_step, empty_grads[0], scan_inputs)
+    key_value_sum = lax.psum_scatter(
+        key_value_terms.reshape(device_count * tok_rows, 2 * local_width).astype(jnp.bfloat16),
+        "fs",
+        scatter_dimension=0,
+        tiled=True,
+    ).astype(jnp.float32)
+    key_grad_rows = key_value_sum[:, :local_width]
+    value_grad_rows = key_value_sum[:, local_width:]
+    projected_grad = jnp.stack(
+        [
+            rotate(query_grad.reshape(tok_rows, local_width), cosine, -sine_table),
+            rotate(key_grad_rows, cosine, -sine_table),
+            value_grad_rows,
+        ],
+        axis=0,
+    ).astype(jnp.bfloat16)
+    qkv_grad = jnp.einsum(
+        "td,jtf->jdf", hidden_one, projected_grad, preferred_element_type=jnp.float32
+    )
+    one_part = jnp.einsum(
+        "jtf,jdf->td", projected_grad, qkv_full, preferred_element_type=jnp.float32
+    )
+    one_grad = lax.psum(one_part.astype(jnp.bfloat16), "tp").astype(jnp.float32)
+    scaled_one = one_grad * gains_full[0].astype(jnp.float32)[None, :]
+    gain_one_grad = jnp.sum(one_grad * normed_one, axis=0)
+    input_grad = residual_grad + rstd_one * (
+        scaled_one - normed_one * jnp.mean(scaled_one * normed_one, axis=1, keepdims=True)
+    )
+    gains_grad = jnp.stack([gain_one_grad, gain_two_grad], axis=0)
+    small_grad = jnp.concatenate(
+        [gains_grad, router_grad, shared_vector_grad[None]], axis=0
+    ).astype(jnp.bfloat16)
+    small_own = lax.psum_scatter(small_grad, "fs", scatter_dimension=1, tiled=True).astype(
+        jnp.float32
+    )
+    qkv_own = lax.psum_scatter(
+        qkv_grad.astype(jnp.bfloat16), "fs", scatter_dimension=1, tiled=True
+    ).astype(jnp.float32)
+    out_own = lax.psum_scatter(
+        out_grad.astype(jnp.bfloat16), "fs", scatter_dimension=1, tiled=True
+    ).astype(jnp.float32)
+    own = grad_slabs.astype(jnp.float32)
+    expert_up_own = jnp.transpose(own[:, :2, :routed_units], (0, 3, 1, 2))
+    expert_down_own = own[:, 2, :routed_units]
+    shared_up_own = jnp.transpose(own[:, :2, routed_units:], (3, 1, 0, 2)).reshape(
+        shared_gate_up.shape
+    )
+    shared_down_own = own[:, 2, routed_units:].reshape(shared_down.shape)
+    return (
+        output,
+        input_grad,
+        qkv_own,
+        out_own,
+        small_own[:2],
+        small_own[2 : 2 + E],
+        small_own[2 + E],
+        expert_up_own,
+        expert_down_own,
+        shared_up_own,
+        shared_down_own,
+    )
+
+
 def solution(mesh):
     return jax.shard_map(
-        shards,
+        shards_units if mesh.shape["fs"] == E else shards_gathered,
         mesh=mesh,
         in_specs=(
             P("fs", None),

time: 1390 us -> 1040 us (0.75)
  waiting for transfers between devices: 1070 us -> 682 us
  local copies, waits for them, and re-layouts: 46.7 us -> 134 us
  blocking collectives: 55.4 us -> 10.5 us
  matrix products: 144 us -> 125 us
    reduce_scatter x9 -> x7, waiting for transfers between devices: 542 us -> 244 us  [the longest x1 73.9 us: shards_units(): lax.psum_scatter(back_part, 'fs', scatter_dimension=0, tiled=True)]
    all_gather x8 -> x6, waiting for transfers between devices: 376 us -> 131 us  [the longest x1 35.9 us: shards_units(): qkv_full = lax.all_gather(qkv_weight, 'fs', axis=1, tiled=True)]
    all_to_all x0 -> x2, waiting for transfers between devices: none -> 180 us  [the longest x1 98.1 us: shards_units(): slabs = lax.all_to_all(slabs, 'fs', 0, 0, tiled=True)]
    concatenate x0 -> x2, local copies, waits for them, and re-layouts: none -> 46.4 us  [the longest x1 39.6 us: shards_units(): jnp.concatenate([input_part, side_part], axis=1).astype(jnp.bfloat16)]
    unnamed x22 -> x16, waiting for transfers between devices: 35.7 us -> 2.11 us
    dot_general x23 -> x20, matrix products: 135 us -> 116 us  [the longest x1 13.4 us: shards_units(): jnp.einsum('td,ud->tu', cotangent_all, weights_by_unit[2], preferred_elem...]
    all_gather x3 -> x1, blocking collectives: 28 us -> 10.5 us  [shards_units(): small_full = lax.all_gather(small, 'fs', axis=1, tiled=True)]
    unnamed x110 -> x146, local copies, waits for them, and re-layouts: 29.4 us -> 45.4 us
  transfers between devices with their start and end apart: 21 -> 18, of which waited for: 19 -> 14; matrix products, arithmetic and copies ran while one was open for 11% -> 17% of each run, Pallas kernels for 0% -> 0%
where the time goes in v1:
time: 1040 us; the launch traced here: 1030 us
  waiting for transfers between devices  682 us (66%)
  local copies, waits for them, and re-layouts  134 us (13%)
  matrix products  125 us (12%)
  other arithmetic  51.2 us (5%)
  between operations  15.2 us (1%)
  starting transfers between devices  11.3 us (1%)
  blocking collectives  10.5 us (1%)
    all_to_all x1, waiting for transfers between devices, shards_units(): slabs = lax.all_to_all(slabs, 'fs', 0, 0, tiled=True)  98.1 us
    all_to_all x1, waiting for transfers between devices, shards_units(): grad_slabs = lax.all_to_all(grad_slabs, 'fs', 0, 0, tiled=True)  82.1 us
    reduce_scatter x1, waiting for transfers between devices, shards_units(): lax.psum_scatter(back_part, 'fs', scatter_dimension=0, tiled=True)  73.9 us
    reduce_scatter x1, waiting for transfers between devices, shards_units(): lax.psum_scatter(mixture_part.astype(jnp.bfloat16), 'fs', scatter_dimensi...  67.6 us
    reduce_scatter x1, waiting for transfers between devices, shards_units(): lax.psum_scatter(qkv_grad.astype(jnp.bfloat16), 'fs', scatter_dimension=1...  59.4 us
    psum x1, waiting for transfers between devices, shards_units(): back_sum = lax.psum(back_own, 'tp').astype(jnp.float32)  54.7 us
    psum x1, waiting for transfers between devices, shards_units(): lax.psum(branch_part.astype(jnp.bfloat16), 'tp').astype(jnp.float32)  51.9 us
    unnamed x146, local copies, waits for them, and re-layouts  45.4 us
  transfers between devices with their start and end apart: 18, of which 14 were waited for; matrix products, arithmetic and copies ran while one was open for 17% of the time, Pallas kernels for 0%

profile of v1, /device:TPU:0, one launch (start us, length us, event | category | flops | bytes accessed | tf_op | source)
XLA Modules:
  0.0 1032.3 jit_solution(17848265531594810003)
XLA Ops:
  9.5 10.5 %all_gather.21 = bf16[11,2048]{1,0:T(8,128)(2,1)S(1)} all-gather(bf16[11,256]{1,0:T(8,128)(2,1)S(1)} %pad_maximum_fusion.10), channel_id=1, replica_groups=mesh['fs'=8,'tp'=4] {'fs'}, dimensions={1}, use_global_device_ids=true | all-gather | bytes 50688 | tf_op jit(solution)/shard_map/all_gather | solution.py:469
  22.3 35.9 %all-gather.8.cloned.1.call-done = bf16[3,2048,512]{2,1,0:T(8,128)(2,1)} async-done(((bf16[3,256,512]{2,1,0:T(8,128)(2,1)}), bf16[3,2048,512]{2,1,0:T(8,128)(2,1)}) %all-gather.8.cloned.1.call-update) | async-done | bytes 6291472 | tf_op jit(solution)/shard_map/all_gather | solution.py:473
  58.2 4.7 convolution_bitcast_fusion.4
  72.4 25.8 %all-gather.10.cloned.1.call-done = bf16[2048,512]{0,1:T(8,128)(2,1)} async-done(((bf16[256,512]{0,1:T(8,128)(2,1)}), bf16[2048,512]{0,1:T(8,128)(2,1)}) %all-gather.10.cloned.1.call-update) | async-done | bytes 2097168 | tf_op jit(solution)/shard_map/all_gather | solution.py:532
  98.2 3.2 reshape.317
  101.4 3.9 copy.280
  105.3 23.2 %all-gather.18.cloned.1.call-done = bf16[1,2048,512]{2,1,0:T(8,128)(2,1)} async-done(((bf16[1,256,512]{2,1,0:T(8,128)(2,1)}), bf16[1,2048,512]{2,1,0:T(8,128)(2,1)}) %all-gather.18.cloned.1.call-update) | async-done | bytes 2097168 | tf_op jit(solution)/shard_map/all_gather | solution.py:533
  128.6 4.0 reshape.288
  135.5 7.1 while.28
  136.8 4.6 conditional.6
  145.2 13.3 %all-gather.12.cloned.1.call-done = bf16[512,2048]{1,0:T(8,128)(2,1)} async-done(((bf16[512,256]{1,0:T(8,128)(2,1)}), bf16[512,2048]{1,0:T(8,128)(2,1)}) %all-gather.12.cloned.1.call-update) | async-done | bytes 2097168 | tf_op jit(solution)/shard_map/all_gather | solution.py:474
  158.5 3.6 convolution_convert_fusion.3
  162.3 51.9 %all-reduce.4.cloned.1.call-done = bf16[256,2048]{0,1:T(8,128)(2,1)} async-done(((bf16[256,2048]{0,1:T(8,128)(2,1)}), bf16[256,2048]{0,1:T(8,128)(2,1)}) %all-reduce.4.cloned.1.call-update) | async-done | bytes 1048592 | tf_op jit(solution)/shard_map/psum | solution.py:567
  218.7 6.8 concatenate.51
  226.3 4.8 copy.285
  234.4 4.1 pad_maximum_fusion
  238.6 4.8 all-to-all-start
  243.9 98.1 %all-to-all-done = bf16[8,3,528,256]{3,2,1,0:T(8,128)(2,1)} async-done(((bf16[8,3,528,256]{3,2,1,0:T(8,128)(2,1)}), bf16[8,3,528,256]{3,2,1,0:T(8,128)(2,1)}, u32[]{:S(2)}, u32[]{:S(2)}) %all-to-all-start) | async-done | bytes 6488096 | tf_op jit(solution)/shard_map/all_to_all | solution.py:488
  342.1 3.3 fusion.106
  351.4 11.5 %fusion.51 = f32[2048,528]{0,1:T(8,128)} fusion(bf16[528,2048]{1,0:T(8,128)(2,1)} %bitcast.257, bf16[2048,2176]{0,1:T(8,128)(2,1)} %all-gather.14.cloned.1.call-done), kind=kOutput, calls=%fused_computation.81 | convolution fusion | flops 4429185024 | bytes 14876672 | tf_op jit(solution)/shard_map/td,ud->tu/dot_general | solution.py:604
  362.9 6.2 fusion.53
  369.1 32.7 %all-gather.16.cloned.1.call-done = bf16[2048,2048]{1,0:T(8,128)(2,1)} async-done(((bf16[256,2048]{1,0:T(8,128)(2,1)}), bf16[2048,2048]{1,0:T(8,128)(2,1)}) %all-gather.16.cloned.1.call-update) | async-done | bytes 8388624 | tf_op jit(solution)/shard_map/all_gather | solution.py:489
  401.8 13.4 %select_reduce_fusion = (bf16[2048]{0:T(1024)(128)(2,1)S(1)}, f32[2048]{0:T(1024)S(1)}, f32[2048,528]{0,1:T(8,128)}, bf16[2048,528]{0,1:T(8,128)(2,1)S(1)}, bf16[2048,528]{0,1:T(8,128)(2,1)S(1)}) fusion(pred[528]{0:T(1024)(128)(4,1)S(1)} %iota_compare_fusion.1, f32[2048,528]{0,1:T(8,128)} %fusion.53, f32[2048,528]{0,1:T(8,128)} %fusion.51, ...), kind=kOutput, calls=%fused_computation.87 | convolution fusion | flops 4451889152 | bytes 27882000 | tf_op jit(solution)/shard_map/td,ud->tu/dot_general | solution.py:610
  415.3 10.4 %fusion.110 = f32[2048,2048]{0,1:T(8,128)} fusion(bf16[2048,528]{0,1:T(8,128)(2,1)S(1)} %get-tuple-element.709, bf16[528,2048]{1,0:T(8,128)(2,1)S(1)} %bitcast.258), kind=kOutput, calls=%fused_computation.206 | convolution fusion | flops 4429185024 | bytes 21102592 | tf_op jit(solution)/shard_map/tu,ud->td/dot_general | solution.py:637
  425.8 12.4 %add_convert_fusion = bf16[2048,2048]{0,1:T(8,128)(2,1)} fusion(f32[2048,2048]{0,1:T(8,128)} %fusion.110, bf16[2048,528]{0,1:T(8,128)(2,1)S(1)} %get-tuple-element.710, bf16[528,2048]{1,0:T(8,128)(2,1)S(1)} %bitcast.256), kind=kOutput, calls=%fused_computation.68 | convolution fusion | flops 4437573632 | bytes 29491200 | tf_op jit(solution)/shard_map/tu,ud->td/dot_general | solution.py:639
  438.3 39.6 %concatenate.55 = bf16[2048,2176]{0,1:T(8,128)(2,1)} concatenate(bf16[2048,2048]{0,1:T(8,128)(2,1)} %add_convert_fusion, bf16[2048,8]{0,1:T(8,128)(2,1)S(1)} %multiply_convert_fusion.3, bf16[2048,1]{0,1:T(2,128)(2,1)S(1)} %broadcast_in_dim.186, bf16[2048,119]{0,1:T(8,128)(2,1)S(1)} %broadcast_in_dim.187), dimensions={1} | concatenate | bytes 17825792 | tf_op jit(solution)/shard_map/concatenate | solution.py:650
  478.0 73.9 %reduce-scatter.12.cloned.1.call-done = bf16[256,2176]{0,1:T(8,128)(2,1)} async-done(((bf16[2048,2176]{0,1:T(8,128)(2,1)}), bf16[256,2176]{0,1:T(8,128)(2,1)}) %reduce-scatter.12.cloned.1.call-update) | async-done | bytes 1114128 | tf_op jit(solution)/shard_map/reduce_scatter | solution.py:651
  553.5 54.7 %all-reduce.6.cloned.1.call-done = bf16[256,2176]{0,1:T(8,128)(2,1)} async-done(((bf16[256,2176]{0,1:T(8,128)(2,1)}), bf16[256,2176]{0,1:T(8,128)(2,1)}) %all-reduce.6.cloned.1.call-update) | async-done | bytes 1114128 | tf_op jit(solution)/shard_map/psum | solution.py:652
  617.3 19.3 %while.29 = (s32[]{:T(128)}, f32[2,128,4,128]{3,1,2,0:T(8,128)}, bf16[2,1024,1024]{2,1,0:T(8,128)(2,1)}, s32[2]{0:T(128)S(1)}, s32[]{:T(128)}, /*index=5*/s32[25...) while((s32[]{:T(128)}, f32[2,128,4,128]{3,1,2,0:T(8,128)}, ...), condition=%wide.region_24.25_spmd.clone, body=%wide.region_21.24_spmd.clone.sunk | while | flops 681247360 | bytes 40258456 | solution.py:761
  618.6 8.4 conditional.7
  638.2 11.7 %convolution_convert_fusion = bf16[2048,2048]{0,1:T(8,128)(2,1)} fusion(bf16[528,2048]{1,0:T(8,128)(2,1)S(1)} %bitcast.254, f32[2048,528]{0,1:T(8,128)} %get-tuple-element.704, f32[2048]{0:T(1024)S(1)} %bitcast.295, f32[2048]{0:T(1024)S(1)} %fusion.86, pred[528]{0:T(1024)(128)(4,1)S(1)} %copy-done.57), kind=kOutput, calls=%fused_computation.69 | convolution fusion | flops 4436623360 | bytes 14893584 | tf_op jit(solution)/shard_map/tu,ud->td/dot_general | solution.py:625
  651.6 43.4 %reduce-scatter.14.cloned.1.call-done = bf16[256,1024]{1,0:T(8,128)(2,1)} async-done(((bf16[2048,1024]{1,0:T(8,128)(2,1)}), bf16[256,1024]{1,0:T(8,128)(2,1)}) %reduce-scatter.14.cloned.1.call-update) | async-done | bytes 524304 | tf_op jit(solution)/shard_map/reduce_scatter | solution.py:762
  696.8 5.7 fusion.68
  702.6 67.6 %reduce-scatter.8.cloned.1.call-done = bf16[256,2048]{0,1:T(8,128)(2,1)} async-done(((bf16[2048,2048]{0,1:T(8,128)(2,1)}), bf16[256,2048]{0,1:T(8,128)(2,1)}) %reduce-scatter.8.cloned.1.call-update) | async-done | bytes 1048592 | tf_op jit(solution)/shard_map/reduce_scatter | solution.py:628
  770.3 10.8 %convolution_convert_fusion.1 = bf16[528,2048]{1,0:T(8,128)(2,1)} fusion(bf16[2048,2048]{1,0:T(8,128)(2,1)} %all-gather.16.cloned.1.call-done, f32[2048,528]{0,1:T(8,128)} %get-tuple-element.704, f32[2048]{0:T(1024)S(1)} %bitcast.296, f32[2048]{0:T(1024)S(1)} %fusion.86, pred[528]{0:T(1024)(128)(4,1)S(1)} %copy-done.57), kind=kOutput, calls=%fused_computation.102 | convolution fusion | flops 4433510400 | bytes 14893584 | tf_op jit(solution)/shard_map/tu,td->ud/dot_general | solution.py:660
  783.7 8.9 fusion.61
  798.0 4.9 fusion.64
  806.9 18.0 %all-reduce.8.cloned.1.call-done = bf16[256,2048]{0,1:T(8,128)(2,1)} async-done(((bf16[256,2048]{0,1:T(8,128)(2,1)}), bf16[256,2048]{0,1:T(8,128)(2,1)}) %all-reduce.8.cloned.1.call-update) | async-done | bytes 1048592 | tf_op jit(solution)/shard_map/psum | solution.py:784
  828.0 5.8 convert_bitcast_fusion
  833.8 6.6 maximum_bitcast_fusion.1
  840.4 4.8 all-to-all-start.1
  845.3 82.1 %all-to-all-done.1 = bf16[8,3,528,256]{3,2,1,0:T(8,128)(2,1)} async-done(((bf16[8,3,528,256]{3,2,1,0:T(8,128)(2,1)}), bf16[8,3,528,256]{3,2,1,0:T(8,128)(2,1)}, u32[]{:S(2)}, u32[]{:S(2)}) %all-to-all-start.1) | async-done | bytes 6488096 | tf_op jit(solution)/shard_map/all_to_all | solution.py:665
  927.4 4.3 copy_convert_fusion
  937.7 3.1 copy.315
  940.9 5.5 copy.316
  946.4 3.6 slice_bitcast_fusion.1
  953.8 3.2 fusion.71
  963.6 59.4 %reduce-scatter.16.cloned.1.call-done = bf16[3,256,512]{1,2,0:T(8,128)(2,1)} async-done(((bf16[3,2048,512]{1,2,0:T(8,128)(2,1)}), bf16[3,256,512]{1,2,0:T(8,128)(2,1)}) %reduce-scatter.16.cloned.1.call-update) | async-done | bytes 786448 | tf_op jit(solution)/shard_map/reduce_scatter | solution.py:797
  (320 shorter events, 108.7 us)
Async XLA Ops:
  7.2 51.0 %all-gather.8.cloned.1.call-start = ((), (), s32[]{:S(2)}) async-start(), calls=%async_computation.9 | async-start | bytes 7077888 | tf_op jit(solution)/shard_map/all_gather | solution.py:473
  7.9 90.2 %all-gather.10.cloned.1.call-start = ((), (), s32[]{:S(2)}) async-start(), calls=%async_computation.10 | async-start | bytes 2359296 | tf_op jit(solution)/shard_map/all_gather | solution.py:532
  20.7 42.2 %copy-start.39 = (f32[256]{0:T(256)}, f32[256]{0:T(256)S(1)}, u32[]{:S(2)}) copy-start(f32[256]{0:T(256)S(1)} %add_rsqrt_fusion.1) | copy-start | bytes 3076
  21.3 41.6 %copy-start.33 = (f32[1,2048]{1,0:T(1,128)}, f32[1,2048]{1,0:T(1,128)S(1)}, u32[]{:S(2)}) copy-start(f32[1,2048]{1,0:T(1,128)S(1)} %get-tuple-element.736) | copy-start | bytes 24580
  21.3 194.6 %copy-start.37 = (f32[1,2048]{1,0:T(1,128)}, f32[1,2048]{1,0:T(1,128)S(1)}, u32[]{:S(2)}) copy-start(f32[1,2048]{1,0:T(1,128)S(1)} %get-tuple-element.735) | copy-start | bytes 24580
  22.3 45.0 %copy-start.24 = (f32[256,64]{0,1:T(8,128)}, f32[256,64]{0,1:T(8,128)S(1)}, u32[]{:S(2)}) copy-start(f32[256,64]{0,1:T(8,128)S(1)} %get-tuple-element.739) | copy-start | bytes 196612
  69.8 58.8 %all-gather.18.cloned.1.call-start = ((), (), s32[]{:S(2)}) async-start(), calls=%async_computation.24 | async-start | bytes 2359296 | tf_op jit(solution)/shard_map/all_gather | solution.py:533
  70.6 87.9 %all-gather.12.cloned.1.call-start = ((), (), s32[]{:S(2)}) async-start(), calls=%async_computation.11 | async-start | bytes 2359296 | tf_op jit(solution)/shard_map/all_gather | solution.py:474
  71.2 142.9 %all-reduce.4.cloned.1.call-start = ((), (), s32[]{:S(2)}) async-start(), calls=%async_computation.12 | async-start | bytes 2097152 | tf_op jit(solution)/shard_map/psum | solution.py:567
  142.6 19.5 %copy-start.6 = (bf16[2,4,2,128,4,128]{5,3,1,4,2,0:T(8,128)(2,1)}, bf16[2,4,2,128,4,128]{5,3,1,4,2,0:T(8,128)(2,1)S(1)}, u32[]{:S(2)}) copy-start(bf16[2,4,2,128,4,128]{5,3,1,4,2,0:T(8,128)(2,1)S(1)} %get-tuple-element.1026) | copy-start | bytes 6291460
  162.2 188.1 %all-gather.14.cloned.1.call-start = ((), (), s32[]{:S(2)}) async-start(), calls=%async_computation.13 | async-start | bytes 10027008 | tf_op jit(solution)/shard_map/all_gather | solution.py:595
  162.2 54.1 %copy-start.27 = (bf16[11,2048]{1,0:T(8,128)(2,1)S(1)}, bf16[11,2048]{1,0:T(8,128)(2,1)}, u32[]{:S(2)}) copy-start(bf16[11,2048]{1,0:T(8,128)(2,1)} %copy-done.26) | copy-start | bytes 135172
  225.6 176.2 %all-gather.16.cloned.1.call-start = ((), (), s32[]{:S(2)}) async-start(), calls=%async_computation.16 | async-start | bytes 9437184 | tf_op jit(solution)/shard_map/all_gather | solution.py:489
  238.6 103.5 %all-to-all-start = ((bf16[8,3,528,256]{3,2,1,0:T(8,128)(2,1)}), bf16[8,3,528,256]{3,2,1,0:T(8,128)(2,1)}, u32[]{:S(2)}, u32[]{:S(2)}) async-start(bf16[8,3,528,256]{3,2,1,0:T(8,128)(2,1)} %pad_maximum_fusion), calls=%async_computation | async-start | bytes 12976128 | tf_op jit(solution)/shard_map/all_to_all | solution.py:488
  243.4 308.5 %reduce-scatter.12.cloned.1.call-start = ((), (), s32[]{:S(2)}) async-start(), calls=%async_computation.17 | async-start | bytes 10027008 | tf_op jit(solution)/shard_map/reduce_scatter | solution.py:651
  243.9 157.9 %copy-start.56 = (pred[528]{0:T(1024)(128)(4,1)}, pred[528]{0:T(1024)(128)(4,1)S(1)}, u32[]{:S(2)}) copy-start(pred[528]{0:T(1024)(128)(4,1)S(1)} %iota_compare_fusion.1) | copy-start | bytes 1588
  351.2 11.7 %slice-start = ((s8[8912896]{0:T(1024)(128)(4,1)}), s8[4194304]{0:T(1024)(128)(4,1)S(1)}, s32[]{:S(2)}) async-start(s8[8912896]{0:T(1024)(128)(4,1)} %bitcast.299), calls=%async_computation.25 | async-start | bytes 8388608
  351.2 50.6 %copy-start.50 = (f32[2048,1]{0,1:T(1,128)}, f32[2048,1]{0,1:T(1,128)S(1)}, u32[]{:S(2)}) copy-start(f32[2048,1]{0,1:T(1,128)S(1)} %slice.173) | copy-start | bytes 24580
  351.3 11.5 %copy-start.19 = (bf16[66,8,8,256]{3,1,2,0:T(8,128)(2,1)S(1)}, bf16[66,8,8,256]{3,1,2,0:T(8,128)(2,1)}, u32[]{:S(2)}) copy-start(bf16[66,8,8,256]{3,1,2,0:T(8,128)(2,1)} %copy.354) | copy-start | bytes 6488068
  351.3 11.5 %slice-start.1 = ((s8[8912896]{0:T(1024)(128)(4,1)}), s8[4194304]{0:T(1024)(128)(4,1)S(1)}, s32[]{:S(2)}) async-start(s8[8912896]{0:T(1024)(128)(4,1)} %bitcast.299), calls=%async_computation.26 | async-start | bytes 8388608
  351.4 11.5 %slice-start.2 = ((s8[8912896]{0:T(1024)(128)(4,1)}), s8[524288]{0:T(1024)(128)(4,1)S(1)}, s32[]{:S(2)}) async-start(s8[8912896]{0:T(1024)(128)(4,1)} %bitcast.299), calls=%async_computation.27 | async-start | bytes 1048576
  401.8 13.5 %copy-start.21 = (bf16[66,8,8,256]{3,1,2,0:T(8,128)(2,1)S(1)}, bf16[66,8,8,256]{3,1,2,0:T(8,128)(2,1)}, u32[]{:S(2)}) copy-start(bf16[66,8,8,256]{3,1,2,0:T(8,128)(2,1)} %copy.353) | copy-start | bytes 6488068
  415.3 10.5 %copy-start.58 = (bf16[2048,528]{0,1:T(8,128)(2,1)}, bf16[2048,528]{0,1:T(8,128)(2,1)S(1)}, u32[]{:S(2)}) copy-start(bf16[2048,528]{0,1:T(8,128)(2,1)S(1)} %get-tuple-element.710) | copy-start | bytes 6488068
  415.3 10.5 %copy-start.20 = (bf16[66,8,8,256]{3,1,2,0:T(8,128)(2,1)S(1)}, bf16[66,8,8,256]{3,1,2,0:T(8,128)(2,1)}, u32[]{:S(2)}) copy-start(bf16[66,8,8,256]{3,1,2,0:T(8,128)(2,1)} %copy.354) | copy-start | bytes 6488068
  477.9 75.6 %copy-start.45 = (bf16[2048]{0:T(1024)(128)(2,1)S(1)}, bf16[2048]{0:T(1024)(128)(2,1)}, u32[]{:S(2)}) copy-start(bf16[2048]{0:T(1024)(128)(2,1)} %get-tuple-element.734) | copy-start | bytes 12292
  477.9 130.4 %all-reduce.6.cloned.1.call-start = ((), (), s32[]{:S(2)}) async-start(), calls=%async_computation.18 | async-start | bytes 2228224 | tf_op jit(solution)/shard_map/psum | solution.py:652
  551.9 143.1 %reduce-scatter.14.cloned.1.call-start = ((), (), s32[]{:S(2)}) async-start(), calls=%async_computation.19 | async-start | bytes 4718592 | tf_op jit(solution)/shard_map/reduce_scatter | solution.py:762
  553.4 56.2 %copy-start.42 = (f32[256]{0:T(256)S(1)}, f32[256]{0:T(256)}, u32[]{:S(2)}) copy-start(f32[256]{0:T(256)} %copy-done.41) | copy-start | bytes 3076
  553.4 56.2 %copy-start.44 = (f32[256]{0:T(256)S(1)}, f32[256]{0:T(256)}, u32[]{:S(2)}) copy-start(f32[256]{0:T(256)} %copy-done.43) | copy-start | bytes 3076
  553.5 57.0 %copy-start.49 = (f32[1,256]{1,0:T(1,128)S(1)}, f32[1,256]{1,0:T(1,128)}, u32[]{:S(2)}) copy-start(f32[1,256]{1,0:T(1,128)} %copy-done.48) | copy-start | bytes 3076
  553.5 57.0 %copy-start.38 = (f32[1,2048]{1,0:T(1,128)S(1)}, f32[1,2048]{1,0:T(1,128)}, u32[]{:S(2)}) copy-start(f32[1,2048]{1,0:T(1,128)} %copy-done.37) | copy-start | bytes 24580
  553.5 57.0 %copy-start.47 = (f32[256]{0:T(256)S(1)}, f32[256]{0:T(256)}, u32[]{:S(2)}) copy-start(f32[256]{0:T(256)} %copy-done.46) | copy-start | bytes 3076
  636.6 133.6 %reduce-scatter.8.cloned.1.call-start = ((), (), s32[]{:S(2)}) async-start(), calls=%async_computation.14 | async-start | bytes 9437184 | tf_op jit(solution)/shard_map/reduce_scatter | solution.py:628
  649.9 175.0 %all-reduce.8.cloned.1.call-start = ((), (), s32[]{:S(2)}) async-start(), calls=%async_computation.20 | async-start | bytes 2097152 | tf_op jit(solution)/shard_map/psum | solution.py:784
  651.2 45.1 %copy-start.25 = (f32[256,64]{0,1:T(8,128)S(1)}, f32[256,64]{0,1:T(8,128)}, u32[]{:S(2)}) copy-start(f32[256,64]{0,1:T(8,128)} %copy-done.24) | copy-start | bytes 196612
  651.2 45.1 %copy-start.32 = (f32[256,64]{0,1:T(8,128)S(1)}, f32[256,64]{0,1:T(8,128)}, u32[]{:S(2)}) copy-start(f32[256,64]{0,1:T(8,128)} %get-tuple-element.737) | copy-start | bytes 196612
  702.6 247.4 %reduce-scatter.10.cloned.1.call-start = ((), (), s32[]{:S(2)}) async-start(), calls=%async_computation.15 | async-start | bytes 1310720 | tf_op jit(solution)/shard_map/reduce_scatter | solution.py:631
  770.2 10.9 %copy-start.4 = (f32[256,2048]{0,1:T(8,128)S(1)}, f32[256,2048]{0,1:T(8,128)}, u32[]{:S(2)}) copy-start(f32[256,2048]{0,1:T(8,128)} %copy-done.3) | copy-start | bytes 6291460
  770.2 10.9 %copy-start.16 = (bf16[2,128,4,128]{3,2,1,0:T(4,128)(2,1)S(1)}, bf16[2,128,4,128]{3,2,1,0:T(4,128)(2,1)}, u32[]{:S(2)}) copy-start(bf16[2,128,4,128]{3,2,1,0:T(4,128)(2,1)} %copy.283) | copy-start | bytes 786436
  770.2 181.8 %reduce-scatter.18.cloned.1.call-start = ((), (), s32[]{:S(2)}) async-start(), calls=%async_computation.22 | async-start | bytes 2359296 | tf_op jit(solution)/shard_map/reduce_scatter | solution.py:800
  783.2 176.6 %reduce-scatter.20.cloned.1.call-start = ((), (), s32[]{:S(2)}) async-start(), calls=%async_computation.23 | async-start | bytes 73728 | tf_op jit(solution)/shard_map/reduce_scatter | solution.py:794
  783.7 14.0 %slice-start.3 = ((s8[8912896]{0:T(1024)(128)(4,1)}), s8[4194304]{0:T(1024)(128)(4,1)S(1)}, s32[]{:S(2)}) async-start(s8[8912896]{0:T(1024)(128)(4,1)} %bitcast.301), calls=%async_computation.28 | async-start | bytes 8388608
  783.7 14.0 %slice-start.4 = ((s8[8912896]{0:T(1024)(128)(4,1)}), s8[4194304]{0:T(1024)(128)(4,1)S(1)}, s32[]{:S(2)}) async-start(s8[8912896]{0:T(1024)(128)(4,1)} %bitcast.301), calls=%async_computation.29 | async-start | bytes 8388608
  805.4 19.5 %copy-start.34 = (f32[1,2048]{1,0:T(1,128)S(1)}, f32[1,2048]{1,0:T(1,128)}, u32[]{:S(2)}) copy-start(f32[1,2048]{1,0:T(1,128)} %copy-done.33) | copy-start | bytes 24580
  805.4 19.5 %copy-start.40 = (f32[256]{0:T(256)S(1)}, f32[256]{0:T(256)}, u32[]{:S(2)}) copy-start(f32[256]{0:T(256)} %copy-done.39) | copy-start | bytes 3076
  805.4 22.6 %copy-start.29 = (bf16[1,256,512]{2,1,0:T(8,128)(2,1)S(1)}, bf16[1,256,512]{2,1,0:T(8,128)(2,1)}, u32[]{:S(2)}) copy-start(bf16[1,256,512]{2,1,0:T(8,128)(2,1)} %copy-done.28) | copy-start | bytes 786436
  827.8 195.2 %reduce-scatter.16.cloned.1.call-start = ((), (), s32[]{:S(2)}) async-start(), calls=%async_computation.21 | async-start | bytes 7077888 | tf_op jit(solution)/shard_map/reduce_scatter | solution.py:797
  840.4 86.9 %all-to-all-start.1 = ((bf16[8,3,528,256]{3,2,1,0:T(8,128)(2,1)}), bf16[8,3,528,256]{3,2,1,0:T(8,128)(2,1)}, u32[]{:S(2)}, u32[]{:S(2)}) async-start(bf16[8,3,528,256]{3,2,1,0:T(8,128)(2,1)} %maximum_bitcast_fusion.1), calls=%async_computation.8 | async-start | bytes 12976128 | tf_op jit(solution)/shard_map/all_to_all | solution.py:665
  (37 other events, 109.7 us)
Sparse Core Ops, SparseCore 0:
  9.9 48.2 all-gather.7
  69.9 28.1 all-gather.9
  100.6 27.8 all-gather.17
  130.3 28.1 all-gather.11
  162.3 51.8 all-reduce.3
  225.7 103.0 all-gather.13
  330.8 70.9 all-gather.15
  478.0 73.8 reduce-scatter.11
  554.4 53.8 all-reduce.5
  636.7 58.2 reduce-scatter.13
  698.8 71.2 reduce-scatter.7
  773.0 51.8 all-reduce.7
  827.3 26.5 reduce-scatter.9
  857.5 66.7 reduce-scatter.17
  927.4 30.5 reduce-scatter.19
  961.2 61.7 reduce-scatter.15

commit v2 on v0

--- a/solution.py
+++ b/solution.py
@@ -3,11 +3,14 @@
 import jax
 import jax.numpy as jnp
 from jax import lax
+from jax.experimental import pallas as pl
+from jax.experimental.pallas import tpu as pltpu
 from jax.sharding import PartitionSpec as P
 
 HD = 128
 E = 8
 SEQ_DEV = 128
+SIDE = 128
 
 
 NORM_EPS = 1e-06
@@ -47,7 +50,7 @@
     return (key_pos <= query_pos[None, :, None, None]) & (key_pos >= query_start[:, :, None, None])
 
 
-def shards(
+def shards_gathered(
     tokens,
     cotangent,
     qkv_weight,
@@ -434,9 +437,722 @@
     )
 
 
+MESH = pl.DeviceIdType.MESH
+X_BIT, Y_BIT, CORE_BIT = 2, 4, 1
+QUARTERS = 4
+SMALL = 16
+
+
+def flip(index, bit):
+    return index + bit - 2 * bit * ((index // bit) % 2)
+
+
+class Links:
+    def __init__(self, send, recv, local):
+        self.fs = lax.axis_index("fs")
+        self.tp = lax.axis_index("tp")
+        self.send, self.recv, self.local = send, recv, local
+        self.used = 0
+        self.used_local = 0
+
+    def peer(self, bits):
+        where = self.fs
+        for bit in (X_BIT, Y_BIT, CORE_BIT):
+            if bits & bit:
+                where = flip(where, bit)
+        return where
+
+    def along(self, step):
+        return lax.rem(self.tp + step, QUARTERS)
+
+    def remote(self, source, target, device, landing):
+        i = self.used
+        self.used += 1
+        out = pltpu.make_async_remote_copy(
+            src_ref=source,
+            dst_ref=target,
+            send_sem=self.send.at[i],
+            recv_sem=self.recv.at[i],
+            device_id=device,
+            device_id_type=MESH,
+        )
+        back = pltpu.make_async_remote_copy(
+            src_ref=landing,
+            dst_ref=landing,
+            send_sem=self.send.at[i],
+            recv_sem=self.recv.at[i],
+            device_id=device,
+            device_id_type=MESH,
+        )
+        return out, back
+
+    def inside(self, source, target):
+        i = self.used_local
+        self.used_local += 1
+        return pltpu.make_async_copy(source, target, self.local.at[i])
+
+    def greet(self, plane, column):
+        barrier = pltpu.get_barrier_semaphore()
+        for bits in plane:
+            pl.semaphore_signal(
+                barrier, inc=1, device_id=(self.peer(bits), self.tp), device_id_type=MESH
+            )
+        for step in column:
+            pl.semaphore_signal(
+                barrier, inc=1, device_id=(self.fs, self.along(step)), device_id_type=MESH
+            )
+        pl.semaphore_wait(barrier, len(plane) + len(column))
+
+
+class Gather:
+    def __init__(self, links, source, place, half):
+        self.links = links
+        fs, tp = links.fs, links.tp
+
+        def to(bits, what, landing, origin=None):
+            return links.remote(
+                what if origin is None else origin, what, (links.peer(bits), tp), landing
+            )
+
+        p = links.peer
+        self.keep = links.inside(source, place(fs))
+        self.to_x = to(X_BIT, place(fs), place(p(X_BIT)), source)
+        self.to_y = to(Y_BIT, place(fs), place(p(Y_BIT)), source)
+        self.to_c = to(CORE_BIT, place(fs), place(p(CORE_BIT)), source)
+        xy = X_BIT + Y_BIT
+        self.x_on = to(Y_BIT, half(p(X_BIT), 0), half(p(xy), 0))
+        self.y_on = to(X_BIT, half(p(Y_BIT), 1), half(p(xy), 1))
+        self.x_core = to(CORE_BIT, place(p(X_BIT)), place(p(X_BIT + CORE_BIT)))
+        self.y_core = to(CORE_BIT, place(p(Y_BIT)), place(p(Y_BIT + CORE_BIT)))
+        self.d_core = [
+            to(CORE_BIT, half(p(xy), h), half(p(xy + CORE_BIT), h)) for h in range(2)
+        ]
+
+    def first(self):
+        self.to_x[0].start()
+        self.to_y[0].start()
+        self.to_c[0].start()
+        self.keep.start()
+
+    def second(self):
+        self.to_x[1].wait_recv()
+        self.x_on[0].start()
+        self.x_core[0].start()
+        self.to_y[1].wait_recv()
+        self.y_on[0].start()
+        self.y_core[0].start()
+
+    def third(self):
+        self.x_on[1].wait_recv()
+        self.d_core[0][0].start()
+        self.y_on[1].wait_recv()
+        self.d_core[1][0].start()
+
+    def last(self):
+        self.keep.wait()
+        for out, back in (self.to_c, self.x_core, self.y_core, *self.d_core):
+            back.wait_recv()
+        for out, back in (
+            self.to_x,
+            self.to_y,
+            self.to_c,
+            self.x_on,
+            self.y_on,
+            self.x_core,
+            self.y_core,
+            *self.d_core,
+        ):
+            out.wait_send()
+
+
+def turn(values, cosine, sine_signed):
+    parts = []
+    for h in range(values.shape[1] // HD):
+        v = values[:, h * HD : (h + 1) * HD]
+        parts.append(v * cosine + pltpu.roll(v, HD // 2, 1) * sine_signed)
+    return jnp.concatenate(parts, axis=1)
+
+
+def matmul(a, b):
+    return jnp.dot(a, b, preferred_element_type=jnp.float32)
+
+
+def matmul_nt(a, b):
+    return lax.dot_general(a, b, (((1,), (1,)), ((), ())), preferred_element_type=jnp.float32)
+
+
+def matmul_tn(a, b):
+    return lax.dot_general(a, b, (((0,), (0,)), ((), ())), preferred_element_type=jnp.float32)
+
+
+def forward_kernel(
+    tokens_ref,
+    cotangent_ref,
+    qkv_ref,
+    out_ref,
+    small_ref,
+    slabs_ref,
+    cos_ref,
+    sin_ref,
+    start_ref,
+    routes_ref,
+    two_ref,
+    residual_ref,
+    scales_ref,
+    attended_ref,
+    query_ref,
+    slabs_all,
+    cotangent_all,
+    kv_out,
+    qkv_out,
+    out_out,
+    small_out,
+    qkv_full,
+    out_full,
+    small_full,
+    kv_own,
+    kv_full,
+    hidden_buf,
+    branch_buf,
+    branch_in,
+    send,
+    recv,
+    local,
+):
+    links = Links(send, recv, local)
+    fs, tp = links.fs, links.tp
+    rows, width = tokens_ref.shape
+    block = width // E
+    local_width = qkv_ref.shape[2]
+    heads = local_width // HD
+    seqs = rows // SEQ_DEV
+    quarter = rows // QUARTERS
+
+    def at_rows(index, size):
+        return pl.ds(pl.multiple_of(index * size, size), size)
+
+    links.greet(range(1, 8), range(1, QUARTERS))
+    small = Gather(
+        links, small_ref, lambda f: small_full.at[f], lambda f, h: small_full.at[f, :, pl.ds(h * 128, 128)]
+    )
+    qkv = Gather(
+        links,
+        qkv_ref,
+        lambda f: qkv_full.at[:, at_rows(f, block)],
+        lambda f, h: qkv_full.at[:, pl.ds(pl.multiple_of(f * block + h * (block // 2), block // 2), block // 2)],
+    )
+    outs = Gather(
+        links,
+        out_ref,
+        lambda f: out_full.at[f],
+        lambda f, h: out_full.at[f, pl.ds(h * (local_width // 2), local_width // 2)],
+    )
+    small.first()
+    qkv.first()
+    small.second()
+    small.third()
+    small.last()
+    tokens = tokens_ref[...].astype(jnp.float32)
+    rstd_one = lax.rsqrt(jnp.mean(tokens * tokens, axis=1, keepdims=True) + NORM_EPS)
+    for b in range(E):
+        cols = slice(b * block, (b + 1) * block)
+        gain = small_full[b, 0:1, :].astype(jnp.float32)
+        hidden_buf[:, cols] = (tokens[:, cols] * rstd_one * gain).astype(jnp.bfloat16)
+    qkv.second()
+    qkv.third()
+    outs.first()
+    qkv.last()
+    hidden = hidden_buf[...]
+    cosine, sine = cos_ref[...], sin_ref[...]
+    kv_own[:, :local_width] = turn(matmul(hidden, qkv_full[1]), cosine, sine).astype(jnp.bfloat16)
+    kv_own[:, local_width:] = matmul(hidden, qkv_full[2]).astype(jnp.bfloat16)
+    kv = Gather(
+        links,
+        kv_own,
+        lambda f: kv_full.at[f],
+        lambda f, h: kv_full.at[f, pl.ds(h * SEQ_DEV, SEQ_DEV)],
+    )
+    kv.first()
+    qkv_keep = links.inside(qkv_full, qkv_out)
+    qkv_keep.start()
+    query_ref[...] = turn(matmul(hidden, qkv_full[0]), cosine, sine).astype(jnp.bfloat16)
+    outs.second()
+    kv.second()
+    outs.third()
+    kv.third()
+    slab_copies = []
+    for bits in (6, 7, 2, 3, 4, 5, 1):
+        peer = links.peer(bits)
+        slab_copies.append(
+            links.remote(slabs_ref.at[peer], slabs_all.at[fs], (peer, tp), slabs_all.at[peer])
+        )
+    for out, back in slab_copies:
+        out.start()
+    slab_own = links.inside(slabs_ref.at[fs], slabs_all.at[fs])
+    slab_own.start()
+    cot = Gather(
+        links,
+        cotangent_ref,
+        lambda f: cotangent_all.at[f],
+        lambda f, h: cotangent_all.at[f, pl.ds(h * SEQ_DEV, SEQ_DEV)],
+    )
+    cot.first()
+    kv.last()
+    kv_keep = links.inside(kv_full, kv_out)
+    kv_keep.start()
+    length = E * SEQ_DEV
+    key_pos = lax.broadcasted_iota(jnp.int32, (SEQ_DEV, length), 1)
+    query_pos = fs * SEQ_DEV + lax.broadcasted_iota(jnp.int32, (SEQ_DEV, length), 0)
+    for s in range(seqs):
+        here = slice(s * SEQ_DEV, (s + 1) * SEQ_DEV)
+        allowed = (key_pos <= query_pos) & (key_pos >= start_ref[here, :])
+        for h in range(heads):
+            cols = slice(h * HD, (h + 1) * HD)
+            vcols = slice(local_width + h * HD, local_width + (h + 1) * HD)
+            keys = kv_full[:, here, cols].reshape(length, HD)
+            values = kv_full[:, here, vcols].reshape(length, HD)
+            scores = matmul_nt(query_ref[here, cols], keys) * (HD ** (-0.5))
+            scores = jnp.where(allowed, scores, NEG_FILL)
+            top = jnp.max(scores, axis=1, keepdims=True)
+            weights = jnp.exp(scores - top)
+            weights = weights / jnp.sum(weights, axis=1, keepdims=True)
+            attended_ref[here, cols] = matmul(weights.astype(jnp.bfloat16), values).astype(
+                jnp.bfloat16
+            )
+    outs.last()
+    out_keep = links.inside(out_full, out_out)
+    out_keep.start()
+    small_keep = links.inside(small_full, small_out)
+    small_keep.start()
+    attended = attended_ref[...]
+    for b in range(E):
+        branch_buf[:, b * block : (b + 1) * block] = matmul(attended, out_full[b]).astype(
+            jnp.bfloat16
+        )
+    branch = []
+    for step in range(1, QUARTERS):
+        peer = links.along(step)
+        branch.append(
+            links.remote(
+                branch_buf.at[at_rows(peer, quarter)],
+                branch_in.at[step - 1],
+                (fs, peer),
+                branch_in.at[step - 1],
+            )
+        )
+    for out, back in branch:
+        out.start()
+    cot.second()
+    for out, back in branch:
+        back.wait_recv()
+    mine = at_rows(tp, quarter)
+    total = branch_buf[mine, :].astype(jnp.float32)
+    for step in range(1, QUARTERS):
+        total = total + branch_in[step - 1].astype(jnp.float32)
+    residual = tokens_ref[mine, :].astype(jnp.float32) + total
+    residual_ref[...] = residual
+    rstd_two = lax.rsqrt(jnp.mean(residual * residual, axis=1, keepdims=True) + NORM_EPS)
+    logits = jnp.zeros((quarter, SMALL), jnp.float32)
+    for b in range(E):
+        cols = slice(b * block, (b + 1) * block)
+        gain = small_full[b, 1:2, :].astype(jnp.float32)
+        part = (residual[:, cols] * rstd_two * gain).astype(jnp.bfloat16)
+        two_ref[:, cols] = part
+        logits = logits + matmul_nt(part, small_full[b])
+    lane = lax.broadcasted_iota(jnp.int32, (quarter, SMALL), 1)
+    routed = (lane >= 2) & (lane < 2 + E)
+    masked = jnp.where(routed, logits, NEG_FILL)
+    odds = jnp.exp(masked - jnp.max(masked, axis=1, keepdims=True))
+    odds = jnp.where(routed, odds, 0.0)
+    probs = odds / jnp.sum(odds, axis=1, keepdims=True)
+    routes = routes_ref[mine, :]
+    chosen = jnp.zeros((quarter, SMALL), jnp.float32)
+    for k in range(routes.shape[1]):
+        chosen = chosen + (routes[:, k : k + 1] == lane - 2).astype(jnp.float32)
+    gate_value = 1.0 / (1.0 + jnp.exp(-logits))
+    scales = jnp.where(lane == 2 + E, gate_value, probs * chosen)
+    scales_ref[...] = jnp.concatenate([scales, probs, chosen], axis=1)
+    cot.third()
+    cot.last()
+    for out, back in slab_copies:
+        back.wait_recv()
+    slab_own.wait()
+    for out, back in slab_copies + branch:
+        out.wait_send()
+    for copy in (qkv_keep, kv_keep, out_keep, small_keep):
+        copy.wait()
+
+
+def forward_call(tokens, cotangent, qkv_weight, out_weight, small, slabs, cosine, sine, start, routes):
+    rows, width = tokens.shape
+    block = width // E
+    local_width = qkv_weight.shape[2]
+    quarter = rows // QUARTERS
+    bf, f32 = jnp.bfloat16, jnp.float32
+    sds = jax.ShapeDtypeStruct
+    vmem = pl.BlockSpec(memory_space=pltpu.VMEM)
+    hbm = pl.BlockSpec(memory_space=pl.ANY)
+    outs = [
+        (sds((quarter, width), bf), vmem),
+        (sds((quarter, width), f32), vmem),
+        (sds((quarter, 3 * SMALL), f32), vmem),
+        (sds((rows, local_width), bf), vmem),
+        (sds((rows, local_width), bf), vmem),
+        (sds(slabs.shape, bf), hbm),
+        (sds((E, rows, width), bf), hbm),
+        (sds((E, rows, 2 * local_width), bf), hbm),
+        (sds((3, width, local_width), bf), hbm),
+        (sds((E, local_width, block), bf), hbm),
+        (sds((E, SMALL, block), bf), hbm),
+    ]
+    return pl.pallas_call(
+        forward_kernel,
+        name="attention_forward",
+        out_shape=[o[0] for o in outs],
+        in_specs=[vmem, hbm, hbm, hbm, hbm, hbm, vmem, vmem, vmem, vmem],
+        out_specs=[o[1] for o in outs],
+        scratch_shapes=[
+            pltpu.VMEM((3, width, local_width), bf),
+            pltpu.VMEM((E, local_width, block), bf),
+            pltpu.VMEM((E, SMALL, block), bf),
+            pltpu.VMEM((rows, 2 * local_width), bf),
+            pltpu.VMEM((E, rows, 2 * local_width), bf),
+            pltpu.VMEM((rows, width), bf),
+            pltpu.VMEM((rows, width), bf),
+            pltpu.VMEM((QUARTERS - 1, quarter, width), bf),
+            pltpu.SemaphoreType.DMA((64,)),
+            pltpu.SemaphoreType.DMA((64,)),
+            pltpu.SemaphoreType.DMA((16,)),
+        ],
+        compiler_params=pltpu.CompilerParams(
+            collective_id=1, has_side_effects=True, vmem_limit_bytes=56 * 2**20
+        ),
+    )(tokens, cotangent, qkv_weight, out_weight, small, slabs, cosine, sine, start, routes)
+
+
+def shards_units(
+    tokens,
+    cotangent,
+    qkv_weight,
+    out_weight,
+    norm_gains,
+    router_weight,
+    shared_gate,
+    expert_gate_up,
+    expert_down,
+    shared_gate_up,
+    shared_down,
+    routes,
+    doc_start,
+):
+    tok_rows, width = tokens.shape
+    seq_count = tok_rows // SEQ_DEV
+    local_width = qkv_weight.shape[2]
+    head_count = local_width // HD
+    quarter = tok_rows // QUARTERS
+    score_scale = HD ** (-0.5)
+    fs_index = lax.axis_index("fs")
+    tp_index = lax.axis_index("tp")
+    fs_size = E
+    query_pos = fs_index * SEQ_DEV + jnp.arange(SEQ_DEV, dtype=jnp.int32)
+    positions = jnp.tile(query_pos, seq_count)
+    half_cos, half_sin = rope_tables(positions)
+    cosine = jnp.concatenate([half_cos, half_cos], axis=1)
+    sine = jnp.concatenate([-half_sin, half_sin], axis=1)
+    small = jnp.concatenate(
+        [
+            norm_gains,
+            router_weight,
+            shared_gate[None],
+            jnp.zeros((SMALL - 3 - E, shared_gate.shape[0]), jnp.bfloat16),
+        ],
+        axis=0,
+    )
+    routed_units = expert_down.shape[1]
+    shared_units = shared_down.shape[0] // fs_size
+    units = routed_units + shared_units
+    block = expert_down.shape[2]
+    expert_up_slabs = jnp.transpose(expert_gate_up, (0, 2, 3, 1))
+    shared_up_slabs = jnp.transpose(
+        shared_gate_up.reshape(block, 2, fs_size, shared_units), (2, 1, 3, 0)
+    )
+    up_slabs = jnp.concatenate([expert_up_slabs, shared_up_slabs], axis=2)
+    down_slabs = jnp.concatenate(
+        [expert_down, shared_down.reshape(fs_size, shared_units, block)], axis=1
+    )
+    slabs = jnp.concatenate([up_slabs, down_slabs[:, None]], axis=1)
+    (
+        two_rows,
+        residual_rows,
+        router_rows,
+        attended,
+        query_rows,
+        slabs,
+        cotangent_all,
+        kv_all,
+        qkv_full,
+        out_full,
+        small_full,
+    ) = forward_call(
+        tokens,
+        cotangent,
+        qkv_weight,
+        out_weight,
+        small,
+        slabs.reshape(fs_size, 3 * units, block),
+        cosine,
+        sine,
+        doc_start[:, None],
+        routes,
+    )
+    cotangent_all = cotangent_all.reshape(-1, width)
+    slabs = slabs.reshape(fs_size, 3, units, block)
+    small_rows = jnp.transpose(small_full, (1, 0, 2)).reshape(SMALL, width)
+    scale_rows = router_rows[:, 2 : 3 + E]
+    probs_rows = router_rows[:, SMALL + 2 : SMALL + 2 + E]
+    chosen_rows = router_rows[:, 2 * SMALL + 2 : 2 * SMALL + 2 + E]
+    scales_high = scale_rows.astype(jnp.bfloat16)
+    scales_low = (scale_rows - scales_high.astype(jnp.float32)).astype(jnp.bfloat16)
+    sent = jnp.concatenate(
+        [
+            two_rows,
+            scales_high,
+            scales_low,
+            jnp.zeros((quarter, SIDE - 2 * (E + 1)), jnp.bfloat16),
+        ],
+        axis=1,
+    )
+    hidden_all = lax.all_gather(sent, ("fs", "tp"), axis=0, tiled=True)
+    side_all = hidden_all[:, width : width + 2 * (E + 1)].astype(jnp.float32)
+    scales_all = side_all[:, : E + 1] + side_all[:, E + 1 :]
+    two_all = hidden_all[:, :width]
+    mine = (jnp.arange(E, dtype=jnp.int32) == fs_index).astype(jnp.float32)
+    routed_scale = jnp.sum(scales_all[:, :E] * mine[None, :], axis=1, keepdims=True)
+    is_routed = jnp.arange(units, dtype=jnp.int32)[None, :] < routed_units
+    scale = jnp.where(is_routed, routed_scale, scales_all[:, E:])
+    weights_by_unit = jnp.transpose(slabs, (1, 2, 0, 3)).reshape(3, units, width)
+    gate_part = jnp.einsum(
+        "td,ud->tu", two_all, weights_by_unit[0], preferred_element_type=jnp.float32
+    )
+    up_part = jnp.einsum(
+        "td,ud->tu", two_all, weights_by_unit[1], preferred_element_type=jnp.float32
+    )
+    hidden_grad = jnp.einsum(
+        "td,ud->tu", cotangent_all, weights_by_unit[2], preferred_element_type=jnp.float32
+    )
+    gate_sigmoid = jax.nn.sigmoid(gate_part)
+    silu = gate_part * gate_sigmoid
+    active = silu * up_part
+    hidden = (scale * active).astype(jnp.bfloat16)
+    dots = active * hidden_grad
+    routed_dot = jnp.sum(jnp.where(is_routed, dots, 0.0), axis=1, keepdims=True)
+    shared_dot = jnp.sum(jnp.where(is_routed, 0.0, dots), axis=1, keepdims=True)
+    active_grad = scale * hidden_grad
+    gate_grad = (
+        active_grad * up_part * gate_sigmoid * (1.0 + gate_part * (1.0 - gate_sigmoid))
+    ).astype(jnp.bfloat16)
+    up_grad = (active_grad * silu).astype(jnp.bfloat16)
+    mixture_part = jnp.einsum(
+        "tu,ud->td", hidden, weights_by_unit[2], preferred_element_type=jnp.float32
+    )
+    mixture_own = lax.psum_scatter(
+        mixture_part.astype(jnp.bfloat16), "fs", scatter_dimension=0, tiled=True
+    )
+    residual_placed = lax.dynamic_update_slice(
+        jnp.zeros((tok_rows, width), jnp.float32), residual_rows, (tp_index * quarter, 0)
+    )
+    output = lax.psum_scatter(
+        (mixture_own.astype(jnp.float32) + residual_placed).astype(jnp.bfloat16),
+        "tp",
+        scatter_dimension=1,
+        tiled=True,
+    )
+    input_part = jnp.einsum(
+        "tu,ud->td", gate_grad, weights_by_unit[0], preferred_element_type=jnp.float32
+    ) + jnp.einsum(
+        "tu,ud->td", up_grad, weights_by_unit[1], preferred_element_type=jnp.float32
+    )
+    side_part = jnp.concatenate(
+        [
+            routed_dot * mine[None, :],
+            shared_dot,
+            jnp.zeros((input_part.shape[0], SIDE - E - 1), jnp.float32),
+        ],
+        axis=1,
+    )
+    back_part = jnp.concatenate([input_part, side_part], axis=1).astype(jnp.bfloat16)
+    back_own = lax.psum_scatter(back_part, "fs", scatter_dimension=0, tiled=True)
+    back_rows = lax.psum_scatter(back_own, "tp", scatter_dimension=0, tiled=True).astype(
+        jnp.float32
+    )
+    input_sum = back_rows[:, :width]
+    gate_sum = back_rows[:, width : width + E]
+    shared_sum = back_rows[:, width + E]
+    grad_by_unit = jnp.stack(
+        [
+            jnp.einsum("tu,td->ud", gate_grad, two_all, preferred_element_type=jnp.float32),
+            jnp.einsum("tu,td->ud", up_grad, two_all, preferred_element_type=jnp.float32),
+            jnp.einsum("tu,td->ud", hidden, cotangent_all, preferred_element_type=jnp.float32),
+        ],
+        axis=0,
+    ).astype(jnp.bfloat16)
+    grad_slabs = jnp.transpose(grad_by_unit.reshape(3, units, fs_size, block), (2, 0, 1, 3))
+    grad_slabs = lax.all_to_all(grad_slabs, "fs", 0, 0, tiled=True)
+    token_rows = lax.dynamic_slice_in_dim(tokens, tp_index * quarter, quarter, 0).astype(
+        jnp.float32
+    )
+    cotangent_rows = lax.dynamic_slice_in_dim(cotangent, tp_index * quarter, quarter, 0).astype(
+        jnp.float32
+    )
+    rstd_one = lax.rsqrt(jnp.mean(token_rows * token_rows, axis=1, keepdims=True) + NORM_EPS)
+    normed_one = token_rows * rstd_one
+    rstd_two = lax.rsqrt(jnp.mean(residual_rows * residual_rows, axis=1, keepdims=True) + NORM_EPS)
+    normed_two = residual_rows * rstd_two
+    gate_value = scale_rows[:, E]
+    chosen_grad = chosen_rows * gate_sum
+    logit_grad = (
+        probs_rows * (chosen_grad - jnp.sum(probs_rows * chosen_grad, axis=1, keepdims=True))
+    ).astype(jnp.bfloat16)
+    gate_logit_grad = (shared_sum * gate_value * (1.0 - gate_value)).astype(jnp.bfloat16)
+    router_grad = jnp.einsum("te,td->ed", logit_grad, two_rows, preferred_element_type=jnp.float32)
+    shared_vector_grad = jnp.einsum(
+        "t,td->d", gate_logit_grad, two_rows, preferred_element_type=jnp.float32
+    )
+    two_grad = (
+        input_sum
+        + jnp.einsum(
+            "te,ed->td", logit_grad, small_rows[2 : 2 + E], preferred_element_type=jnp.float32
+        )
+        + gate_logit_grad.astype(jnp.float32)[:, None]
+        * small_rows[2 + E].astype(jnp.float32)[None, :]
+    )
+    scaled_two = two_grad * small_rows[1].astype(jnp.float32)[None, :]
+    gain_two_grad = jnp.sum(two_grad * normed_two, axis=0)
+    residual_grad = cotangent_rows + rstd_two * (
+        scaled_two - normed_two * jnp.mean(scaled_two * normed_two, axis=1, keepdims=True)
+    )
+    branch_grad = lax.all_gather(residual_grad.astype(jnp.bfloat16), "tp", axis=0, tiled=True)
+    out_grad = jnp.einsum("tf,td->fd", attended, branch_grad, preferred_element_type=jnp.float32)
+    attended_grad = jnp.einsum(
+        "tbd,bfd->tf",
+        branch_grad.reshape(tok_rows, fs_size, block),
+        out_full,
+        preferred_element_type=jnp.float32,
+    ).astype(jnp.bfloat16)
+    grad_heads = attended_grad.reshape(seq_count, SEQ_DEV, head_count, HD)
+    query_heads = query_rows.reshape(seq_count, SEQ_DEV, head_count, HD)
+    kv_heads = kv_all.reshape(fs_size, seq_count, SEQ_DEV, 2, head_count, HD)
+    key_heads, value_heads = kv_heads[:, :, :, 0], kv_heads[:, :, :, 1]
+    query_start = doc_start.reshape(seq_count, SEQ_DEV)
+    allowed = key_mask(query_pos, query_start, 0, fs_size)[:, None]
+    scores = (
+        jnp.einsum("pqhd,gpkhd->phqgk", query_heads, key_heads, preferred_element_type=jnp.float32)
+        * score_scale
+    )
+    scores = jnp.where(allowed, scores, NEG_FILL)
+    exps = jnp.exp(scores - jnp.max(scores, axis=(3, 4), keepdims=True))
+    probs = exps / jnp.sum(exps, axis=(3, 4), keepdims=True)
+    weights_grad = jnp.einsum(
+        "pqhd,gpkhd->phqgk", grad_heads, value_heads, preferred_element_type=jnp.float32
+    )
+    delta = jnp.sum(probs * weights_grad, axis=(3, 4), keepdims=True)
+    score_grad = (probs * (weights_grad - delta)).astype(jnp.bfloat16)
+    query_grad = (
+        jnp.einsum("phqgk,gpkhd->pqhd", score_grad, key_heads, preferred_element_type=jnp.float32)
+        * score_scale
+    )
+    key_grad = (
+        jnp.einsum(
+            "phqgk,pqhd->gpkhd", score_grad, query_heads, preferred_element_type=jnp.float32
+        )
+        * score_scale
+    )
+    value_grad = jnp.einsum(
+        "phqgk,pqhd->gpkhd",
+        probs.astype(jnp.bfloat16),
+        grad_heads,
+        preferred_element_type=jnp.float32,
+    )
+    terms = jnp.concatenate(
+        [
+            key_grad.reshape(fs_size * tok_rows, local_width),
+            value_grad.reshape(fs_size * tok_rows, local_width),
+        ],
+        axis=1,
+    ).astype(jnp.bfloat16)
+    key_value_sum = lax.psum_scatter(terms, "fs", scatter_dimension=0, tiled=True).astype(
+        jnp.float32
+    )
+    projected_grad = jnp.stack(
+        [
+            rotate(query_grad.reshape(tok_rows, local_width), half_cos, -half_sin),
+            rotate(key_value_sum[:, :local_width], half_cos, -half_sin),
+            key_value_sum[:, local_width:],
+        ],
+        axis=0,
+    ).astype(jnp.bfloat16)
+    token_all = tokens.astype(jnp.float32)
+    rstd_all = lax.rsqrt(jnp.mean(token_all * token_all, axis=1, keepdims=True) + NORM_EPS)
+    hidden_one = (token_all * rstd_all * small_rows[0].astype(jnp.float32)[None, :]).astype(
+        jnp.bfloat16
+    )
+    qkv_grad = jnp.einsum(
+        "td,jtf->jdf", hidden_one, projected_grad, preferred_element_type=jnp.float32
+    )
+    one_part = jnp.einsum(
+        "jtf,jdf->td", projected_grad, qkv_full, preferred_element_type=jnp.float32
+    )
+    one_grad = lax.psum_scatter(
+        one_part.astype(jnp.bfloat16), "tp", scatter_dimension=0, tiled=True
+    ).astype(jnp.float32)
+    scaled_one = one_grad * small_rows[0].astype(jnp.float32)[None, :]
+    gain_one_grad = jnp.sum(one_grad * normed_one, axis=0)
+    input_grad_rows = residual_grad + rstd_one * (
+        scaled_one - normed_one * jnp.mean(scaled_one * normed_one, axis=1, keepdims=True)
+    )
+    input_grad = lax.all_gather(
+        input_grad_rows.astype(jnp.bfloat16), "tp", axis=0, tiled=True
+    ).astype(jnp.float32)
+    small_grad = jnp.concatenate(
+        [gain_one_grad[None], gain_two_grad[None], router_grad, shared_vector_grad[None]], axis=0
+    )
+    small_own = lax.psum(
+        lax.psum_scatter(
+            small_grad.astype(jnp.bfloat16), "fs", scatter_dimension=1, tiled=True
+        ),
+        "tp",
+    ).astype(jnp.float32)
+    qkv_own = lax.psum_scatter(
+        qkv_grad.astype(jnp.bfloat16), "fs", scatter_dimension=1, tiled=True
+    ).astype(jnp.float32)
+    out_own = lax.psum_scatter(
+        out_grad.astype(jnp.bfloat16), "fs", scatter_dimension=1, tiled=True
+    ).astype(jnp.float32)
+    own = grad_slabs.astype(jnp.float32)
+    expert_up_own = jnp.transpose(own[:, :2, :routed_units], (0, 3, 1, 2))
+    expert_down_own = own[:, 2, :routed_units]
+    shared_up_own = jnp.transpose(own[:, :2, routed_units:], (3, 1, 0, 2)).reshape(
+        shared_gate_up.shape
+    )
+    shared_down_own = own[:, 2, routed_units:].reshape(shared_down.shape)
+    return (
+        output,
+        input_grad,
+        qkv_own,
+        out_own,
+        small_own[:2],
+        small_own[2 : 2 + E],
+        small_own[2 + E],
+        expert_up_own,
+        expert_down_own,
+        shared_up_own,
+        shared_down_own,
+    )
+
+
 def solution(mesh):
     return jax.shard_map(
-        shards,
+        shards_units if dict(mesh.shape) == {"fs": E, "tp": QUARTERS} else shards_gathered,
         mesh=mesh,
         in_specs=(
             P("fs", None),

time: 1390 us -> 905 us (0.65)
  waiting for transfers between devices: 1070 us -> 427 us
  Pallas kernels: 0 us -> 175 us
  local copies, waits for them, and re-layouts: 46.7 us -> 104 us
  blocking collectives: 55.4 us -> 10.1 us
  matrix products: 144 us -> 118 us
    all_gather x8 -> x3, waiting for transfers between devices: 376 us -> 86 us  [the longest x1 68.6 us: shards_units(): hidden_all = lax.all_gather(sent, ('fs', 'tp'), axis=0, tiled=True)]
    reduce_scatter x9, waiting for transfers between devices: 542 us -> 268 us  [the longest x1 72.5 us: shards_units(): lax.psum_scatter(back_part, 'fs', scatter_dimension=0, tiled=True)]
    pallas_call x0 -> x1, Pallas kernels: none -> 175 us  [forward_call(): pl.pallas_call(forward_kernel, name='attention_forward', out_shape=[o[0]...]
    psum x3 -> x0, waiting for transfers between devices: 111 us -> none  [the longest x1 47.7 us: shards(): lax.psum(input_part.astype(jnp.bfloat16), 'tp').astype(jnp.float32)]
    all_to_all x0 -> x1, waiting for transfers between devices: none -> 72.7 us  [shards_units(): grad_slabs = lax.all_to_all(grad_slabs, 'fs', 0, 0, tiled=True)]
    unnamed x22 -> x12, waiting for transfers between devices: 35.7 us -> 0.2 us
    all_gather x3 -> x0, blocking collectives: 28 us -> none  [the longest x1 10.5 us: shards(): lax.all_gather(norm_gains, 'fs', axis=1, tiled=True)]
    dot_general x30 -> x21, matrix products: 144 us -> 118 us  [the longest x1 12.9 us: shards_units(): jnp.einsum('tu,ud->td', up_grad, weights_by_unit[1], preferred_element_ty...]
  transfers between devices with their start and end apart: 21 -> 13, of which waited for: 19 -> 10; matrix products, arithmetic and copies ran while one was open for 11% -> 16% of each run, Pallas kernels for 0% -> 0%
where the time goes in v2:
time: 905 us; the launch traced here: 896 us
  waiting for transfers between devices  427 us (47%)
  Pallas kernels  175 us (19%)
  matrix products  118 us (13%)
  local copies, waits for them, and re-layouts  104 us (11%)
  other arithmetic  42 us (5%)
  between operations  15.6 us (2%)
  blocking collectives  10.1 us (1%)
    pallas_call x1, Pallas kernels, forward_call(): pl.pallas_call(forward_kernel, name='attention_forward', out_shape=[o[0]...  175 us
    all_to_all x1, waiting for transfers between devices, shards_units(): grad_slabs = lax.all_to_all(grad_slabs, 'fs', 0, 0, tiled=True)  72.7 us
    reduce_scatter x1, waiting for transfers between devices, shards_units(): lax.psum_scatter(back_part, 'fs', scatter_dimension=0, tiled=True)  72.5 us
    all_gather x1, waiting for transfers between devices, shards_units(): hidden_all = lax.all_gather(sent, ('fs', 'tp'), axis=0, tiled=True)  68.6 us
    reduce_scatter x1, waiting for transfers between devices, shards_units(): lax.psum_scatter(mixture_part.astype(jnp.bfloat16), 'fs', scatter_dimensi...  61.6 us
    reduce_scatter x1, waiting for transfers between devices, shards_units(): lax.psum_scatter(terms, 'fs', scatter_dimension=0, tiled=True)  35.9 us
    unnamed x136, local copies, waits for them, and re-layouts  31.1 us
    reduce_scatter x1, waiting for transfers between devices, shards_units(): lax.psum_scatter(one_part.astype(jnp.bfloat16), 'tp', scatter_dimension=0...  28.3 us
  transfers between devices with their start and end apart: 13, of which 10 were waited for; matrix products, arithmetic and copies ran while one was open for 16% of the time, Pallas kernels for 0%

profile of v2, /device:TPU:0, one launch (start us, length us, event | category | flops | bytes accessed | tf_op | source)
XLA Modules:
  0.0 896.1 jit_solution(11064046567487649028)
XLA Ops:
  7.3 3.8 copy.150
  17.6 4.1 pad_maximum_fusion
  22.5 174.9 %attention_forward.1 = (bf16[64,2048]{1,0:T(8,128)(2,1)}, f32[64,2048]{1,0:T(8,128)}, f32[64,48]{1,0:T(8,128)}, bf16[256,512]{1,0:T(8,128)(2,1)}, bf16[256,512]{...) custom-call(bf16[256,2048]{1,0:T(8,128)(2,1)} %tokens_ref.1, ...), custom_call_target="tpu_custom_call" | custom-call | tf_op jit(solution)/shard_map/attention_forward/pallas_call | solution.py:808
  200.3 5.4 copy.247
  210.9 68.6 %all-gather.4.cloned.1.call-done = bf16[2048,2176]{1,0:T(8,128)(2,1)} async-done(((bf16[64,2176]{1,0:T(8,128)(2,1)}), bf16[2048,2176]{1,0:T(8,128)(2,1)}) %all-gather.4.cloned.1.call-update) | async-done | bytes 8912912 | tf_op jit(solution)/shard_map/all_gather | solution.py:925
  282.2 10.2 %fusion.6 = f32[2048,528]{0,1:T(8,128)} fusion(bf16[528,2048]{1,0:T(8,128)(2,1)S(1)} %bitcast.180, bf16[2048,2176]{1,0:T(8,128)(2,1)} %all-gather.4.cloned.1.call-done), kind=kOutput, calls=%fused_computation.16 | convolution fusion | flops 4429185024 | bytes 14876672 | tf_op jit(solution)/shard_map/td,ud->tu/dot_general | solution.py:934
  292.5 6.2 fusion.4
  298.8 11.0 %select_reduce_fusion = (bf16[2048]{0:T(1024)(128)(2,1)S(1)}, f32[2048]{0:T(1024)S(1)}, f32[2048,528]{0,1:T(8,128)}, bf16[2048,528]{0,1:T(8,128)(2,1)S(1)}, bf16[2048,528]{0,1:T(8,128)(2,1)S(1)}) fusion(pred[528]{0:T(1024)(128)(4,1)S(1)} %iota_compare_fusion, f32[2048,528]{0,1:T(8,128)} %fusion.4, f32[2048,528]{0,1:T(8,128)} %fusion.6, ...), kind=kOutput, calls=%fused_computation.19 | convolution fusion | flops 4451889152 | bytes 27882000 | tf_op jit(solution)/shard_map/td,ud->tu/dot_general | solution.py:940
  309.8 10.2 %fusion.74 = f32[2048,2048]{1,0:T(8,128)} fusion(bf16[2048,528]{0,1:T(8,128)(2,1)S(1)} %get-tuple-element.97, bf16[528,2048]{1,0:T(8,128)(2,1)S(1)} %bitcast.181), kind=kOutput, calls=%fused_computation.149 | convolution fusion | flops 4429185024 | bytes 21102592 | tf_op jit(solution)/shard_map/tu,ud->td/dot_general | solution.py:970
  320.6 12.9 %add_convert_fusion = bf16[2048,2048]{1,0:T(8,128)(2,1)} fusion(f32[2048,2048]{1,0:T(8,128)} %fusion.74, bf16[2048,528]{0,1:T(8,128)(2,1)S(1)} %get-tuple-element.98, bf16[528,2048]{1,0:T(8,128)(2,1)S(1)} %bitcast.179), kind=kOutput, calls=%fused_computation | convolution fusion | flops 4437573632 | bytes 29491200 | tf_op jit(solution)/shard_map/tu,ud->td/dot_general | solution.py:972
  333.6 13.8 %concatenate.50 = bf16[2048,2176]{1,0:T(8,128)(2,1)} concatenate(bf16[2048,2048]{1,0:T(8,128)(2,1)} %add_convert_fusion, bf16[2048,8]{1,0:T(8,128)(2,1)S(1)} %multiply_convert_fusion.4, bf16[2048,1]{1,0:T(8,128)(2,1)S(1)} %broadcast_in_dim.142, bf16[2048,119]{1,0:T(8,128)(2,1)S(1)} %broadcast_in_dim.136), dimensions={1} | concatenate | bytes 17825792 | tf_op jit(solution)/shard_map/concatenate | solution.py:983
  347.5 72.5 %reduce-scatter.14.cloned.1.call-done = bf16[256,2176]{1,0:T(8,128)(2,1)} async-done(((bf16[2048,2176]{1,0:T(8,128)(2,1)}), bf16[256,2176]{1,0:T(8,128)(2,1)}) %reduce-scatter.14.cloned.1.call-update) | async-done | bytes 1114128 | tf_op jit(solution)/shard_map/reduce_scatter | solution.py:984
  420.1 7.8 reshape.268
  429.8 20.7 %reduce-scatter.16.cloned.1.call-done = bf16[64,2176]{1,0:T(8,128)(2,1)} async-done(((bf16[256,2176]{1,0:T(8,128)(2,1)}), bf16[64,2176]{1,0:T(8,128)(2,1)}) %reduce-scatter.16.cloned.1.call-update) | async-done | bytes 278544 | tf_op jit(solution)/shard_map/reduce_scatter | solution.py:985
  455.3 4.3 fusion.72
  460.5 2.1 copy-done.1
  464.1 17.4 %all-gather.6.cloned.1.call-done = bf16[256,2048]{1,0:T(8,128)(2,1)} async-done(((bf16[64,2048]{1,0:T(8,128)(2,1)}), bf16[256,2048]{1,0:T(8,128)(2,1)}) %all-gather.6.cloned.1.call-update) | async-done | bytes 1048592 | tf_op jit(solution)/shard_map/all_gather | solution.py:1034
  481.5 3.4 fusion.39
  488.4 5.4 convert_bitcast_fusion.2
  501.0 4.2 copy.173
  505.3 2.1 copy.248
  507.5 2.7 pad_maximum_fusion.1
  510.9 11.6 %convolution_convert_fusion = bf16[2048,2048]{1,0:T(8,128)(2,1)} fusion(bf16[528,2048]{1,0:T(8,128)(2,1)} %bitcast.177, f32[2048,528]{0,1:T(8,128)} %get-tuple-element.94, f32[2048]{0:T(1024)S(1)} %copy-done.35, f32[2048]{0:T(1024)S(1)} %copy-done.38, pred[528]{0:T(1024)(128)(4,1)S(1)} %copy-done.50), kind=kOutput, calls=%fused_computation.1 | convolution fusion | flops 4436623360 | bytes 14893584 | tf_op jit(solution)/shard_map/tu,ud->td/dot_general | solution.py:955
  522.6 2.6 fusion.38
  525.3 35.9 %reduce-scatter.18.cloned.1.call-done = bf16[256,1024]{1,0:T(8,128)(2,1)} async-done(((bf16[2048,1024]{1,0:T(8,128)(2,1)}), bf16[256,1024]{1,0:T(8,128)(2,1)}) %reduce-scatter.18.cloned.1.call-update) | async-done | bytes 524304 | tf_op jit(solution)/shard_map/reduce_scatter | solution.py:1083
  564.9 5.8 fusion.19
  570.8 2.1 convolution_convert_fusion.1
  574.2 61.6 %reduce-scatter.10.cloned.1.call-done = bf16[256,2048]{1,0:T(8,128)(2,1)} async-done(((bf16[2048,2048]{1,0:T(8,128)(2,1)}), bf16[256,2048]{1,0:T(8,128)(2,1)}) %reduce-scatter.10.cloned.1.call-update) | async-done | bytes 1048592 | tf_op jit(solution)/shard_map/reduce_scatter | solution.py:958
  637.7 28.3 %reduce-scatter.20.cloned.1.call-done = bf16[64,2048]{1,0:T(8,128)(2,1)} async-done(((bf16[256,2048]{1,0:T(8,128)(2,1)}), bf16[64,2048]{1,0:T(8,128)(2,1)}) %reduce-scatter.20.cloned.1.call-update) | async-done | bytes 262160 | tf_op jit(solution)/shard_map/reduce_scatter | solution.py:1105
  668.1 2.2 fusion.53
  670.4 12.8 %copy.178 = bf16[2048,2048]{1,0:T(8,128)(2,1)} copy(bf16[2048,2048]{0,1:T(8,128)(2,1)} %bitcast.163) | data formatting | bytes 16777216 | tf_op jit(solution)/shard_map/tu,td->ud/dot_general | solution.py:995
  683.5 5.7 convert_bitcast_fusion
  689.3 8.7 fusion.13
  699.6 8.5 fusion.16
  709.4 9.0 %convert_bitcast_fusion.1 = bf16[1,528,8,256]{3,1,2,0:T(8,128)(2,1)S(1)} fusion(bf16[8,256,2048]{2,1,0:T(8,128)(2,1)} %bitcast.167, f32[2048,528]{0,1:T(8,128)S(1)} %bitcast.206, f32[2048]{0:T(1024)S(1)} %copy-done.36, f32[2048]{0:T(1024)S(1)} %copy-done.39, pred[528]{0:T(1024)(128)(4,1)S(1)} %copy-done.51), kind=kOutput, calls=%fused_computation.48 | convolution fusion | flops 4433510400 | bytes 14893584 | tf_op jit(solution)/shard_map/tu,td->ud/dot_general | solution.py:995
  719.2 3.2 copy.181
  722.3 4.8 all-to-all-start
  728.3 72.7 %all-to-all-done = bf16[8,3,528,256]{3,2,1,0:T(8,128)(2,1)} async-done(((bf16[8,3,528,256]{3,2,1,0:T(8,128)(2,1)}), bf16[8,3,528,256]{3,2,1,0:T(8,128)(2,1)}, u32[]{:S(2)}, u32[]{:S(2)}) %all-to-all-start) | async-done | bytes 6488096 | tf_op jit(solution)/shard_map/all_to_all | solution.py:1000
  801.1 4.9 copy_convert_fusion
  807.9 3.7 copy.184
  811.7 2.6 copy-done
  814.3 3.4 copy.185
  817.7 3.6 slice_bitcast_fusion.1
  823.1 10.1 %psum.7 = bf16[11,256]{1,0:T(8,128)(2,1)S(1)} all-reduce(bf16[11,256]{1,0:T(8,128)(2,1)} %reduce-scatter.26.cloned.1.call-done), channel_id=1, replica_groups=mesh['fs'=8,'tp'=4] {'tp'}, use_global_device_ids=true, to_apply=%region_23.24 | all-reduce | flops 2816 | bytes 11264 | tf_op jit(solution)/shard_map/psum | solution.py:1119
  835.0 2.8 convert_element_type.190
  837.8 21.2 %reduce-scatter.22.cloned.1.call-done = bf16[3,256,512]{1,2,0:T(8,128)(2,1)} async-done(((bf16[3,2048,512]{1,2,0:T(8,128)(2,1)}), bf16[3,256,512]{1,2,0:T(8,128)(2,1)}) %reduce-scatter.22.cloned.1.call-update) | async-done | bytes 786448 | tf_op jit(solution)/shard_map/reduce_scatter | solution.py:1125
  859.0 2.6 copy.183
  861.6 27.4 %reduce-scatter.12.cloned.1.call-done = bf16[256,512]{1,0:T(8,128)(2,1)} async-done(((bf16[256,2048]{1,0:T(8,128)(2,1)}), bf16[256,512]{1,0:T(8,128)(2,1)}) %reduce-scatter.12.cloned.1.call-update) | async-done | bytes 262160 | tf_op jit(solution)/shard_map/reduce_scatter | solution.py:964
  (246 shorter events, 59.0 us)
Async XLA Ops:
  7.2 8.2 copy-start.15
  7.2 272.4 %all-gather.4.cloned.1.call-start = ((), (), s32[]{:S(2)}) async-start(), calls=%async_computation.10 | async-start | bytes 9191424 | tf_op jit(solution)/shard_map/all_gather | solution.py:925
  15.4 6.4 copy-start.17
  200.1 219.9 %reduce-scatter.14.cloned.1.call-start = ((), (), s32[]{:S(2)}) async-start(), calls=%async_computation.13 | async-start | bytes 10027008 | tf_op jit(solution)/shard_map/reduce_scatter | solution.py:984
  210.9 87.8 %copy-start.11 = (bf16[66,8,8,256]{3,1,2,0:T(8,128)(2,1)}, bf16[66,8,8,256]{3,1,2,0:T(8,128)(2,1)S(1)}, u32[]{:S(2)}) copy-start(bf16[66,8,8,256]{3,1,2,0:T(8,128)(2,1)S(1)} %copy.213) | copy-start | bytes 6488068
  210.9 87.8 %copy-start.49 = (pred[528]{0:T(1024)(128)(4,1)}, pred[528]{0:T(1024)(128)(4,1)S(1)}, u32[]{:S(2)}) copy-start(pred[528]{0:T(1024)(128)(4,1)S(1)} %iota_compare_fusion) | copy-start | bytes 1588
  281.8 16.9 %copy-start.34 = (f32[2048]{0:T(1024)}, f32[2048]{0:T(1024)S(1)}, u32[]{:S(2)}) copy-start(f32[2048]{0:T(1024)S(1)} %slice_reduce_fusion) | copy-start | bytes 24580
  281.8 10.6 %slice-start.2 = ((s8[8912896]{0:T(1024)(128)(4,1)}), s8[4194304]{0:T(1024)(128)(4,1)S(1)}, s32[]{:S(2)}) async-start(s8[8912896]{0:T(1024)(128)(4,1)} %bitcast.200), calls=%async_computation.24 | async-start | bytes 8388608
  282.2 16.6 %copy-start.37 = (f32[2048]{0:T(1024)}, f32[2048]{0:T(1024)S(1)}, u32[]{:S(2)}) copy-start(f32[2048]{0:T(1024)S(1)} %fusion.44) | copy-start | bytes 24580
  282.2 10.3 %copy-start.12 = (bf16[66,8,8,256]{3,1,2,0:T(8,128)(2,1)S(1)}, bf16[66,8,8,256]{3,1,2,0:T(8,128)(2,1)}, u32[]{:S(2)}) copy-start(bf16[66,8,8,256]{3,1,2,0:T(8,128)(2,1)} %copy.212) | copy-start | bytes 6488068
  282.2 10.2 %slice-start.3 = ((s8[8912896]{0:T(1024)(128)(4,1)}), s8[4194304]{0:T(1024)(128)(4,1)S(1)}, s32[]{:S(2)}) async-start(s8[8912896]{0:T(1024)(128)(4,1)} %bitcast.200), calls=%async_computation.25 | async-start | bytes 8388608
  282.2 10.2 %slice-start.4 = ((s8[8912896]{0:T(1024)(128)(4,1)}), s8[524288]{0:T(1024)(128)(4,1)S(1)}, s32[]{:S(2)}) async-start(s8[8912896]{0:T(1024)(128)(4,1)} %bitcast.200), calls=%async_computation.26 | async-start | bytes 1048576
  282.2 16.5 %slice-start = ((s8[8388608]{0:T(1024)(128)(4,1)}), s8[4194304]{0:T(1024)(128)(4,1)S(1)}, s32[]{:S(2)}) async-start(s8[8388608]{0:T(1024)(128)(4,1)} %bitcast.164), calls=%async_computation.22 | async-start | bytes 8388608
  292.5 6.3 slice-start.1
  309.8 10.2 %copy-start.52 = (bf16[2048,528]{0,1:T(8,128)(2,1)}, bf16[2048,528]{0,1:T(8,128)(2,1)S(1)}, u32[]{:S(2)}) copy-start(bf16[2048,528]{0,1:T(8,128)(2,1)S(1)} %get-tuple-element.97) | copy-start | bytes 6488068
  309.8 10.9 %copy-start.53 = (bf16[2048,528]{0,1:T(8,128)(2,1)}, bf16[2048,528]{0,1:T(8,128)(2,1)S(1)}, u32[]{:S(2)}) copy-start(bf16[2048,528]{0,1:T(8,128)(2,1)S(1)} %get-tuple-element.98) | copy-start | bytes 6488068
  347.4 72.7 %copy-start.29 = (bf16[8,16,256]{2,1,0:T(8,128)(2,1)S(1)}, bf16[8,16,256]{2,1,0:T(8,128)(2,1)}, u32[]{:S(2)}) copy-start(bf16[8,16,256]{2,1,0:T(8,128)(2,1)} %get-tuple-element.27) | copy-start | bytes 196612
  347.4 103.0 %reduce-scatter.16.cloned.1.call-start = ((), (), s32[]{:S(2)}) async-start(), calls=%async_computation.14 | async-start | bytes 1392640 | tf_op jit(solution)/shard_map/reduce_scatter | solution.py:985
  420.0 61.5 %all-gather.6.cloned.1.call-start = ((), (), s32[]{:S(2)}) async-start(), calls=%async_computation.15 | async-start | bytes 1310720 | tf_op jit(solution)/shard_map/all_gather | solution.py:1034
  420.1 7.9 copy-start.22
  420.1 8.8 copy-start.3
  420.1 31.4 %copy-start.16 = (f32[64,48]{1,0:T(8,128)S(1)}, f32[64,48]{1,0:T(8,128)}, u32[]{:S(2)}) copy-start(f32[64,48]{1,0:T(8,128)} %get-tuple-element.23) | copy-start | bytes 36868
  428.0 27.1 %copy-start.42 = (s32[256]{0:T(256)S(1)}, s32[256]{0:T(256)}, u32[]{:S(2)}) copy-start(s32[256]{0:T(256)} %param.25) | copy-start | bytes 3076
  429.1 25.9 %copy-start.40 = (f32[64]{0:T(128)}, f32[64]{0:T(128)S(1)}, u32[]{:S(2)}) copy-start(f32[64]{0:T(128)S(1)} %add_rsqrt_fusion.2) | copy-start | bytes 772
  429.8 25.2 %copy-start.26 = (f32[1,8,256]{2,0,1:T(1,128)}, f32[1,8,256]{2,0,1:T(1,128)S(1)}, u32[]{:S(2)}) copy-start(f32[1,8,256]{2,0,1:T(1,128)S(1)} %get-tuple-element.117) | copy-start | bytes 24580
  454.7 106.5 %reduce-scatter.18.cloned.1.call-start = ((), (), s32[]{:S(2)}) async-start(), calls=%async_computation.16 | async-start | bytes 4718592 | tf_op jit(solution)/shard_map/reduce_scatter | solution.py:1083
  510.2 125.6 %reduce-scatter.10.cloned.1.call-start = ((), (), s32[]{:S(2)}) async-start(), calls=%async_computation.11 | async-start | bytes 9437184 | tf_op jit(solution)/shard_map/reduce_scatter | solution.py:958
  522.5 41.0 %copy-start.18 = (f32[256,64]{1,0:T(8,128)S(1)}, f32[256,64]{1,0:T(8,128)}, u32[]{:S(2)}) copy-start(f32[256,64]{1,0:T(8,128)} %copy-done.17) | copy-start | bytes 196612
  522.5 143.4 %reduce-scatter.20.cloned.1.call-start = ((), (), s32[]{:S(2)}) async-start(), calls=%async_computation.17 | async-start | bytes 1310720 | tf_op jit(solution)/shard_map/reduce_scatter | solution.py:1105
  564.4 6.3 copy-start.23
  570.7 250.6 %reduce-scatter.24.cloned.1.call-start = ((), (), s32[]{:S(2)}) async-start(), calls=%async_computation.20 | async-start | bytes 2359296 | tf_op jit(solution)/shard_map/reduce_scatter | solution.py:1128
  570.8 66.5 %copy-start.10 = (bf16[64,2048]{1,0:T(8,128)(2,1)S(1)}, bf16[64,2048]{1,0:T(8,128)(2,1)}, u32[]{:S(2)}) copy-start(bf16[64,2048]{1,0:T(8,128)(2,1)} %get-tuple-element.22) | copy-start | bytes 786436
  570.8 66.5 %copy-start.47 = (bf16[64]{0:T(256)(128)(2,1)S(1)}, bf16[64]{0:T(256)(128)(2,1)}, u32[]{:S(2)}) copy-start(bf16[64]{0:T(256)(128)(2,1)} %copy-done.46) | copy-start | bytes 388
  570.8 66.6 %copy-start.32 = (bf16[2048]{0:T(1024)(128)(2,1)S(1)}, bf16[2048]{0:T(1024)(128)(2,1)}, u32[]{:S(2)}) copy-start(bf16[2048]{0:T(1024)(128)(2,1)} %get-tuple-element.92) | copy-start | bytes 12292
  572.9 93.1 %copy-start.28 = (f32[1,8,256]{2,0,1:T(1,128)S(1)}, f32[1,8,256]{2,0,1:T(1,128)}, u32[]{:S(2)}) copy-start(f32[1,8,256]{2,0,1:T(1,128)} %get-tuple-element.116) | copy-start | bytes 24580
  572.9 95.2 %copy-start.27 = (f32[1,8,256]{2,0,1:T(1,128)S(1)}, f32[1,8,256]{2,0,1:T(1,128)}, u32[]{:S(2)}) copy-start(f32[1,8,256]{2,0,1:T(1,128)} %copy-done.26) | copy-start | bytes 24580
  572.9 95.2 %copy-start.41 = (f32[64]{0:T(128)S(1)}, f32[64]{0:T(128)}, u32[]{:S(2)}) copy-start(f32[64]{0:T(128)} %copy-done.40) | copy-start | bytes 772
  572.9 95.2 %copy-start.45 = (f32[64]{0:T(128)S(1)}, f32[64]{0:T(128)}, u32[]{:S(2)}) copy-start(f32[64]{0:T(128)} %copy-done.44) | copy-start | bytes 772
  572.9 250.2 %reduce-scatter.26.cloned.1.call-start = ((), (), s32[]{:S(2)}) async-start(), calls=%async_computation.21 | async-start | bytes 73728 | tf_op jit(solution)/shard_map/reduce_scatter | solution.py:1120
  668.0 167.0 %all-gather.8.cloned.1.call-start = ((), (), s32[]{:S(2)}) async-start(), calls=%async_computation.18 | async-start | bytes 1310720 | tf_op jit(solution)/shard_map/all_gather | solution.py:1113
  670.4 188.7 %reduce-scatter.22.cloned.1.call-start = ((), (), s32[]{:S(2)}) async-start(), calls=%async_computation.19 | async-start | bytes 7077888 | tf_op jit(solution)/shard_map/reduce_scatter | solution.py:1125
  670.4 12.8 %copy-start.6 = (bf16[256,2048]{1,0:T(8,128)(2,1)S(1)}, bf16[256,2048]{1,0:T(8,128)(2,1)}, u32[]{:S(2)}) copy-start(bf16[256,2048]{1,0:T(8,128)(2,1)} %tokens_ref.1) | copy-start | bytes 3145732
  670.4 13.1 %copy-start.21 = (bf16[1,256,512]{2,1,0:T(8,128)(2,1)S(1)}, bf16[1,256,512]{2,1,0:T(8,128)(2,1)}, u32[]{:S(2)}) copy-start(bf16[1,256,512]{2,1,0:T(8,128)(2,1)} %get-tuple-element.113) | copy-start | bytes 786436
  698.0 11.4 %slice-start.5 = ((s8[4325376]{0:T(1024)(128)(4,1)}), s8[4194304]{0:T(1024)(128)(4,1)S(1)}, s32[]{:S(2)}) async-start(s8[4325376]{0:T(1024)(128)(4,1)} %bitcast.205), calls=%async_computation.27 | async-start | bytes 8388608
  699.6 9.7 %slice-start.6 = ((s8[4325376]{0:T(1024)(128)(4,1)}), s8[131072]{0:T(1024)(128)(4,1)S(1)}, s32[]{:S(2)}) async-start(s8[4325376]{0:T(1024)(128)(4,1)} %bitcast.205), calls=%async_computation.28 | async-start | bytes 262144
  722.3 78.7 %all-to-all-start = ((bf16[8,3,528,256]{3,2,1,0:T(8,128)(2,1)}), bf16[8,3,528,256]{3,2,1,0:T(8,128)(2,1)}, u32[]{:S(2)}, u32[]{:S(2)}) async-start(bf16[8,3,528,256]{3,2,1,0:T(8,128)(2,1)} %copy.181), calls=%async_computation.9 | async-start | bytes 12976128 | tf_op jit(solution)/shard_map/all_to_all | solution.py:1000
  727.1 161.9 %reduce-scatter.12.cloned.1.call-start = ((), (), s32[]{:S(2)}) async-start(), calls=%async_computation.12 | async-start | bytes 1310720 | tf_op jit(solution)/shard_map/reduce_scatter | solution.py:964
  805.9 8.4 copy-start
  (27 other events, 86.6 us)
Sparse Core Ops, SparseCore 0:
  200.2 79.2 all-gather.3
  347.5 72.3 reduce-scatter.13
  422.3 28.1 reduce-scatter.15
  454.8 26.5 all-gather.5
  510.3 50.8 reduce-scatter.17
  564.5 71.2 reduce-scatter.9
  638.8 27.1 reduce-scatter.19
  669.8 39.8 reduce-scatter.23
  713.0 54.1 reduce-scatter.25
  769.2 25.1 all-gather.7
  797.8 61.2 reduce-scatter.21
  861.9 27.0 reduce-scatter.11

commit v3 on v2

--- a/solution.py
+++ b/solution.py
@@ -1,3 +1,4 @@
+import functools
 import math
 
 import jax
@@ -515,7 +516,7 @@
             )
 
         p = links.peer
-        self.keep = links.inside(source, place(fs))
+        self.keep = None if source is None else links.inside(source, place(fs))
         self.to_x = to(X_BIT, place(fs), place(p(X_BIT)), source)
         self.to_y = to(Y_BIT, place(fs), place(p(Y_BIT)), source)
         self.to_c = to(CORE_BIT, place(fs), place(p(CORE_BIT)), source)
@@ -532,7 +533,8 @@
         self.to_x[0].start()
         self.to_y[0].start()
         self.to_c[0].start()
-        self.keep.start()
+        if self.keep is not None:
+            self.keep.start()
 
     def second(self):
         self.to_x[1].wait_recv()
@@ -549,7 +551,8 @@
         self.d_core[1][0].start()
 
     def last(self):
-        self.keep.wait()
+        if self.keep is not None:
+            self.keep.wait()
         for out, back in (self.to_c, self.x_core, self.y_core, *self.d_core):
             back.wait_recv()
         for out, back in (
@@ -772,6 +775,11 @@
     gate_value = 1.0 / (1.0 + jnp.exp(-logits))
     scales = jnp.where(lane == 2 + E, gate_value, probs * chosen)
     scales_ref[...] = jnp.concatenate([scales, probs, chosen], axis=1)
+    high = scales.astype(jnp.bfloat16)
+    low = (scales - high.astype(jnp.float32)).astype(jnp.bfloat16)
+    two_ref[:, width:] = jnp.concatenate(
+        [high, low, jnp.zeros((quarter, SIDE - 2 * SMALL), jnp.bfloat16)], axis=1
+    )
     cot.third()
     cot.last()
     for out, back in slab_copies:
@@ -793,7 +801,7 @@
     vmem = pl.BlockSpec(memory_space=pltpu.VMEM)
     hbm = pl.BlockSpec(memory_space=pl.ANY)
     outs = [
-        (sds((quarter, width), bf), vmem),
+        (sds((quarter, width + SIDE), bf), vmem),
         (sds((quarter, width), f32), vmem),
         (sds((quarter, 3 * SMALL), f32), vmem),
         (sds((rows, local_width), bf), vmem),
@@ -828,6 +836,399 @@
             collective_id=1, has_side_effects=True, vmem_limit_bytes=56 * 2**20
         ),
     )(tokens, cotangent, qkv_weight, out_weight, small, slabs, cosine, sine, start, routes)
+
+
+def flip_by(index, bits):
+    total = 0
+    for bit in (1, 2, 4):
+        a, b = (index // bit) % 2, (bits // bit) % 2
+        total = total + bit * (a + b - 2 * a * b)
+    return total
+
+
+def expert_kernel(
+    routed,
+    two_ref,
+    router_ref,
+    residual_ref,
+    cotangent_ref,
+    cotangent_all,
+    slabs_ref,
+    small_ref,
+    output_ref,
+    branch_ref,
+    back_ref,
+    small_grad_ref,
+    grads_out,
+    two_all,
+    cot_all,
+    weights,
+    units,
+    first,
+    parts,
+    core_in,
+    diag_in,
+    side_in,
+    rows_in,
+    cols_in,
+    staged,
+    send,
+    recv,
+    local,
+    credit,
+):
+    links = Links(send, recv, local)
+    fs, tp = links.fs, links.tp
+    quarter = two_ref.shape[0]
+    rows = quarter * QUARTERS
+    width = residual_ref.shape[1]
+    block = width // E
+    count = weights.shape[0] // 3
+    out_width = output_ref.shape[1]
+    back_width = width + SIDE
+    whole = back_width + width
+
+    def at_rows(index, size):
+        return pl.ds(pl.multiple_of(index * size, size), size)
+
+    links.greet(range(1, 8), range(1, QUARTERS))
+    along = []
+    for step in range(1, QUARTERS):
+        here = two_all.at[fs, at_rows(tp, quarter)]
+        landing = two_all.at[fs, at_rows(links.along(QUARTERS - step), quarter)]
+        along.append(links.remote(two_ref, here, (fs, links.along(step)), landing))
+    gathers = []
+    for step in range(QUARTERS):
+        q = links.along(QUARTERS - step) if step else tp
+        gathers.append(
+            Gather(
+                links,
+                two_ref if step == 0 else None,
+                lambda f, q=q: two_all.at[f, at_rows(q, quarter)],
+                lambda f, h, q=q: two_all.at[f, at_rows(q * 2 + h, quarter // 2)],
+            )
+        )
+    gathers[0].first()
+    for out, back in along:
+        out.start()
+    loads = [
+        links.inside(slabs_ref.at[g], weights.at[:, pl.ds(g * block, block)]) for g in range(E)
+    ]
+    loads.append(links.inside(cotangent_all, cot_all))
+    for load in loads:
+        load.start()
+    for step in range(1, QUARTERS):
+        along[step - 1][1].wait_recv()
+        gathers[step].first()
+        gathers[step - 1].second()
+        if step >= 2:
+            gathers[step - 2].third()
+    gathers[3].second()
+    gathers[2].third()
+    gathers[3].third()
+    for load in loads:
+        load.wait()
+    for gather in gathers:
+        gather.last()
+
+    core_copies = []
+    for i in range(4):
+        core_copies.append(
+            links.remote(
+                parts.at[i % 2], core_in.at[i % 2], (links.peer(CORE_BIT), tp), core_in.at[i % 2]
+            )
+        )
+    half_rows = rows // 2
+    diag_y = links.remote(
+        parts.at[2, pl.ds(0, half_rows)], diag_in.at[0], (links.peer(Y_BIT), tp), diag_in.at[0]
+    )
+    diag_x = links.remote(
+        parts.at[2, pl.ds(half_rows, half_rows)],
+        diag_in.at[1],
+        (links.peer(X_BIT), tp),
+        diag_in.at[1],
+    )
+    side_x = links.remote(parts.at[3], side_in.at[0], (links.peer(X_BIT), tp), side_in.at[0])
+    side_y = links.remote(parts.at[4], side_in.at[1], (links.peer(Y_BIT), tp), side_in.at[1])
+
+    sub = lax.broadcasted_iota(jnp.int32, (8, SIDE), 0)
+    lane = lax.broadcasted_iota(jnp.int32, (8, SIDE), 1)
+    mine, common = 2 + fs, 2 + E
+    pick_in = (
+        ((sub == 0) & ((lane == mine) | (lane == mine + SMALL)))
+        | ((sub == 1) & ((lane == common) | (lane == common + SMALL)))
+    ).astype(jnp.bfloat16)
+    pick_out = (((sub == 0) & (lane == mine)) | ((sub == 1) & (lane == common))).astype(
+        jnp.bfloat16
+    )
+
+    def one_block(index, slot):
+        first[: 2 * count] = matmul_nt(weights[: 2 * count], two_all[index, :, :width])
+        first[2 * count :] = matmul_nt(weights[2 * count :], cot_all[index])
+        scale = matmul_nt(pick_in, two_all[index, :, width:])
+        cols = pl.ds(pl.multiple_of(index * rows, rows), rows)
+        dots = []
+        for group, (low, high) in enumerate(((0, routed), (routed, count))):
+            gate = first[low:high]
+            up = first[count + low : count + high]
+            grad = first[2 * count + low : 2 * count + high]
+            by = scale[group : group + 1]
+            sigmoid = 1.0 / (1.0 + jnp.exp(-gate))
+            silu = gate * sigmoid
+            active = silu * up
+            units[2 * count + low : 2 * count + high, cols] = (by * active).astype(jnp.bfloat16)
+            dots.append(jnp.sum(active * grad, axis=0, keepdims=True))
+            active_grad = by * grad
+            units[low:high, cols] = (
+                active_grad * up * sigmoid * (1.0 + gate * (1.0 - sigmoid))
+            ).astype(jnp.bfloat16)
+            units[count + low : count + high, cols] = (active_grad * silu).astype(jnp.bfloat16)
+        both = jnp.concatenate([*dots, jnp.zeros((6, rows), jnp.float32)], axis=0)
+        parts[slot, :, width:back_width] = matmul_tn(both.astype(jnp.bfloat16), pick_out).astype(
+            jnp.bfloat16
+        )
+        tile = 512
+        for n in range(width // tile):
+            at = slice(n * tile, (n + 1) * tile)
+            parts[slot, :, at] = matmul_tn(units[: 2 * count, cols], weights[: 2 * count, at]).astype(
+                jnp.bfloat16
+            )
+            beyond = slice(back_width + n * tile, back_width + (n + 1) * tile)
+            parts[slot, :, beyond] = matmul_tn(
+                units[2 * count :, cols], weights[2 * count :, at]
+            ).astype(jnp.bfloat16)
+
+    chunk = 32
+
+    def add_in(slot, others):
+        @pl.loop(0, rows // chunk)
+        def _(r):
+            at = pl.ds(pl.multiple_of(r * chunk, chunk), chunk)
+            total = parts[slot, at, :].astype(jnp.float32)
+            for ref in others:
+                total = total + ref[at, :].astype(jnp.float32)
+            parts[slot, at, :] = total.astype(jnp.bfloat16)
+
+    def add_half(slot, ref, start):
+        @pl.loop(0, half_rows // chunk)
+        def _(r):
+            at = pl.ds(pl.multiple_of(start + r * chunk, chunk), chunk)
+            there = pl.ds(pl.multiple_of(r * chunk, chunk), chunk)
+            total = parts[slot, at, :].astype(jnp.float32) + ref[there, :].astype(jnp.float32)
+            parts[slot, at, :] = total.astype(jnp.bfloat16)
+
+    def free_core():
+        pl.semaphore_signal(
+            credit, inc=1, device_id=(links.peer(CORE_BIT), tp), device_id_type=MESH
+        )
+
+    @pl.loop(0, 8)
+    def _(t):
+        pair = t // 2
+        second = t % 2
+        bits = 7 - 4 * pair + 6 * (pair // 2) - second
+        index = flip_by(fs, bits)
+        slot = second * (2 + pair - 3 * (pair // 3)) + (1 - second) * (pair % 2)
+
+        @pl.when(t == 4)
+        def _():
+            core_copies[0][0].wait_send()
+
+        @pl.when(t == 6)
+        def _():
+            core_copies[1][0].wait_send()
+
+        @pl.when(t == 7)
+        def _():
+            diag_y[0].wait_send()
+            diag_x[0].wait_send()
+
+        one_block(index, slot)
+        for i in range(4):
+
+            @pl.when(t == 2 * i)
+            def _(i=i):
+                if i >= 2:
+                    pl.semaphore_wait(credit, 1)
+                core_copies[i][0].start()
+
+        @pl.when(t == 1)
+        def _():
+            core_copies[0][1].wait_recv()
+            add_in(2, [core_in.at[0]])
+            free_core()
+            diag_y[0].start()
+            diag_x[0].start()
+
+        @pl.when(t == 3)
+        def _():
+            core_copies[1][1].wait_recv()
+            add_in(3, [core_in.at[1]])
+            free_core()
+            diag_y[1].wait_recv()
+            add_half(3, diag_in.at[0], 0)
+            side_x[0].start()
+
+        @pl.when(t == 5)
+        def _():
+            core_copies[2][1].wait_recv()
+            add_in(4, [core_in.at[0]])
+            diag_x[1].wait_recv()
+            add_half(4, diag_in.at[1], half_rows)
+            side_y[0].start()
+
+        @pl.when(t == 7)
+        def _():
+            core_copies[3][1].wait_recv()
+            add_in(2, [core_in.at[1]])
+
+    keeps = []
+
+    def weight_grads(g):
+        at = pl.ds(g * block, block)
+        if g >= 2:
+            keeps[g - 2].wait()
+        hidden_cols = two_all[:, :, at].reshape(E * rows, block)
+        staged[g % 2, : 2 * count] = matmul(units[: 2 * count], hidden_cols).astype(jnp.bfloat16)
+        cot_cols = cot_all[:, :, at].reshape(E * rows, block)
+        staged[g % 2, 2 * count :] = matmul(units[2 * count :], cot_cols).astype(jnp.bfloat16)
+        keep = links.inside(staged.at[g % 2], grads_out.at[g])
+        keep.start()
+        keeps.append(keep)
+
+    for g in range(E // 2):
+        weight_grads(g)
+    side_x[1].wait_recv()
+    side_y[1].wait_recv()
+    add_in(2, [side_in.at[0], side_in.at[1]])
+    own = at_rows(tp, quarter)
+    parts[2, own, back_width:] = (
+        parts[2, own, back_width:].astype(jnp.float32) + residual_ref[...]
+    ).astype(jnp.bfloat16)
+    column = []
+    for step in range(1, QUARTERS):
+        peer = links.along(step)
+        column.append(
+            links.remote(
+                parts.at[2, at_rows(peer, quarter), pl.ds(0, back_width)],
+                rows_in.at[step - 1],
+                (fs, peer),
+                rows_in.at[step - 1],
+            )
+        )
+    for step in range(1, QUARTERS):
+        peer = links.along(step)
+        column.append(
+            links.remote(
+                parts.at[2, :, pl.ds(pl.multiple_of(back_width + peer * out_width, 128), out_width)],
+                cols_in.at[step - 1],
+                (fs, peer),
+                cols_in.at[step - 1],
+            )
+        )
+    for out, back in column:
+        out.start()
+    for g in range(E // 2, E):
+        weight_grads(g)
+    for out, back in column[:3]:
+        back.wait_recv()
+    total = parts[2, own, :back_width].astype(jnp.float32)
+    for step in range(1, QUARTERS):
+        total = total + rows_in[step - 1].astype(jnp.float32)
+    dots = total[:, width : width + SMALL]
+    scales = router_ref[:, :SMALL]
+    probs = router_ref[:, SMALL : 2 * SMALL]
+    chosen = router_ref[:, 2 * SMALL :]
+    chosen_grad = chosen * dots
+    logit_grad = probs * (chosen_grad - jnp.sum(probs * chosen_grad, axis=1, keepdims=True))
+    gate_lane = lax.broadcasted_iota(jnp.int32, (quarter, SMALL), 1) == 2 + E
+    logit_grad = jnp.where(gate_lane, dots * scales * (1.0 - scales), logit_grad).astype(
+        jnp.bfloat16
+    )
+    residual = residual_ref[...]
+    rstd = lax.rsqrt(jnp.mean(residual * residual, axis=1, keepdims=True) + NORM_EPS)
+    mean = jnp.zeros((quarter, 1), jnp.float32)
+    for b in range(E):
+        at = slice(b * block, (b + 1) * block)
+        two_grad = total[:, at] + matmul(logit_grad, small_ref[b])
+        normed = residual[:, at] * rstd
+        gain = small_ref[b, 1:2, :].astype(jnp.float32)
+        back_ref[:, at] = two_grad
+        mean = mean + jnp.sum(two_grad * gain * normed, axis=1, keepdims=True)
+        grads = matmul_tn(logit_grad, two_all[fs, own, at])
+        sub = lax.broadcasted_iota(jnp.int32, (SMALL, block), 0)
+        gain_grad = jnp.sum(two_grad * normed, axis=0, keepdims=True)
+        small_grad_ref[:, at] = jnp.where(sub == 1, gain_grad, grads)
+    mean = mean / width
+    for b in range(E):
+        at = slice(b * block, (b + 1) * block)
+        gain = small_ref[b, 1:2, :].astype(jnp.float32)
+        normed = residual[:, at] * rstd
+        grad = cotangent_ref[own, at].astype(jnp.float32) + rstd * (
+            back_ref[:, at] * gain - normed * mean
+        )
+        back_ref[:, at] = grad
+        branch_ref[:, at] = grad.astype(jnp.bfloat16)
+    for out, back in column[3:]:
+        back.wait_recv()
+    start = pl.multiple_of(back_width + tp * out_width, 128)
+    total = parts[2, :, pl.ds(start, out_width)].astype(jnp.float32)
+    for step in range(1, QUARTERS):
+        total = total + cols_in[step - 1].astype(jnp.float32)
+    output_ref[...] = total.astype(jnp.bfloat16)
+    for out, back in along + core_copies[2:] + [side_x, side_y] + column:
+        out.wait_send()
+    for keep in keeps[-2:]:
+        keep.wait()
+
+
+def expert_call(
+    two_rows, router_rows, residual_rows, cotangent, cotangent_all, slabs, small_full, out_width, routed
+):
+    quarter, width = residual_rows.shape
+    rows = quarter * QUARTERS
+    back_width = width + SIDE
+    block = width // E
+    bf, f32 = jnp.bfloat16, jnp.float32
+    sds = jax.ShapeDtypeStruct
+    vmem = pl.BlockSpec(memory_space=pltpu.VMEM)
+    hbm = pl.BlockSpec(memory_space=pl.ANY)
+    outs = [
+        (sds((rows, out_width), bf), vmem),
+        (sds((quarter, width), bf), vmem),
+        (sds((quarter, width), f32), vmem),
+        (sds((SMALL, width), f32), vmem),
+        (sds(slabs.shape, bf), hbm),
+    ]
+    units = slabs.shape[1]
+    return pl.pallas_call(
+        functools.partial(expert_kernel, routed),
+        name="experts",
+        out_shape=[o[0] for o in outs],
+        in_specs=[vmem, vmem, vmem, vmem, hbm, hbm, vmem],
+        out_specs=[o[1] for o in outs],
+        scratch_shapes=[
+            pltpu.VMEM((E, rows, back_width), bf),
+            pltpu.VMEM((E, rows, width), bf),
+            pltpu.VMEM((units, width), bf),
+            pltpu.VMEM((units, E * rows), bf),
+            pltpu.VMEM((units, rows), f32),
+            pltpu.VMEM((5, rows, back_width + width), bf),
+            pltpu.VMEM((2, rows, back_width + width), bf),
+            pltpu.VMEM((2, rows // 2, back_width + width), bf),
+            pltpu.VMEM((2, rows, back_width + width), bf),
+            pltpu.VMEM((QUARTERS - 1, quarter, back_width), bf),
+            pltpu.VMEM((QUARTERS - 1, rows, out_width), bf),
+            pltpu.VMEM((2, units, block), bf),
+            pltpu.SemaphoreType.DMA((64,)),
+            pltpu.SemaphoreType.DMA((64,)),
+            pltpu.SemaphoreType.DMA((24,)),
+            pltpu.SemaphoreType.REGULAR,
+        ],
+        compiler_params=pltpu.CompilerParams(
+            collective_id=2, has_side_effects=True, vmem_limit_bytes=62 * 2**20
+        ),
+    )(two_rows, router_rows, residual_rows, cotangent, cotangent_all, slabs, small_full)
 
 
 def shards_units(
@@ -905,133 +1306,27 @@
         doc_start[:, None],
         routes,
     )
-    cotangent_all = cotangent_all.reshape(-1, width)
-    slabs = slabs.reshape(fs_size, 3, units, block)
+    output, branch_rows, residual_grad, small_grad, grad_slabs = expert_call(
+        two_rows,
+        router_rows,
+        residual_rows,
+        cotangent,
+        cotangent_all,
+        slabs,
+        small_full,
+        width // QUARTERS,
+        routed_units,
+    )
+    grad_slabs = lax.all_to_all(
+        grad_slabs.reshape(fs_size, 3, units, block), "fs", 0, 0, tiled=True
+    )
     small_rows = jnp.transpose(small_full, (1, 0, 2)).reshape(SMALL, width)
-    scale_rows = router_rows[:, 2 : 3 + E]
-    probs_rows = router_rows[:, SMALL + 2 : SMALL + 2 + E]
-    chosen_rows = router_rows[:, 2 * SMALL + 2 : 2 * SMALL + 2 + E]
-    scales_high = scale_rows.astype(jnp.bfloat16)
-    scales_low = (scale_rows - scales_high.astype(jnp.float32)).astype(jnp.bfloat16)
-    sent = jnp.concatenate(
-        [
-            two_rows,
-            scales_high,
-            scales_low,
-            jnp.zeros((quarter, SIDE - 2 * (E + 1)), jnp.bfloat16),
-        ],
-        axis=1,
-    )
-    hidden_all = lax.all_gather(sent, ("fs", "tp"), axis=0, tiled=True)
-    side_all = hidden_all[:, width : width + 2 * (E + 1)].astype(jnp.float32)
-    scales_all = side_all[:, : E + 1] + side_all[:, E + 1 :]
-    two_all = hidden_all[:, :width]
-    mine = (jnp.arange(E, dtype=jnp.int32) == fs_index).astype(jnp.float32)
-    routed_scale = jnp.sum(scales_all[:, :E] * mine[None, :], axis=1, keepdims=True)
-    is_routed = jnp.arange(units, dtype=jnp.int32)[None, :] < routed_units
-    scale = jnp.where(is_routed, routed_scale, scales_all[:, E:])
-    weights_by_unit = jnp.transpose(slabs, (1, 2, 0, 3)).reshape(3, units, width)
-    gate_part = jnp.einsum(
-        "td,ud->tu", two_all, weights_by_unit[0], preferred_element_type=jnp.float32
-    )
-    up_part = jnp.einsum(
-        "td,ud->tu", two_all, weights_by_unit[1], preferred_element_type=jnp.float32
-    )
-    hidden_grad = jnp.einsum(
-        "td,ud->tu", cotangent_all, weights_by_unit[2], preferred_element_type=jnp.float32
-    )
-    gate_sigmoid = jax.nn.sigmoid(gate_part)
-    silu = gate_part * gate_sigmoid
-    active = silu * up_part
-    hidden = (scale * active).astype(jnp.bfloat16)
-    dots = active * hidden_grad
-    routed_dot = jnp.sum(jnp.where(is_routed, dots, 0.0), axis=1, keepdims=True)
-    shared_dot = jnp.sum(jnp.where(is_routed, 0.0, dots), axis=1, keepdims=True)
-    active_grad = scale * hidden_grad
-    gate_grad = (
-        active_grad * up_part * gate_sigmoid * (1.0 + gate_part * (1.0 - gate_sigmoid))
-    ).astype(jnp.bfloat16)
-    up_grad = (active_grad * silu).astype(jnp.bfloat16)
-    mixture_part = jnp.einsum(
-        "tu,ud->td", hidden, weights_by_unit[2], preferred_element_type=jnp.float32
-    )
-    mixture_own = lax.psum_scatter(
-        mixture_part.astype(jnp.bfloat16), "fs", scatter_dimension=0, tiled=True
-    )
-    residual_placed = lax.dynamic_update_slice(
-        jnp.zeros((tok_rows, width), jnp.float32), residual_rows, (tp_index * quarter, 0)
-    )
-    output = lax.psum_scatter(
-        (mixture_own.astype(jnp.float32) + residual_placed).astype(jnp.bfloat16),
-        "tp",
-        scatter_dimension=1,
-        tiled=True,
-    )
-    input_part = jnp.einsum(
-        "tu,ud->td", gate_grad, weights_by_unit[0], preferred_element_type=jnp.float32
-    ) + jnp.einsum(
-        "tu,ud->td", up_grad, weights_by_unit[1], preferred_element_type=jnp.float32
-    )
-    side_part = jnp.concatenate(
-        [
-            routed_dot * mine[None, :],
-            shared_dot,
-            jnp.zeros((input_part.shape[0], SIDE - E - 1), jnp.float32),
-        ],
-        axis=1,
-    )
-    back_part = jnp.concatenate([input_part, side_part], axis=1).astype(jnp.bfloat16)
-    back_own = lax.psum_scatter(back_part, "fs", scatter_dimension=0, tiled=True)
-    back_rows = lax.psum_scatter(back_own, "tp", scatter_dimension=0, tiled=True).astype(
-        jnp.float32
-    )
-    input_sum = back_rows[:, :width]
-    gate_sum = back_rows[:, width : width + E]
-    shared_sum = back_rows[:, width + E]
-    grad_by_unit = jnp.stack(
-        [
-            jnp.einsum("tu,td->ud", gate_grad, two_all, preferred_element_type=jnp.float32),
-            jnp.einsum("tu,td->ud", up_grad, two_all, preferred_element_type=jnp.float32),
-            jnp.einsum("tu,td->ud", hidden, cotangent_all, preferred_element_type=jnp.float32),
-        ],
-        axis=0,
-    ).astype(jnp.bfloat16)
-    grad_slabs = jnp.transpose(grad_by_unit.reshape(3, units, fs_size, block), (2, 0, 1, 3))
-    grad_slabs = lax.all_to_all(grad_slabs, "fs", 0, 0, tiled=True)
     token_rows = lax.dynamic_slice_in_dim(tokens, tp_index * quarter, quarter, 0).astype(
         jnp.float32
     )
-    cotangent_rows = lax.dynamic_slice_in_dim(cotangent, tp_index * quarter, quarter, 0).astype(
-        jnp.float32
-    )
     rstd_one = lax.rsqrt(jnp.mean(token_rows * token_rows, axis=1, keepdims=True) + NORM_EPS)
     normed_one = token_rows * rstd_one
-    rstd_two = lax.rsqrt(jnp.mean(residual_rows * residual_rows, axis=1, keepdims=True) + NORM_EPS)
-    normed_two = residual_rows * rstd_two
-    gate_value = scale_rows[:, E]
-    chosen_grad = chosen_rows * gate_sum
-    logit_grad = (
-        probs_rows * (chosen_grad - jnp.sum(probs_rows * chosen_grad, axis=1, keepdims=True))
-    ).astype(jnp.bfloat16)
-    gate_logit_grad = (shared_sum * gate_value * (1.0 - gate_value)).astype(jnp.bfloat16)
-    router_grad = jnp.einsum("te,td->ed", logit_grad, two_rows, preferred_element_type=jnp.float32)
-    shared_vector_grad = jnp.einsum(
-        "t,td->d", gate_logit_grad, two_rows, preferred_element_type=jnp.float32
-    )
-    two_grad = (
-        input_sum
-        + jnp.einsum(
-            "te,ed->td", logit_grad, small_rows[2 : 2 + E], preferred_element_type=jnp.float32
-        )
-        + gate_logit_grad.astype(jnp.float32)[:, None]
-        * small_rows[2 + E].astype(jnp.float32)[None, :]
-    )
-    scaled_two = two_grad * small_rows[1].astype(jnp.float32)[None, :]
-    gain_two_grad = jnp.sum(two_grad * normed_two, axis=0)
-    residual_grad = cotangent_rows + rstd_two * (
-        scaled_two - normed_two * jnp.mean(scaled_two * normed_two, axis=1, keepdims=True)
-    )
-    branch_grad = lax.all_gather(residual_grad.astype(jnp.bfloat16), "tp", axis=0, tiled=True)
+    branch_grad = lax.all_gather(branch_rows, "tp", axis=0, tiled=True)
     out_grad = jnp.einsum("tf,td->fd", attended, branch_grad, preferred_element_type=jnp.float32)
     attended_grad = jnp.einsum(
         "tbd,bfd->tf",
@@ -1113,9 +1408,7 @@
     input_grad = lax.all_gather(
         input_grad_rows.astype(jnp.bfloat16), "tp", axis=0, tiled=True
     ).astype(jnp.float32)
-    small_grad = jnp.concatenate(
-        [gain_one_grad[None], gain_two_grad[None], router_grad, shared_vector_grad[None]], axis=0
-    )
+    small_grad = jnp.concatenate([gain_one_grad[None], small_grad[1 : 3 + E]], axis=0)
     small_own = lax.psum(
         lax.psum_scatter(
             small_grad.astype(jnp.bfloat16), "fs", scatter_dimension=1, tiled=True

time: 905 us -> 742 us (0.82)
  waiting for transfers between devices: 427 us -> 231 us
  Pallas kernels: 175 us -> 365 us
  matrix products: 118 us -> 26 us
  local copies, waits for them, and re-layouts: 104 us -> 52.3 us
  other arithmetic: 42 us -> 29.3 us
    pallas_call x0 -> x1, Pallas kernels: none -> 191 us  [expert_call(): pl.pallas_call(functools.partial(expert_kernel, routed), name='experts',...]
    reduce_scatter x4 -> x0, waiting for transfers between devices: 182 us -> none  [the longest x1 72.5 us: shards_units(): lax.psum_scatter(back_part, 'fs', scatter_dimension=0, tiled=True)]
    dot_general x12 -> x0, matrix products: 89.5 us -> none  [the longest x1 12.9 us: shards_units(): jnp.einsum('tu,ud->td', up_grad, weights_by_unit[1], preferred_element_ty...]
    all_gather x2 -> x1, waiting for transfers between devices: 86 us -> 14.2 us  [shards_units(): branch_grad = lax.all_gather(branch_rows, 'tp', axis=0, tiled=True)]
    reduce_scatter x1, waiting for transfers between devices: 0.01 us -> 51.3 us  [shards_units(): lax.psum_scatter(out_grad.astype(jnp.bfloat16), 'fs', scatter_dimension=1...]
    all_to_all x1, waiting for transfers between devices: 72.7 us -> 29.3 us  [shards_units(): lax.all_to_all(grad_slabs.reshape(fs_size, 3, units, block), 'fs', 0, 0,...]
    reduce_scatter x1, waiting for transfers between devices: 21.2 us -> 61.9 us  [shards_units(): lax.psum_scatter(qkv_grad.astype(jnp.bfloat16), 'fs', scatter_dimension=1...]
    concatenate x2 -> x0, local copies, waits for them, and re-layouts: 15.6 us -> none  [the longest x1 13.8 us: shards_units(): jnp.concatenate([input_part, side_part], axis=1).astype(jnp.bfloat16)]
  transfers between devices with their start and end apart: 13 -> 8, of which waited for: 10 -> 7; matrix products, arithmetic and copies ran while one was open for 16% -> 7% of each run, Pallas kernels for 0% -> 0%
where the time goes in v3:
time: 742 us; the launch traced here: 734 us
  Pallas kernels  365 us (49%)
  waiting for transfers between devices  231 us (31%)
  local copies, waits for them, and re-layouts  52.3 us (7%)
  other arithmetic  29.3 us (4%)
  matrix products  26 us (4%)
  between operations  15.1 us (2%)
  blocking collectives  10.1 us (1%)
    pallas_call x1, Pallas kernels, expert_call(): pl.pallas_call(functools.partial(expert_kernel, routed), name='experts',...  191 us
    pallas_call x1, Pallas kernels, forward_call(): pl.pallas_call(forward_kernel, name='attention_forward', out_shape=[o[0]...  175 us
    reduce_scatter x1, waiting for transfers between devices, shards_units(): lax.psum_scatter(qkv_grad.astype(jnp.bfloat16), 'fs', scatter_dimension=1...  61.9 us
    reduce_scatter x1, waiting for transfers between devices, shards_units(): lax.psum_scatter(out_grad.astype(jnp.bfloat16), 'fs', scatter_dimension=1...  51.3 us
    reduce_scatter x1, waiting for transfers between devices, shards_units(): lax.psum_scatter(terms, 'fs', scatter_dimension=0, tiled=True)  48.1 us
    all_to_all x1, waiting for transfers between devices, shards_units(): lax.all_to_all(grad_slabs.reshape(fs_size, 3, units, block), 'fs', 0, 0,...  29.3 us
    reduce_scatter x1, waiting for transfers between devices, shards_units(): lax.psum_scatter(one_part.astype(jnp.bfloat16), 'tp', scatter_dimension=0...  24.1 us
    unnamed x48, local copies, waits for them, and re-layouts  22.6 us
  transfers between devices with their start and end apart: 8, of which 7 were waited for; matrix products, arithmetic and copies ran while one was open for 7% of the time, Pallas kernels for 0%

profile of v3, /device:TPU:0, one launch (start us, length us, event | category | flops | bytes accessed | tf_op | source)
XLA Modules:
  0.0 734.1 jit_solution(6013187722001969442)
XLA Ops:
  8.6 3.7 copy.71
  12.3 1.5 copy.74.start_ref
  13.8 1.5 copy.75.routes_ref
  15.2 0.8 broadcast_in_dim.23
  16.8 1.2 maximum_bitcast_fusion
  18.2 4.1 pad_maximum_fusion
  22.9 174.8 %attention_forward.1 = (bf16[64,2176]{1,0:T(8,128)(2,1)}, f32[64,2048]{1,0:T(8,128)}, f32[64,48]{1,0:T(8,128)}, bf16[256,512]{1,0:T(8,128)(2,1)}, bf16[256,512]{...) custom-call(bf16[256,2048]{1,0:T(8,128)(2,1)} %tokens_ref.1, ...), custom_call_target="tpu_custom_call" | custom-call | tf_op jit(solution)/shard_map/attention_forward/pallas_call | solution.py:816
  197.8 190.6 %experts.1 = (bf16[256,512]{1,0:T(8,128)(2,1)}, bf16[64,2048]{1,0:T(8,128)(2,1)}, f32[64,2048]{1,0:T(8,128)}, f32[16,2048]{1,0:T(8,128)}, bf16[8,1584,256]{2,1,0:T(8,128)(2,1)}) custom-call(bf16[64,2176]{1,0:T(8,128)(2,1)} %get-tuple-element.27.two_ref, f32[64,48]{1,0:T(8,128)} %get-tuple-element.28.router_ref, f32[64,2048]{1,0:T(8,128)} %get-tuple-element.29.residual_ref, ...), custom_call_target="tpu_custom_call" | custom-call | tf_op jit(solution)/shard_map/experts/pallas_call | solution.py:1204
  388.5 7.9 %reshape.192 = bf16[8,2,128,2,4,128]{5,4,3,2,1,0:T(4,128)(2,1)} reshape(bf16[8,256,1024]{2,1,0:T(8,128)(2,1)} %get-tuple-element.35) | data formatting | bytes 8388608 | tf_op jit(solution)/shard_map/reshape | solution.py:1339
  397.2 4.4 fusion.39
  401.6 0.9 fusion
  402.4 2.0 copy-done.1
  404.4 0.9 fusion.2
  405.4 14.2 %all-gather.3.cloned.1.call-done = bf16[256,2048]{1,0:T(8,128)(2,1)} async-done(((bf16[64,2048]{1,0:T(8,128)(2,1)}), bf16[256,2048]{1,0:T(8,128)(2,1)}) %all-gather.3.cloned.1.call-update) | async-done | bytes 1048592 | tf_op jit(solution)/shard_map/all_gather | solution.py:1329
  419.6 2.7 fusion.18
  422.5 5.4 convert_bitcast_fusion.1
  427.9 1.6 multiply_reduce_fusion
  429.5 1.4 multiply_convert_fusion.1
  431.6 1.8 copy.87
  433.4 1.7 copy.153
  435.1 4.2 copy.90
  439.3 2.1 copy.152
  441.6 2.7 pad_maximum_fusion.1
  444.6 2.5 fusion.17
  447.1 48.1 %reduce-scatter.6.cloned.1.call-done = bf16[256,1024]{1,0:T(8,128)(2,1)} async-done(((bf16[2048,1024]{1,0:T(8,128)(2,1)}), bf16[256,1024]{1,0:T(8,128)(2,1)}) %reduce-scatter.6.cloned.1.call-update) | async-done | bytes 524304 | tf_op jit(solution)/shard_map/reduce_scatter | solution.py:1378
  495.2 1.1 slice_convert_fusion
  498.2 5.7 fusion.3
  504.1 2.1 convolution_convert_fusion
  506.4 0.8 slice_convert_fusion.2
  507.2 24.1 %reduce-scatter.8.cloned.1.call-done = bf16[64,2048]{1,0:T(8,128)(2,1)} async-done(((bf16[256,2048]{1,0:T(8,128)(2,1)}), bf16[64,2048]{1,0:T(8,128)(2,1)}) %reduce-scatter.8.cloned.1.call-update) | async-done | bytes 262160 | tf_op jit(solution)/shard_map/reduce_scatter | solution.py:1400
  531.3 1.3 fusion.33
  533.3 1.8 fusion.30
  535.5 4.6 convert_bitcast_fusion
  540.1 4.8 all-to-all-start
  545.0 51.3 %reduce-scatter.12.cloned.1.call-done = bf16[512,256]{1,0:T(8,128)(2,1)} async-done(((bf16[512,2048]{1,0:T(8,128)(2,1)}), bf16[512,256]{1,0:T(8,128)(2,1)}) %reduce-scatter.12.cloned.1.call-update) | async-done | bytes 262160 | tf_op jit(solution)/shard_map/reduce_scatter | solution.py:1421
  596.2 1.8 convert_element_type.95
  598.0 29.3 %all-to-all-done = bf16[8,3,528,256]{3,2,1,0:T(8,128)(2,1)} async-done(((bf16[8,3,528,256]{3,2,1,0:T(8,128)(2,1)}), bf16[8,3,528,256]{3,2,1,0:T(8,128)(2,1)}, u32[]{:S(2)}, u32[]{:S(2)}) %all-to-all-start) | async-done | bytes 6488096 | tf_op jit(solution)/shard_map/all_to_all | solution.py:1320
  627.3 4.3 copy_convert_fusion
  631.9 1.4 slice.89
  633.7 3.7 copy.97
  637.4 1.1 copy-done
  638.5 3.4 copy.98
  641.9 3.6 slice_bitcast_fusion.1
  645.5 10.1 %psum.7 = bf16[11,256]{1,0:T(8,128)(2,1)S(1)} all-reduce(bf16[11,256]{1,0:T(8,128)(2,1)} %reduce-scatter.14.cloned.1.call-done), channel_id=1, replica_groups=mesh['fs'=8,'tp'=4] {'tp'}, use_global_device_ids=true, to_apply=%region_12.13 | all-reduce | flops 2816 | bytes 11264 | tf_op jit(solution)/shard_map/psum | solution.py:1412
  657.3 1.6 all-gather.5.cloned.1.call-done
  658.9 2.8 convert_element_type.88
  661.7 61.9 %reduce-scatter.10.cloned.1.call-done = bf16[3,256,512]{1,2,0:T(8,128)(2,1)} async-done(((bf16[3,2048,512]{1,2,0:T(8,128)(2,1)}), bf16[3,256,512]{1,2,0:T(8,128)(2,1)}) %reduce-scatter.10.cloned.1.call-update) | async-done | bytes 786448 | tf_op jit(solution)/shard_map/reduce_scatter | solution.py:1418
  723.6 2.6 copy.96
  (95 shorter events, 11.5 us)
Async XLA Ops:
  7.2 9.6 %copy-start.8 = (bf16[8,352,256]{2,1,0:T(8,128)(2,1)S(1)}, bf16[8,352,256]{2,1,0:T(8,128)(2,1)}, u32[]{:S(2)}) copy-start(bf16[8,352,256]{2,1,0:T(8,128)(2,1)} %param.21) | copy-start | bytes 4325380
  7.2 412.4 %all-gather.3.cloned.1.call-start = ((), (), s32[]{:S(2)}) async-start(), calls=%async_computation.6 | async-start | bytes 1310720 | tf_op jit(solution)/shard_map/all_gather | solution.py:1329
  15.2 2.9 copy-start.6
  18.2 4.1 copy-start.18
  18.2 4.1 copy-start.19
  388.4 106.9 %reduce-scatter.6.cloned.1.call-start = ((), (), s32[]{:S(2)}) async-start(), calls=%async_computation.7 | async-start | bytes 4718592 | tf_op jit(solution)/shard_map/reduce_scatter | solution.py:1378
  388.4 7.9 %copy-start.15 = (bf16[256,512]{1,0:T(8,128)(2,1)S(1)}, bf16[256,512]{1,0:T(8,128)(2,1)}, u32[]{:S(2)}) copy-start(bf16[256,512]{1,0:T(8,128)(2,1)} %get-tuple-element.36) | copy-start | bytes 786436
  388.4 8.5 %copy-start.17 = (s32[256]{0:T(256)S(1)}, s32[256]{0:T(256)}, u32[]{:S(2)}) copy-start(s32[256]{0:T(256)} %param.25) | copy-start | bytes 3076
  402.4 2.0 copy-start.1
  422.5 5.4 copy-start.2
  422.5 5.4 copy-start.7
  430.9 2.5 copy-start.3
  439.3 2.2 copy-start.4
  444.3 87.0 %reduce-scatter.8.cloned.1.call-start = ((), (), s32[]{:S(2)}) async-start(), calls=%async_computation.8 | async-start | bytes 1310720 | tf_op jit(solution)/shard_map/reduce_scatter | solution.py:1400
  498.2 5.7 copy-start.13
  498.2 5.8 copy-start.9
  498.2 5.8 copy-start.10
  503.9 2.2 copy-start.16
  503.9 2.3 copy-start.5
  504.0 29.3 %copy-start.11 = (f32[64,2048]{1,0:T(8,128)S(1)}, f32[64,2048]{1,0:T(8,128)}, u32[]{:S(2)}) copy-start(f32[64,2048]{1,0:T(8,128)} %get-tuple-element.34) | copy-start | bytes 1572868
  504.0 92.3 %reduce-scatter.12.cloned.1.call-start = ((), (), s32[]{:S(2)}) async-start(), calls=%async_computation.11 | async-start | bytes 2359296 | tf_op jit(solution)/shard_map/reduce_scatter | solution.py:1421
  506.1 29.4 %copy-start.14 = (bf16[1,256,512]{2,1,0:T(8,128)(2,1)S(1)}, bf16[1,256,512]{2,1,0:T(8,128)(2,1)}, u32[]{:S(2)}) copy-start(bf16[1,256,512]{2,1,0:T(8,128)(2,1)} %copy-done.13) | copy-start | bytes 786436
  506.1 139.4 %reduce-scatter.14.cloned.1.call-start = ((), (), s32[]{:S(2)}) async-start(), calls=%async_computation.12 | async-start | bytes 73728 | tf_op jit(solution)/shard_map/reduce_scatter | solution.py:1413
  533.2 125.7 %all-gather.5.cloned.1.call-start = ((), (), s32[]{:S(2)}) async-start(), calls=%async_computation.9 | async-start | bytes 1310720 | tf_op jit(solution)/shard_map/all_gather | solution.py:1408
  535.2 188.4 %reduce-scatter.10.cloned.1.call-start = ((), (), s32[]{:S(2)}) async-start(), calls=%async_computation.10 | async-start | bytes 7077888 | tf_op jit(solution)/shard_map/reduce_scatter | solution.py:1418
  540.1 87.2 %all-to-all-start = ((bf16[8,3,528,256]{3,2,1,0:T(8,128)(2,1)}), bf16[8,3,528,256]{3,2,1,0:T(8,128)(2,1)}, u32[]{:S(2)}, u32[]{:S(2)}) async-start(bf16[8,3,528,256]{3,2,1,0:T(8,128)(2,1)} %bitcast.106), calls=%async_computation.5 | async-start | bytes 12976128 | tf_op jit(solution)/shard_map/all_to_all | solution.py:1320
  631.6 6.8 copy-start
  645.5 80.7 %copy-start.12 = (bf16[256,512]{1,0:T(8,128)(2,1)S(1)}, bf16[256,512]{1,0:T(8,128)(2,1)}, u32[]{:S(2)}) copy-start(bf16[256,512]{1,0:T(8,128)(2,1)} %get-tuple-element.110) | copy-start | bytes 786436
Sparse Core Ops, SparseCore 0:
  388.5 31.0 all-gather.2
  444.4 50.8 reduce-scatter.5
  504.1 27.1 reduce-scatter.7
  535.0 61.2 reduce-scatter.11
  599.9 28.4 reduce-scatter.13
  630.4 28.4 all-gather.4
  662.3 61.2 reduce-scatter.9

commit v4 on v3

--- a/solution.py
+++ b/solution.py
@@ -604,6 +604,7 @@
     scales_ref,
     attended_ref,
     query_ref,
+    hidden_buf,
     slabs_all,
     cotangent_all,
     kv_out,
@@ -615,7 +616,6 @@
     small_full,
     kv_own,
     kv_full,
-    hidden_buf,
     branch_buf,
     branch_in,
     send,
@@ -806,6 +806,7 @@
         (sds((quarter, 3 * SMALL), f32), vmem),
         (sds((rows, local_width), bf), vmem),
         (sds((rows, local_width), bf), vmem),
+        (sds((rows, width), bf), vmem),
         (sds(slabs.shape, bf), hbm),
         (sds((E, rows, width), bf), hbm),
         (sds((E, rows, 2 * local_width), bf), hbm),
@@ -825,7 +826,6 @@
             pltpu.VMEM((E, SMALL, block), bf),
             pltpu.VMEM((rows, 2 * local_width), bf),
             pltpu.VMEM((E, rows, 2 * local_width), bf),
-            pltpu.VMEM((rows, width), bf),
             pltpu.VMEM((rows, width), bf),
             pltpu.VMEM((QUARTERS - 1, quarter, width), bf),
             pltpu.SemaphoreType.DMA((64,)),
@@ -1231,6 +1231,429 @@
     )(two_rows, router_rows, residual_rows, cotangent, cotangent_all, slabs, small_full)
 
 
+class Scatter:
+    def __init__(self, links, parts, core_in, diag_in, side_in):
+        self.links, self.parts = links, parts
+        self.core_in, self.diag_in, self.side_in = core_in, diag_in, side_in
+        self.rows = parts.shape[1]
+        p, tp = links.peer, links.tp
+        half = self.rows // 2
+        self.core = [
+            links.remote(
+                parts.at[p(bits + CORE_BIT)], core_in.at[i], (p(CORE_BIT), tp), core_in.at[i]
+            )
+            for i, bits in enumerate((6, 2, 4, 0))
+        ]
+        self.diag = [
+            links.remote(
+                parts.at[p(6), pl.ds(h * half, half)], diag_in.at[h], (p(bits), tp), diag_in.at[h]
+            )
+            for h, bits in enumerate((Y_BIT, X_BIT))
+        ]
+        self.side = [
+            links.remote(parts.at[p(bits)], side_in.at[i], (p(bits), tp), side_in.at[i])
+            for i, bits in enumerate((X_BIT, Y_BIT))
+        ]
+
+    def add(self, index, first, count, refs, target=None):
+        chunk = 32
+
+        @pl.loop(0, count // chunk)
+        def _(r):
+            here = pl.ds(pl.multiple_of(first + r * chunk, chunk), chunk)
+            there = pl.ds(pl.multiple_of(r * chunk, chunk), chunk)
+            total = self.parts[index, here, :].astype(jnp.float32)
+            for ref in refs:
+                total = total + ref[there, :].astype(jnp.float32)
+            if target is None:
+                self.parts[index, here, :] = total.astype(jnp.bfloat16)
+            else:
+                target[here, :] = total
+
+    def to_core(self):
+        for out, back in self.core:
+            out.start()
+
+    def diagonal(self):
+        self.core[0][1].wait_recv()
+        self.add(self.links.peer(6), 0, self.rows, [self.core_in.at[0]])
+        for out, back in self.diag:
+            out.start()
+
+    def sideways(self, i):
+        index = self.links.peer((X_BIT, Y_BIT)[i])
+        self.core[1 + i][1].wait_recv()
+        self.add(index, 0, self.rows, [self.core_in.at[1 + i]])
+        self.diag[i][1].wait_recv()
+        self.add(index, i * (self.rows // 2), self.rows // 2, [self.diag_in.at[i]])
+        self.side[i][0].start()
+
+    def finish(self, target):
+        self.core[3][1].wait_recv()
+        for out, back in self.side:
+            back.wait_recv()
+        self.add(
+            self.links.fs,
+            0,
+            self.rows,
+            [self.core_in.at[3], self.side_in.at[0], self.side_in.at[1]],
+            target,
+        )
+
+    def sent(self):
+        for out, back in self.core + self.diag + self.side:
+            out.wait_send()
+
+
+def backward_kernel(
+    branch_ref,
+    residual_ref,
+    small_grad_ref,
+    attended_ref,
+    query_ref,
+    hidden_ref,
+    tokens_ref,
+    kv_ref,
+    qkv_ref,
+    out_ref,
+    small_ref,
+    cos_ref,
+    sin_ref,
+    start_ref,
+    slabs_ref,
+    input_grad_ref,
+    qkv_own,
+    out_own,
+    small_own,
+    slabs_all,
+    kv_full,
+    qkv_full,
+    out_full,
+    branch_all,
+    odds,
+    query_grad,
+    projected,
+    kv_total,
+    kv_parts,
+    kv_core,
+    kv_diag,
+    kv_side,
+    qkv_parts,
+    qkv_core,
+    qkv_diag,
+    qkv_side,
+    out_parts,
+    out_core,
+    out_diag,
+    out_side,
+    one_parts,
+    one_in,
+    grad_rows,
+    small_parts,
+    small_in,
+    small_column,
+    send,
+    recv,
+    local,
+):
+    links = Links(send, recv, local)
+    fs, tp = links.fs, links.tp
+    quarter, width = residual_ref.shape
+    rows = quarter * QUARTERS
+    block = width // E
+    local_width = query_ref.shape[1]
+    heads = local_width // HD
+    seqs = rows // SEQ_DEV
+    length = E * SEQ_DEV
+    scale = HD ** (-0.5)
+
+    def at_rows(index, size):
+        return pl.ds(pl.multiple_of(index * size, size), size)
+
+    own = at_rows(tp, quarter)
+    links.greet(range(1, 8), range(1, QUARTERS))
+    branch = []
+    for step in range(1, QUARTERS):
+        here = branch_all.at[own]
+        landing = branch_all.at[at_rows(links.along(QUARTERS - step), quarter)]
+        branch.append(links.remote(branch_ref, here, (fs, links.along(step)), landing))
+    for out, back in branch:
+        out.start()
+    branch_all[own, :] = branch_ref[...]
+    slab_copies = []
+    for bits in (6, 7, 2, 3, 4, 5, 1):
+        peer = links.peer(bits)
+        slab_copies.append(
+            links.remote(slabs_ref.at[peer], slabs_all.at[fs], (peer, tp), slabs_all.at[peer])
+        )
+    for out, back in slab_copies:
+        out.start()
+    slab_own = links.inside(slabs_ref.at[fs], slabs_all.at[fs])
+    slab_own.start()
+    kv_load = links.inside(kv_ref, kv_full)
+    kv_load.start()
+    out_load = links.inside(out_ref, out_full)
+    out_load.start()
+    qkv_load = links.inside(qkv_ref, qkv_full)
+    qkv_load.start()
+    kv_sum = Scatter(links, kv_parts, kv_core, kv_diag, kv_side)
+    qkv_sum = Scatter(links, qkv_parts, qkv_core, qkv_diag, qkv_side)
+    out_sum = Scatter(links, out_parts, out_core, out_diag, out_side)
+
+    kv_load.wait()
+    key_pos = lax.broadcasted_iota(jnp.int32, (SEQ_DEV, length), 1)
+    query_pos = fs * SEQ_DEV + lax.broadcasted_iota(jnp.int32, (SEQ_DEV, length), 0)
+    for s in range(seqs):
+        here = slice(s * SEQ_DEV, (s + 1) * SEQ_DEV)
+        allowed = (key_pos <= query_pos) & (key_pos >= start_ref[here, :])
+        for h in range(heads):
+            cols = slice(h * HD, (h + 1) * HD)
+            keys = kv_full[:, here, cols].reshape(length, HD)
+            scores = matmul_nt(query_ref[here, cols], keys) * scale
+            scores = jnp.where(allowed, scores, NEG_FILL)
+            top = jnp.max(scores, axis=1, keepdims=True)
+            weights = jnp.exp(scores - top)
+            odds[s * heads + h] = weights / jnp.sum(weights, axis=1, keepdims=True)
+    out_load.wait()
+    for out, back in branch:
+        back.wait_recv()
+    attended_grad = jnp.zeros((rows, local_width), jnp.float32)
+    for b in range(E):
+        attended_grad = attended_grad + matmul_nt(
+            branch_all[:, b * block : (b + 1) * block], out_full[b]
+        )
+    query_grad[...] = attended_grad.astype(jnp.bfloat16)
+    for s in range(seqs):
+        here = slice(s * SEQ_DEV, (s + 1) * SEQ_DEV)
+        for h in range(heads):
+            cols = slice(h * HD, (h + 1) * HD)
+            vcols = slice(local_width + h * HD, local_width + (h + 1) * HD)
+            keys = kv_full[:, here, cols].reshape(length, HD)
+            values = kv_full[:, here, vcols].reshape(length, HD)
+            grad = query_grad[here, cols]
+            probs = odds[s * heads + h]
+            weights_grad = matmul_nt(grad, values)
+            delta = jnp.sum(probs * weights_grad, axis=1, keepdims=True)
+            score_grad = (probs * (weights_grad - delta)).astype(jnp.bfloat16)
+            key_grad = matmul_tn(score_grad, query_ref[here, cols]) * scale
+            value_grad = matmul_tn(probs.astype(jnp.bfloat16), grad)
+            kv_parts[:, here, cols] = key_grad.astype(jnp.bfloat16).reshape(E, SEQ_DEV, HD)
+            kv_parts[:, here, vcols] = value_grad.astype(jnp.bfloat16).reshape(E, SEQ_DEV, HD)
+            projected[0, here, cols] = turn(
+                matmul(score_grad, keys) * scale, cos_ref[here, :], -sin_ref[here, :]
+            ).astype(jnp.bfloat16)
+    kv_sum.to_core()
+    attended = attended_ref[...]
+    for b in range(E):
+        cols = slice(b * block, (b + 1) * block)
+        out_parts[b] = matmul_tn(attended, branch_all[:, cols]).astype(jnp.bfloat16)
+    kv_sum.diagonal()
+    out_sum.to_core()
+
+    def weight_grad(j):
+        for b in range(E):
+            cols = slice(b * block, (b + 1) * block)
+            qkv_parts[b, j * block : (j + 1) * block] = matmul_tn(
+                hidden_ref[:, cols], projected[j]
+            ).astype(jnp.bfloat16)
+
+    weight_grad(0)
+    kv_sum.sideways(0)
+    kv_sum.sideways(1)
+    out_sum.diagonal()
+    qkv_load.wait()
+    kv_sum.finish(kv_total)
+    projected[1] = turn(kv_total[:, :local_width], cos_ref[...], -sin_ref[...]).astype(jnp.bfloat16)
+    projected[2] = kv_total[:, local_width:].astype(jnp.bfloat16)
+    for b in range(E):
+        cols = slice(b * block, (b + 1) * block)
+        part = jnp.zeros((rows, block), jnp.float32)
+        for j in range(3):
+            part = part + matmul_nt(projected[j], qkv_full[j, cols])
+        one_parts[:, cols] = part.astype(jnp.bfloat16)
+    column = []
+    for step in range(1, QUARTERS):
+        peer = links.along(step)
+        column.append(
+            links.remote(
+                one_parts.at[at_rows(peer, quarter)],
+                one_in.at[step - 1],
+                (fs, peer),
+                one_in.at[step - 1],
+            )
+        )
+    for out, back in column:
+        out.start()
+    weight_grad(1)
+    weight_grad(2)
+    qkv_sum.to_core()
+    out_sum.sideways(0)
+    out_sum.sideways(1)
+    qkv_sum.diagonal()
+    qkv_sum.sideways(0)
+    qkv_sum.sideways(1)
+    for out, back in column:
+        back.wait_recv()
+    tokens = tokens_ref[own, :].astype(jnp.float32)
+    rstd = lax.rsqrt(jnp.mean(tokens * tokens, axis=1, keepdims=True) + NORM_EPS)
+    total = one_parts[own, :].astype(jnp.float32)
+    for step in range(1, QUARTERS):
+        total = total + one_in[step - 1].astype(jnp.float32)
+    mean = jnp.zeros((quarter, 1), jnp.float32)
+    sub = lax.broadcasted_iota(jnp.int32, (SMALL, block), 0)
+    for b in range(E):
+        at = slice(b * block, (b + 1) * block)
+        gain = small_ref[b, 0:1, :].astype(jnp.float32)
+        normed = tokens[:, at] * rstd
+        mean = mean + jnp.sum(total[:, at] * gain * normed, axis=1, keepdims=True)
+        gain_grad = jnp.sum(total[:, at] * normed, axis=0, keepdims=True)
+        small_parts[b] = jnp.where(sub == 0, gain_grad, small_grad_ref[:, at])
+    mean = mean / width
+    for b in range(E):
+        at = slice(b * block, (b + 1) * block)
+        gain = small_ref[b, 0:1, :].astype(jnp.float32)
+        normed = tokens[:, at] * rstd
+        grad_rows[:, at] = (
+            residual_ref[:, at] + rstd * (total[:, at] * gain - normed * mean)
+        ).astype(jnp.bfloat16)
+    spread = []
+    for step in range(1, QUARTERS):
+        peer = links.along(step)
+        landing = input_grad_ref.at[at_rows(links.along(QUARTERS - step), quarter)]
+        spread.append(links.remote(grad_rows, input_grad_ref.at[own], (fs, peer), landing))
+    for out, back in spread:
+        out.start()
+    keep = links.inside(grad_rows, input_grad_ref.at[own])
+    keep.start()
+    small_copies = []
+    for bits in range(1, E):
+        peer = links.peer(bits)
+        small_copies.append(
+            links.remote(
+                small_parts.at[peer], small_in.at[bits - 1], (peer, tp), small_in.at[bits - 1]
+            )
+        )
+    for out, back in small_copies:
+        out.start()
+    out_sum.finish(out_own)
+    for out, back in small_copies:
+        back.wait_recv()
+    small_total = small_parts[fs]
+    for bits in range(1, E):
+        small_total = small_total + small_in[bits - 1]
+    small_column[tp] = small_total
+    small_spread = []
+    for step in range(1, QUARTERS):
+        here = small_column.at[tp]
+        landing = small_column.at[links.along(QUARTERS - step)]
+        small_spread.append(links.remote(here, here, (fs, links.along(step)), landing))
+    for out, back in small_spread:
+        out.start()
+    qkv_sum.finish(qkv_own)
+    for out, back in small_spread:
+        back.wait_recv()
+    small_own[...] = small_column[0] + small_column[1] + small_column[2] + small_column[3]
+    for out, back in spread + slab_copies:
+        back.wait_recv()
+    slab_own.wait()
+    keep.wait()
+    for out, back in branch + slab_copies + column + spread + small_copies + small_spread:
+        out.wait_send()
+    for scatter in (kv_sum, out_sum, qkv_sum):
+        scatter.sent()
+
+
+def backward_call(
+    branch_rows,
+    residual_grad,
+    small_grad,
+    attended,
+    query_rows,
+    hidden_one,
+    tokens,
+    kv_all,
+    qkv_full,
+    out_full,
+    small_full,
+    cosine,
+    sine,
+    start,
+    slabs,
+):
+    quarter, width = residual_grad.shape
+    rows = quarter * QUARTERS
+    block = width // E
+    local_width = query_rows.shape[1]
+    bf, f32 = jnp.bfloat16, jnp.float32
+    sds = jax.ShapeDtypeStruct
+    vmem = pl.BlockSpec(memory_space=pltpu.VMEM)
+    hbm = pl.BlockSpec(memory_space=pl.ANY)
+    outs = [
+        (sds((rows, width), bf), hbm),
+        (sds((3 * block, local_width), f32), vmem),
+        (sds((local_width, block), f32), vmem),
+        (sds((SMALL, block), f32), vmem),
+        (sds(slabs.shape, bf), hbm),
+    ]
+
+    def scatter_scratch(count, columns):
+        return [
+            pltpu.VMEM((E, count, columns), bf),
+            pltpu.VMEM((4, count, columns), bf),
+            pltpu.VMEM((2, count // 2, columns), bf),
+            pltpu.VMEM((2, count, columns), bf),
+        ]
+
+    return pl.pallas_call(
+        backward_kernel,
+        name="attention_backward",
+        out_shape=[o[0] for o in outs],
+        in_specs=[vmem] * 7 + [hbm] * 3 + [vmem] * 4 + [hbm],
+        out_specs=[o[1] for o in outs],
+        scratch_shapes=[
+            pltpu.VMEM((E, rows, 2 * local_width), bf),
+            pltpu.VMEM((3, width, local_width), bf),
+            pltpu.VMEM((E, local_width, block), bf),
+            pltpu.VMEM((rows, width), bf),
+            pltpu.VMEM((rows // SEQ_DEV * local_width // HD, SEQ_DEV, E * SEQ_DEV), f32),
+            pltpu.VMEM((rows, local_width), bf),
+            pltpu.VMEM((3, rows, local_width), bf),
+            pltpu.VMEM((rows, 2 * local_width), f32),
+            *scatter_scratch(rows, 2 * local_width),
+            *scatter_scratch(3 * block, local_width),
+            *scatter_scratch(local_width, block),
+            pltpu.VMEM((rows, width), bf),
+            pltpu.VMEM((QUARTERS - 1, quarter, width), bf),
+            pltpu.VMEM((quarter, width), bf),
+            pltpu.VMEM((E, SMALL, block), f32),
+            pltpu.VMEM((E - 1, SMALL, block), f32),
+            pltpu.VMEM((QUARTERS, SMALL, block), f32),
+            pltpu.SemaphoreType.DMA((64,)),
+            pltpu.SemaphoreType.DMA((64,)),
+            pltpu.SemaphoreType.DMA((16,)),
+        ],
+        compiler_params=pltpu.CompilerParams(
+            collective_id=3, has_side_effects=True, vmem_limit_bytes=62 * 2**20
+        ),
+    )(
+        branch_rows,
+        residual_grad,
+        small_grad,
+        attended,
+        query_rows,
+        hidden_one,
+        tokens,
+        kv_all,
+        qkv_full,
+        out_full,
+        small_full,
+        cosine,
+        sine,
+        start,
+        slabs,
+    )
+
+
 def shards_units(
     tokens,
     cotangent,
@@ -1249,9 +1672,7 @@
     tok_rows, width = tokens.shape
     seq_count = tok_rows // SEQ_DEV
     local_width = qkv_weight.shape[2]
-    head_count = local_width // HD
     quarter = tok_rows // QUARTERS
-    score_scale = HD ** (-0.5)
     fs_index = lax.axis_index("fs")
     tp_index = lax.axis_index("tp")
     fs_size = E
@@ -1288,6 +1709,7 @@
         router_rows,
         attended,
         query_rows,
+        hidden_one,
         slabs,
         cotangent_all,
         kv_all,
@@ -1317,110 +1739,25 @@
         width // QUARTERS,
         routed_units,
     )
-    grad_slabs = lax.all_to_all(
-        grad_slabs.reshape(fs_size, 3, units, block), "fs", 0, 0, tiled=True
-    )
-    small_rows = jnp.transpose(small_full, (1, 0, 2)).reshape(SMALL, width)
-    token_rows = lax.dynamic_slice_in_dim(tokens, tp_index * quarter, quarter, 0).astype(
-        jnp.float32
-    )
-    rstd_one = lax.rsqrt(jnp.mean(token_rows * token_rows, axis=1, keepdims=True) + NORM_EPS)
-    normed_one = token_rows * rstd_one
-    branch_grad = lax.all_gather(branch_rows, "tp", axis=0, tiled=True)
-    out_grad = jnp.einsum("tf,td->fd", attended, branch_grad, preferred_element_type=jnp.float32)
-    attended_grad = jnp.einsum(
-        "tbd,bfd->tf",
-        branch_grad.reshape(tok_rows, fs_size, block),
+    input_grad, qkv_own, out_own, small_own, grad_slabs = backward_call(
+        branch_rows,
+        residual_grad,
+        small_grad,
+        attended,
+        query_rows,
+        hidden_one,
+        tokens,
+        kv_all,
+        qkv_full,
         out_full,
-        preferred_element_type=jnp.float32,
-    ).astype(jnp.bfloat16)
-    grad_heads = attended_grad.reshape(seq_count, SEQ_DEV, head_count, HD)
-    query_heads = query_rows.reshape(seq_count, SEQ_DEV, head_count, HD)
-    kv_heads = kv_all.reshape(fs_size, seq_count, SEQ_DEV, 2, head_count, HD)
-    key_heads, value_heads = kv_heads[:, :, :, 0], kv_heads[:, :, :, 1]
-    query_start = doc_start.reshape(seq_count, SEQ_DEV)
-    allowed = key_mask(query_pos, query_start, 0, fs_size)[:, None]
-    scores = (
-        jnp.einsum("pqhd,gpkhd->phqgk", query_heads, key_heads, preferred_element_type=jnp.float32)
-        * score_scale
-    )
-    scores = jnp.where(allowed, scores, NEG_FILL)
-    exps = jnp.exp(scores - jnp.max(scores, axis=(3, 4), keepdims=True))
-    probs = exps / jnp.sum(exps, axis=(3, 4), keepdims=True)
-    weights_grad = jnp.einsum(
-        "pqhd,gpkhd->phqgk", grad_heads, value_heads, preferred_element_type=jnp.float32
-    )
-    delta = jnp.sum(probs * weights_grad, axis=(3, 4), keepdims=True)
-    score_grad = (probs * (weights_grad - delta)).astype(jnp.bfloat16)
-    query_grad = (
-        jnp.einsum("phqgk,gpkhd->pqhd", score_grad, key_heads, preferred_element_type=jnp.float32)
-        * score_scale
-    )
-    key_grad = (
-        jnp.einsum(
-            "phqgk,pqhd->gpkhd", score_grad, query_heads, preferred_element_type=jnp.float32
-        )
-        * score_scale
-    )
-    value_grad = jnp.einsum(
-        "phqgk,pqhd->gpkhd",
-        probs.astype(jnp.bfloat16),
-        grad_heads,
-        preferred_element_type=jnp.float32,
-    )
-    terms = jnp.concatenate(
-        [
-            key_grad.reshape(fs_size * tok_rows, local_width),
-            value_grad.reshape(fs_size * tok_rows, local_width),
-        ],
-        axis=1,
-    ).astype(jnp.bfloat16)
-    key_value_sum = lax.psum_scatter(terms, "fs", scatter_dimension=0, tiled=True).astype(
-        jnp.float32
-    )
-    projected_grad = jnp.stack(
-        [
-            rotate(query_grad.reshape(tok_rows, local_width), half_cos, -half_sin),
-            rotate(key_value_sum[:, :local_width], half_cos, -half_sin),
-            key_value_sum[:, local_width:],
-        ],
-        axis=0,
-    ).astype(jnp.bfloat16)
-    token_all = tokens.astype(jnp.float32)
-    rstd_all = lax.rsqrt(jnp.mean(token_all * token_all, axis=1, keepdims=True) + NORM_EPS)
-    hidden_one = (token_all * rstd_all * small_rows[0].astype(jnp.float32)[None, :]).astype(
-        jnp.bfloat16
-    )
-    qkv_grad = jnp.einsum(
-        "td,jtf->jdf", hidden_one, projected_grad, preferred_element_type=jnp.float32
-    )
-    one_part = jnp.einsum(
-        "jtf,jdf->td", projected_grad, qkv_full, preferred_element_type=jnp.float32
-    )
-    one_grad = lax.psum_scatter(
-        one_part.astype(jnp.bfloat16), "tp", scatter_dimension=0, tiled=True
-    ).astype(jnp.float32)
-    scaled_one = one_grad * small_rows[0].astype(jnp.float32)[None, :]
-    gain_one_grad = jnp.sum(one_grad * normed_one, axis=0)
-    input_grad_rows = residual_grad + rstd_one * (
-        scaled_one - normed_one * jnp.mean(scaled_one * normed_one, axis=1, keepdims=True)
-    )
-    input_grad = lax.all_gather(
-        input_grad_rows.astype(jnp.bfloat16), "tp", axis=0, tiled=True
-    ).astype(jnp.float32)
-    small_grad = jnp.concatenate([gain_one_grad[None], small_grad[1 : 3 + E]], axis=0)
-    small_own = lax.psum(
-        lax.psum_scatter(
-            small_grad.astype(jnp.bfloat16), "fs", scatter_dimension=1, tiled=True
-        ),
-        "tp",
-    ).astype(jnp.float32)
-    qkv_own = lax.psum_scatter(
-        qkv_grad.astype(jnp.bfloat16), "fs", scatter_dimension=1, tiled=True
-    ).astype(jnp.float32)
-    out_own = lax.psum_scatter(
-        out_grad.astype(jnp.bfloat16), "fs", scatter_dimension=1, tiled=True
-    ).astype(jnp.float32)
+        small_full,
+        cosine,
+        sine,
+        doc_start[:, None],
+        grad_slabs,
+    )
+    input_grad = input_grad.astype(jnp.float32)
+    grad_slabs = grad_slabs.reshape(fs_size, 3, units, block)
     own = grad_slabs.astype(jnp.float32)
     expert_up_own = jnp.transpose(own[:, :2, :routed_units], (0, 3, 1, 2))
     expert_down_own = own[:, 2, :routed_units]
@@ -1431,7 +1768,7 @@
     return (
         output,
         input_grad,
-        qkv_own,
+        qkv_own.reshape(qkv_weight.shape),
         out_own,
         small_own[:2],
         small_own[2 : 2 + E],

time: 742 us -> 569 us (0.77)
  waiting for transfers between devices: 231 us -> 0 us
  Pallas kernels: 365 us -> 518 us
  matrix products: 26 us -> 0 us
  local copies, waits for them, and re-layouts: 52.3 us -> 26.9 us
  other arithmetic: 29.3 us -> 15.4 us
  between operations: 15.1 us -> 1.21 us
  blocking collectives: 10.1 us -> 0 us
    reduce_scatter x5 -> x0, waiting for transfers between devices: 185 us -> none  [the longest x1 61.9 us: shards_units(): lax.psum_scatter(qkv_grad.astype(jnp.bfloat16), 'fs', scatter_dimension=1...]
    pallas_call x0 -> x1, Pallas kernels: none -> 153 us  [backward_call(): pl.pallas_call(backward_kernel, name='attention_backward', out_shape=[o[0...]
    all_to_all x1 -> x0, waiting for transfers between devices: 29.3 us -> none  [shards_units(): lax.all_to_all(grad_slabs.reshape(fs_size, 3, units, block), 'fs', 0, 0,...]
    dot_general x9 -> x0, matrix products: 26 us -> none  [the longest x1 5.7 us: shards_units(): jnp.einsum('jtf,jdf->td', projected_grad, qkv_full, preferred_element_typ...]
    all_gather x2 -> x0, waiting for transfers between devices: 15.8 us -> none  [the longest x1 14.2 us: shards_units(): branch_grad = lax.all_gather(branch_rows, 'tp', axis=0, tiled=True)]
    unnamed x48 -> x17, local copies, waits for them, and re-layouts: 22.6 us -> 12.1 us
    psum x1 -> x0, blocking collectives: 10.1 us -> none  [shards_units(): lax.psum(lax.psum_scatter(small_grad.astype(jnp.bfloat16), 'fs', scatter_...]
    reshape x6 -> x0, local copies, waits for them, and re-layouts: 8.61 us -> none  [the longest x1 7.92 us: shards_units(): kv_heads = kv_all.reshape(fs_size, seq_count, SEQ_DEV, 2, head_count, HD)]
  transfers between devices with their start and end apart: 8 -> 0, of which waited for: 7 -> 0; matrix products, arithmetic and copies ran while one was open for 7% -> 0% of each run, Pallas kernels for 0% -> 0%
where the time goes in v4:
time: 569 us; the launch traced here: 562 us
  Pallas kernels  518 us (91%)
  local copies, waits for them, and re-layouts  26.9 us (5%)
  other arithmetic  15.4 us (3%)
    pallas_call x1, Pallas kernels, expert_call(): pl.pallas_call(functools.partial(expert_kernel, routed), name='experts',...  190 us
    pallas_call x1, Pallas kernels, forward_call(): pl.pallas_call(forward_kernel, name='attention_forward', out_shape=[o[0]...  175 us
    pallas_call x1, Pallas kernels, backward_call(): pl.pallas_call(backward_kernel, name='attention_backward', out_shape=[o[0...  153 us
    unnamed x17, local copies, waits for them, and re-layouts  12.1 us

profile of v4, /device:TPU:0, one launch (start us, length us, event | category | flops | bytes accessed | tf_op | source)
XLA Modules:
  0.0 561.6 jit_solution(9998368847768834665)
XLA Ops:
  0.6 0.0 copy-start.2
  0.7 0.1 pad.12.clone
  0.8 0.7 broadcast_in_dim.15
  1.5 1.4 maximum_maximum_fusion.small_ref
  2.9 1.5 copy.32.start_ref
  4.4 1.5 copy.33.routes_ref
  5.8 0.5 fusion
  6.4 0.8 pad_maximum_fusion.1
  7.2 3.7 copy.29
  10.9 0.0 copy-start
  10.9 0.0 copy-done.2
  10.9 1.4 maximum_bitcast_fusion
  12.4 0.6 copy-done
  13.0 4.1 pad_maximum_fusion
  17.1 175.2 %attention_forward.1 = (bf16[64,2176]{1,0:T(8,128)(2,1)}, f32[64,2048]{1,0:T(8,128)}, f32[64,48]{1,0:T(8,128)}, bf16[256,512]{1,0:T(8,128)(2,1)}, bf16[256,512]{...) custom-call(bf16[256,2048]{1,0:T(8,128)(2,1)} %tokens_ref.3, ...), custom_call_target="tpu_custom_call" | custom-call | tf_op jit(solution)/shard_map/attention_forward/pallas_call | solution.py:817
  192.3 190.3 %experts.1 = (bf16[256,512]{1,0:T(8,128)(2,1)}, bf16[64,2048]{1,0:T(8,128)(2,1)}, f32[64,2048]{1,0:T(8,128)}, f32[16,2048]{1,0:T(8,128)}, bf16[8,1584,256]{2,1,0:T(8,128)(2,1)}) custom-call(bf16[64,2176]{1,0:T(8,128)(2,1)} %get-tuple-element.33.two_ref, f32[64,48]{1,0:T(8,128)} %get-tuple-element.34.router_ref, f32[64,2048]{1,0:T(8,128)} %get-tuple-element.35.residual_ref, ...), custom_call_target="tpu_custom_call" | custom-call | tf_op jit(solution)/shard_map/experts/pallas_call | solution.py:1204
  382.6 152.6 %attention_backward.1 = (bf16[256,2048]{1,0:T(8,128)(2,1)}, f32[768,512]{1,0:T(8,128)}, f32[512,256]{1,0:T(8,128)}, f32[16,256]{1,0:T(8,128)}, bf16[8,1584,256]{2,1,0:T(8,128)(2,1)}) custom-call(bf16[64,2048]{1,0:T(8,128)(2,1)} %get-tuple-element.40.branch_ref, f32[64,2048]{1,0:T(8,128)} %get-tuple-element.41.residual_ref, ...), custom_call_target="tpu_custom_call" | custom-call | tf_op jit(solution)/shard_map/attention_backward/pallas_call | solution.py:1607
  535.1 1.3 slice.23
  536.4 1.3 slice.21
  537.7 1.3 slice.22
  539.0 2.8 convert_element_type.22
  541.8 2.3 slice.31
  544.1 1.7 slice.30
  545.8 0.2 copy.39
  546.0 3.4 copy.37
  549.5 4.3 convert.1
  553.8 1.8 slice_bitcast_fusion.1
  555.6 0.0 copy-start.4
  555.6 0.0 copy-start.1
  555.6 2.9 slice_bitcast_fusion
  558.5 0.0 copy-done.4
  558.5 0.0 copy-start.3
  558.5 0.7 copy.45
  559.2 0.0 copy-done.1
  559.2 1.1 copy.46
  560.3 0.0 copy-done.3
  560.3 0.8 copy.47
  (4 shorter events, 0.0 us)
Async XLA Ops:
  0.6 10.3 %copy-start.2 = (bf16[8,352,256]{2,1,0:T(8,128)(2,1)S(1)}, bf16[8,352,256]{2,1,0:T(8,128)(2,1)}, u32[]{:S(2)}) copy-start(bf16[8,352,256]{2,1,0:T(8,128)(2,1)} %param.21) | copy-start | bytes 4325380
  10.9 2.0 copy-start
  555.6 2.9 copy-start.4
  555.6 3.6 copy-start.1
  558.5 1.9 copy-start.3

commit v5 on v4

--- a/solution.py
+++ b/solution.py
@@ -442,6 +442,7 @@
 X_BIT, Y_BIT, CORE_BIT = 2, 4, 1
 QUARTERS = 4
 SMALL = 16
+CUT = 1536
 
 
 def flip(index, bit):
@@ -568,6 +569,67 @@
             out.wait_send()
 
 
+class CrossGather:
+    def __init__(self, links, source, blocks):
+        self.links = links
+        tp = links.tp
+        size = source.shape[0]
+
+        def slot(k, h=None):
+            start, count = (3 - k // 2) * size, size
+            if h is not None:
+                count = size // 2
+                start = start + h * count
+            return blocks.at[1, pl.ds(start, count)]
+
+        def to(bits, start, there):
+            return links.remote(start, there, (links.peer(bits), tp), there)
+
+        x, y, c = X_BIT, Y_BIT, CORE_BIT
+        self.keep = links.inside(source, slot(0))
+        self.to_x = to(x, source, slot(x))
+        self.to_y = to(y, source, slot(y))
+        self.x_on = to(y, slot(x, 0), slot(x + y, 0))
+        self.y_on = to(x, slot(y, 1), slot(x + y, 1))
+        self.along = []
+        for step in range(1, QUARTERS):
+            there = blocks.at[2 * step + 1]
+            self.along.append(
+                links.remote(blocks.at[1], there, (links.fs, links.along(step)), there)
+            )
+        self.core = [
+            to(c, blocks.at[2 * s + 1], blocks.at[2 * s]) for s in range(QUARTERS)
+        ]
+
+    def first(self):
+        self.to_x[0].start()
+        self.to_y[0].start()
+        self.keep.start()
+
+    def second(self):
+        self.to_x[1].wait_recv()
+        self.x_on[0].start()
+        self.to_y[1].wait_recv()
+        self.y_on[0].start()
+
+    def third(self):
+        self.keep.wait()
+        self.x_on[1].wait_recv()
+        self.y_on[1].wait_recv()
+        for out, back in self.along:
+            out.start()
+        self.core[0][0].start()
+
+    def last(self):
+        for s, (out, back) in enumerate(self.along):
+            back.wait_recv()
+            self.core[s + 1][0].start()
+        for out, back in self.core:
+            back.wait_recv()
+        for out, back in (self.to_x, self.to_y, self.x_on, self.y_on, *self.along, *self.core):
+            out.wait_send()
+
+
 def turn(values, cosine, sine_signed):
     parts = []
     for h in range(values.shape[1] // HD):
@@ -576,6 +638,15 @@
     return jnp.concatenate(parts, axis=1)
 
 
+def as_column(row):
+    size = row.shape[1]
+    same = lax.broadcasted_iota(jnp.int32, (size, size), 0) == lax.broadcasted_iota(
+        jnp.int32, (size, size), 1
+    )
+    spread = jnp.where(same, row.astype(jnp.float32), 0.0)
+    return jnp.sum(spread, axis=1, keepdims=True).astype(jnp.int32)
+
+
 def matmul(a, b):
     return jnp.dot(a, b, preferred_element_type=jnp.float32)
 
@@ -593,13 +664,18 @@
     cotangent_ref,
     qkv_ref,
     out_ref,
-    small_ref,
-    slabs_ref,
+    gains_ref,
+    router_ref,
+    gate_ref,
+    up_ref,
+    shared_up_ref,
+    down_ref,
+    shared_down_ref,
     cos_ref,
     sin_ref,
     start_ref,
     routes_ref,
-    two_ref,
+    two_out,
     residual_ref,
     scales_ref,
     attended_ref,
@@ -607,6 +683,7 @@
     hidden_buf,
     slabs_all,
     cotangent_all,
+    cotangent_plane,
     kv_out,
     qkv_out,
     out_out,
@@ -618,6 +695,8 @@
     kv_full,
     branch_buf,
     branch_in,
+    two_ref,
+    small_ref,
     send,
     recv,
     local,
@@ -634,6 +713,16 @@
     def at_rows(index, size):
         return pl.ds(pl.multiple_of(index * size, size), size)
 
+    f32 = jnp.float32
+    small_ref[...] = jnp.concatenate(
+        [
+            gains_ref[...].astype(f32),
+            router_ref[...].astype(f32),
+            gate_ref[...].astype(f32),
+            jnp.zeros((SMALL - 3 - E, block), f32),
+        ],
+        axis=0,
+    ).astype(jnp.bfloat16)
     links.greet(range(1, 8), range(1, QUARTERS))
     small = Gather(
         links, small_ref, lambda f: small_full.at[f], lambda f, h: small_full.at[f, :, pl.ds(h * 128, 128)]
@@ -650,20 +739,34 @@
         lambda f: out_full.at[f],
         lambda f, h: out_full.at[f, pl.ds(h * (local_width // 2), local_width // 2)],
     )
+    cut = cotangent_all.shape[2]
+    cot = CrossGather(
+        links, cotangent_ref.at[at_rows(tp, quarter), pl.ds(0, cut)], cotangent_all
+    )
+    cot_plane = Gather(
+        links,
+        cotangent_ref.at[:, pl.ds(cut, width - cut)],
+        lambda f: cotangent_plane.at[f],
+        lambda f, h: cotangent_plane.at[f, pl.ds(h * SEQ_DEV, SEQ_DEV)],
+    )
     small.first()
+    cot.first()
     qkv.first()
     small.second()
     small.third()
     small.last()
+    cot.second()
     tokens = tokens_ref[...].astype(jnp.float32)
     rstd_one = lax.rsqrt(jnp.mean(tokens * tokens, axis=1, keepdims=True) + NORM_EPS)
     for b in range(E):
         cols = slice(b * block, (b + 1) * block)
         gain = small_full[b, 0:1, :].astype(jnp.float32)
         hidden_buf[:, cols] = (tokens[:, cols] * rstd_one * gain).astype(jnp.bfloat16)
+    cot.third()
     qkv.second()
     qkv.third()
     outs.first()
+    cot_plane.first()
     qkv.last()
     hidden = hidden_buf[...]
     cosine, sine = cos_ref[...], sin_ref[...]
@@ -683,23 +786,34 @@
     kv.second()
     outs.third()
     kv.third()
+    cot_plane.second()
+    routed, shared = down_ref.shape[1], shared_down_ref.shape[0] // E
+
+    def slab(peer, where):
+        units = pl.ds(pl.multiple_of(peer * shared, 16), shared)
+        pieces = [
+            up_ref.at[peer],
+            shared_up_ref.at[0, units],
+            shared_up_ref.at[1, units],
+            down_ref.at[peer],
+            shared_down_ref.at[units],
+        ]
+        placed, at = [], 0
+        for piece, size in zip(pieces, (2 * routed, shared, shared, routed, shared), strict=True):
+            placed.append((piece, slabs_all.at[where, pl.ds(at, size)]))
+            at += size
+        return placed
+
     slab_copies = []
     for bits in (6, 7, 2, 3, 4, 5, 1):
         peer = links.peer(bits)
-        slab_copies.append(
-            links.remote(slabs_ref.at[peer], slabs_all.at[fs], (peer, tp), slabs_all.at[peer])
-        )
+        for (piece, place), (_, landing) in zip(slab(peer, fs), slab(peer, peer), strict=True):
+            slab_copies.append(links.remote(piece, place, (peer, tp), landing))
     for out, back in slab_copies:
         out.start()
-    slab_own = links.inside(slabs_ref.at[fs], slabs_all.at[fs])
-    slab_own.start()
-    cot = Gather(
-        links,
-        cotangent_ref,
-        lambda f: cotangent_all.at[f],
-        lambda f, h: cotangent_all.at[f, pl.ds(h * SEQ_DEV, SEQ_DEV)],
-    )
-    cot.first()
+    slab_own = [links.inside(piece, place) for piece, place in slab(fs, fs)]
+    for copy in slab_own:
+        copy.start()
     kv.last()
     kv_keep = links.inside(kv_full, kv_out)
     kv_keep.start()
@@ -708,7 +822,7 @@
     query_pos = fs * SEQ_DEV + lax.broadcasted_iota(jnp.int32, (SEQ_DEV, length), 0)
     for s in range(seqs):
         here = slice(s * SEQ_DEV, (s + 1) * SEQ_DEV)
-        allowed = (key_pos <= query_pos) & (key_pos >= start_ref[here, :])
+        allowed = (key_pos <= query_pos) & (key_pos >= as_column(start_ref[s : s + 1, :]))
         for h in range(heads):
             cols = slice(h * HD, (h + 1) * HD)
             vcols = slice(local_width + h * HD, local_width + (h + 1) * HD)
@@ -723,6 +837,7 @@
                 jnp.bfloat16
             )
     outs.last()
+    cot_plane.third()
     out_keep = links.inside(out_full, out_out)
     out_keep.start()
     small_keep = links.inside(small_full, small_out)
@@ -745,7 +860,6 @@
         )
     for out, back in branch:
         out.start()
-    cot.second()
     for out, back in branch:
         back.wait_recv()
     mine = at_rows(tp, quarter)
@@ -768,10 +882,14 @@
     odds = jnp.exp(masked - jnp.max(masked, axis=1, keepdims=True))
     odds = jnp.where(routed, odds, 0.0)
     probs = odds / jnp.sum(odds, axis=1, keepdims=True)
-    routes = routes_ref[mine, :]
-    chosen = jnp.zeros((quarter, SMALL), jnp.float32)
-    for k in range(routes.shape[1]):
-        chosen = chosen + (routes[:, k : k + 1] == lane - 2).astype(jnp.float32)
+    expert = lax.broadcasted_iota(jnp.int32, (SMALL, rows), 0) - 2
+    named = jnp.zeros((SMALL, rows), jnp.float32)
+    for k in range(routes_ref.shape[0]):
+        named = named + (routes_ref[k : k + 1, :] == expert).astype(jnp.float32)
+    pick = lax.broadcasted_iota(jnp.int32, (quarter, rows), 1) == (
+        tp * quarter + lax.broadcasted_iota(jnp.int32, (quarter, rows), 0)
+    )
+    chosen = matmul_nt(pick.astype(jnp.bfloat16), named.astype(jnp.bfloat16))
     gate_value = 1.0 / (1.0 + jnp.exp(-logits))
     scales = jnp.where(lane == 2 + E, gate_value, probs * chosen)
     scales_ref[...] = jnp.concatenate([scales, probs, chosen], axis=1)
@@ -780,18 +898,41 @@
     two_ref[:, width:] = jnp.concatenate(
         [high, low, jnp.zeros((quarter, SIDE - 2 * SMALL), jnp.bfloat16)], axis=1
     )
-    cot.third()
+    two_keep = links.inside(two_ref, two_out.at[0])
+    two_keep.start()
+    two_along = []
+    for step in range(1, QUARTERS):
+        there = two_out.at[step]
+        two_along.append(links.remote(two_ref, there, (fs, links.along(step)), there))
+    for out, back in two_along:
+        out.start()
+    cot_plane.last()
     cot.last()
-    for out, back in slab_copies:
+    for out, back in slab_copies + two_along:
         back.wait_recv()
-    slab_own.wait()
-    for out, back in slab_copies + branch:
+    for out, back in slab_copies + branch + two_along:
         out.wait_send()
-    for copy in (qkv_keep, kv_keep, out_keep, small_keep):
+    for copy in (*slab_own, two_keep, qkv_keep, kv_keep, out_keep, small_keep):
         copy.wait()
 
 
-def forward_call(tokens, cotangent, qkv_weight, out_weight, small, slabs, cosine, sine, start, routes):
+def forward_call(
+    tokens,
+    cotangent,
+    qkv_weight,
+    out_weight,
+    norm_gains,
+    router_weight,
+    shared_gate,
+    up,
+    shared_up,
+    down,
+    shared_down,
+    cosine,
+    sine,
+    start,
+    routes,
+):
     rows, width = tokens.shape
     block = width // E
     local_width = qkv_weight.shape[2]
@@ -801,14 +942,15 @@
     vmem = pl.BlockSpec(memory_space=pltpu.VMEM)
     hbm = pl.BlockSpec(memory_space=pl.ANY)
     outs = [
-        (sds((quarter, width + SIDE), bf), vmem),
+        (sds((QUARTERS, quarter, width + SIDE), bf), hbm),
         (sds((quarter, width), f32), vmem),
         (sds((quarter, 3 * SMALL), f32), vmem),
         (sds((rows, local_width), bf), vmem),
         (sds((rows, local_width), bf), vmem),
         (sds((rows, width), bf), vmem),
-        (sds(slabs.shape, bf), hbm),
-        (sds((E, rows, width), bf), hbm),
+        (sds((E, 3 * (down.shape[1] + shared_down.shape[0] // E), block), bf), hbm),
+        (sds((E, rows, CUT), bf), hbm),
+        (sds((E, rows, width - CUT), bf), hbm),
         (sds((E, rows, 2 * local_width), bf), hbm),
         (sds((3, width, local_width), bf), hbm),
         (sds((E, local_width, block), bf), hbm),
@@ -818,7 +960,7 @@
         forward_kernel,
         name="attention_forward",
         out_shape=[o[0] for o in outs],
-        in_specs=[vmem, hbm, hbm, hbm, hbm, hbm, vmem, vmem, vmem, vmem],
+        in_specs=[vmem, hbm, hbm, hbm, vmem, vmem, vmem, hbm, hbm, hbm, hbm, vmem, vmem, vmem, vmem],
         out_specs=[o[1] for o in outs],
         scratch_shapes=[
             pltpu.VMEM((3, width, local_width), bf),
@@ -828,22 +970,81 @@
             pltpu.VMEM((E, rows, 2 * local_width), bf),
             pltpu.VMEM((rows, width), bf),
             pltpu.VMEM((QUARTERS - 1, quarter, width), bf),
-            pltpu.SemaphoreType.DMA((64,)),
-            pltpu.SemaphoreType.DMA((64,)),
-            pltpu.SemaphoreType.DMA((16,)),
+            pltpu.VMEM((quarter, width + SIDE), bf),
+            pltpu.VMEM((SMALL, block), bf),
+            pltpu.SemaphoreType.DMA((128,)),
+            pltpu.SemaphoreType.DMA((128,)),
+            pltpu.SemaphoreType.DMA((32,)),
         ],
         compiler_params=pltpu.CompilerParams(
             collective_id=1, has_side_effects=True, vmem_limit_bytes=56 * 2**20
         ),
-    )(tokens, cotangent, qkv_weight, out_weight, small, slabs, cosine, sine, start, routes)
-
-
-def flip_by(index, bits):
-    total = 0
-    for bit in (1, 2, 4):
-        a, b = (index // bit) % 2, (bits // bit) % 2
-        total = total + bit * (a + b - 2 * a * b)
-    return total
+    )(
+        tokens,
+        cotangent,
+        qkv_weight,
+        out_weight,
+        norm_gains,
+        router_weight,
+        shared_gate,
+        up,
+        shared_up,
+        down,
+        shared_down,
+        cosine,
+        sine,
+        start,
+        routes,
+    )
+
+
+class RowGather:
+    def __init__(self, links, source, slot, half):
+        self.links = links
+
+        def to(bits, owner, h=None):
+            view = slot if h is None else lambda k: half(k, h)
+            start = source if owner == 0 and source is not None else view(owner)
+            return links.remote(
+                start, view(owner ^ bits), (links.peer(bits), links.tp), view(owner ^ bits)
+            )
+
+        x, y, c = X_BIT, Y_BIT, CORE_BIT
+        self.keep = None if source is None else links.inside(source, slot(0))
+        self.own = [to(x, 0), to(y, 0), to(c, 0)]
+        self.x_on = [to(y, x, 0), to(c, x)]
+        self.y_on = [to(x, y, 1), to(c, y)]
+        self.d_on = [to(c, x + y, 0), to(c, x + y, 1)]
+
+    def first(self):
+        for out, back in self.own:
+            out.start()
+        if self.keep is not None:
+            self.keep.start()
+
+    def second(self):
+        self.own[0][1].wait_recv()
+        for out, back in self.x_on:
+            out.start()
+        self.own[1][1].wait_recv()
+        for out, back in self.y_on:
+            out.start()
+
+    def third(self):
+        self.x_on[0][1].wait_recv()
+        self.d_on[0][0].start()
+        self.y_on[0][1].wait_recv()
+        self.d_on[1][0].start()
+
+    def last(self):
+        if self.keep is not None:
+            self.keep.wait()
+        for out, back in (self.own[2], self.x_on[1], self.y_on[1], *self.d_on):
+            back.wait_recv()
+
+    def sent(self):
+        for out, back in self.own + self.x_on + self.y_on + self.d_on:
+            out.wait_send()
 
 
 def expert_kernel(
@@ -853,6 +1054,7 @@
     residual_ref,
     cotangent_ref,
     cotangent_all,
+    cotangent_plane,
     slabs_ref,
     small_ref,
     output_ref,
@@ -871,6 +1073,8 @@
     side_in,
     rows_in,
     cols_in,
+    own_rows,
+    own_cols,
     staged,
     send,
     recv,
@@ -879,77 +1083,109 @@
 ):
     links = Links(send, recv, local)
     fs, tp = links.fs, links.tp
-    quarter = two_ref.shape[0]
+    quarter, width = residual_ref.shape
     rows = quarter * QUARTERS
-    width = residual_ref.shape[1]
     block = width // E
     count = weights.shape[0] // 3
     out_width = output_ref.shape[1]
     back_width = width + SIDE
-    whole = back_width + width
 
     def at_rows(index, size):
         return pl.ds(pl.multiple_of(index * size, size), size)
 
     links.greet(range(1, 8), range(1, QUARTERS))
-    along = []
-    for step in range(1, QUARTERS):
-        here = two_all.at[fs, at_rows(tp, quarter)]
-        landing = two_all.at[fs, at_rows(links.along(QUARTERS - step), quarter)]
-        along.append(links.remote(two_ref, here, (fs, links.along(step)), landing))
+
+    def slot(s, k, h=None):
+        start = (3 - k // 2) * quarter
+        size = quarter
+        if h is not None:
+            size = quarter // 2
+            start = start + h * size
+        return two_all.at[2 * s + 1 - k % 2, pl.ds(start, size)]
+
     gathers = []
-    for step in range(QUARTERS):
-        q = links.along(QUARTERS - step) if step else tp
+    for s in range(QUARTERS):
         gathers.append(
-            Gather(
+            RowGather(
                 links,
-                two_ref if step == 0 else None,
-                lambda f, q=q: two_all.at[f, at_rows(q, quarter)],
-                lambda f, h, q=q: two_all.at[f, at_rows(q * 2 + h, quarter // 2)],
+                two_ref.at[s],
+                lambda k, s=s: slot(s, k),
+                lambda k, h, s=s: slot(s, k, h),
             )
         )
     gathers[0].first()
-    for out, back in along:
-        out.start()
+    gathers[1].first()
     loads = [
         links.inside(slabs_ref.at[g], weights.at[:, pl.ds(g * block, block)]) for g in range(E)
     ]
-    loads.append(links.inside(cotangent_all, cot_all))
+    cut = cotangent_all.shape[2]
+    loads.append(links.inside(cotangent_all, cot_all.at[:, :, pl.ds(0, cut)]))
+    for s in range(QUARTERS):
+        q = links.along(QUARTERS - s)
+        for k in range(E):
+            there = cot_all.at[
+                2 * s + 1 - k % 2, pl.ds((3 - k // 2) * quarter, quarter), pl.ds(cut, width - cut)
+            ]
+            loads.append(
+                links.inside(cotangent_plane.at[links.peer(k), at_rows(q, quarter)], there)
+            )
     for load in loads:
         load.start()
-    for step in range(1, QUARTERS):
-        along[step - 1][1].wait_recv()
-        gathers[step].first()
-        gathers[step - 1].second()
-        if step >= 2:
-            gathers[step - 2].third()
-    gathers[3].second()
-    gathers[2].third()
-    gathers[3].third()
-    for load in loads:
-        load.wait()
-    for gather in gathers:
-        gather.last()
-
-    core_copies = []
-    for i in range(4):
-        core_copies.append(
-            links.remote(
-                parts.at[i % 2], core_in.at[i % 2], (links.peer(CORE_BIT), tp), core_in.at[i % 2]
+
+    core = [
+        links.remote(
+            parts.at[s % 2], core_in.at[s % 2], (links.peer(CORE_BIT), tp), core_in.at[s % 2]
+        )
+        for s in range(QUARTERS)
+    ]
+    diag, side, rows_along, cols_along = [], [], [], []
+    for s in range(QUARTERS):
+        held = parts.at[2 + s % 3]
+        diag.append(
+            [
+                links.remote(
+                    held.at[pl.ds(h * (quarter // 2), quarter // 2)],
+                    diag_in.at[s, h],
+                    (links.peer(bits), tp),
+                    diag_in.at[s, h],
+                )
+                for h, bits in enumerate((Y_BIT, X_BIT))
+            ]
+        )
+        side.append(
+            [
+                links.remote(
+                    held.at[pl.ds((3 - bits // 2) * quarter, quarter)],
+                    side_in.at[s, i],
+                    (links.peer(bits), tp),
+                    side_in.at[s, i],
+                )
+                for i, bits in enumerate((X_BIT, Y_BIT))
+            ]
+        )
+        last = pl.ds(3 * quarter, quarter)
+        if s:
+            rows_along.append(
+                links.remote(
+                    held.at[last, pl.ds(0, back_width)],
+                    rows_in.at[s - 1],
+                    (fs, links.along(QUARTERS - s)),
+                    rows_in.at[s - 1],
+                )
             )
-        )
-    half_rows = rows // 2
-    diag_y = links.remote(
-        parts.at[2, pl.ds(0, half_rows)], diag_in.at[0], (links.peer(Y_BIT), tp), diag_in.at[0]
-    )
-    diag_x = links.remote(
-        parts.at[2, pl.ds(half_rows, half_rows)],
-        diag_in.at[1],
-        (links.peer(X_BIT), tp),
-        diag_in.at[1],
-    )
-    side_x = links.remote(parts.at[3], side_in.at[0], (links.peer(X_BIT), tp), side_in.at[0])
-    side_y = links.remote(parts.at[4], side_in.at[1], (links.peer(Y_BIT), tp), side_in.at[1])
+        q = links.along(QUARTERS - s)
+        for step in range(1, QUARTERS):
+            peer = links.along(step)
+            start = pl.multiple_of(back_width + peer * out_width, 128)
+            q_there = links.along(2 * QUARTERS - s - step)
+            cols_along.append(
+                links.remote(
+                    held.at[last, pl.ds(start, out_width)],
+                    cols_in.at[step - 1, at_rows(q, quarter)],
+                    (fs, peer),
+                    cols_in.at[step - 1, at_rows(q_there, quarter)],
+                )
+            )
 
     sub = lax.broadcasted_iota(jnp.int32, (8, SIDE), 0)
     lane = lax.broadcasted_iota(jnp.int32, (8, SIDE), 1)
@@ -962,125 +1198,163 @@
         jnp.bfloat16
     )
 
-    def one_block(index, slot):
-        first[: 2 * count] = matmul_nt(weights[: 2 * count], two_all[index, :, :width])
-        first[2 * count :] = matmul_nt(weights[2 * count :], cot_all[index])
-        scale = matmul_nt(pick_in, two_all[index, :, width:])
-        cols = pl.ds(pl.multiple_of(index * rows, rows), rows)
+    def one_block(t, slot_out, pause):
+        first[: 2 * count] = matmul_nt(weights[: 2 * count], two_all[t, :, :width])
+        pause(0)
+        first[2 * count :] = matmul_nt(weights[2 * count :], cot_all[t])
+        scale = matmul_nt(pick_in, two_all[t, :, width:])
+        cols = pl.ds(pl.multiple_of(t * rows, rows), rows)
         dots = []
-        for group, (low, high) in enumerate(((0, routed), (routed, count))):
-            gate = first[low:high]
-            up = first[count + low : count + high]
-            grad = first[2 * count + low : 2 * count + high]
+        shared = count - routed
+        groups = ((0, 2 * count, routed), (2 * routed, 2 * count + routed, shared))
+        for group, (low, last, size) in enumerate(groups):
+            gate = first[low : low + size]
+            up = first[low + size : low + 2 * size]
+            grad = first[last : last + size]
             by = scale[group : group + 1]
             sigmoid = 1.0 / (1.0 + jnp.exp(-gate))
             silu = gate * sigmoid
             active = silu * up
-            units[2 * count + low : 2 * count + high, cols] = (by * active).astype(jnp.bfloat16)
+            units[last : last + size, cols] = (by * active).astype(jnp.bfloat16)
             dots.append(jnp.sum(active * grad, axis=0, keepdims=True))
             active_grad = by * grad
-            units[low:high, cols] = (
+            units[low : low + size, cols] = (
                 active_grad * up * sigmoid * (1.0 + gate * (1.0 - sigmoid))
             ).astype(jnp.bfloat16)
-            units[count + low : count + high, cols] = (active_grad * silu).astype(jnp.bfloat16)
+            units[low + size : low + 2 * size, cols] = (active_grad * silu).astype(jnp.bfloat16)
         both = jnp.concatenate([*dots, jnp.zeros((6, rows), jnp.float32)], axis=0)
-        parts[slot, :, width:back_width] = matmul_tn(both.astype(jnp.bfloat16), pick_out).astype(
-            jnp.bfloat16
-        )
+        parts[slot_out, :, width:back_width] = matmul_tn(
+            both.astype(jnp.bfloat16), pick_out
+        ).astype(jnp.bfloat16)
+        pause(1)
         tile = 512
         for n in range(width // tile):
             at = slice(n * tile, (n + 1) * tile)
-            parts[slot, :, at] = matmul_tn(units[: 2 * count, cols], weights[: 2 * count, at]).astype(
-                jnp.bfloat16
-            )
+            parts[slot_out, :, at] = matmul_tn(
+                units[: 2 * count, cols], weights[: 2 * count, at]
+            ).astype(jnp.bfloat16)
+            if n == 1:
+                pause(2)
+        for n in range(width // tile):
+            at = slice(n * tile, (n + 1) * tile)
             beyond = slice(back_width + n * tile, back_width + (n + 1) * tile)
-            parts[slot, :, beyond] = matmul_tn(
+            parts[slot_out, :, beyond] = matmul_tn(
                 units[2 * count :, cols], weights[2 * count :, at]
             ).astype(jnp.bfloat16)
-
-    chunk = 32
-
-    def add_in(slot, others):
-        @pl.loop(0, rows // chunk)
-        def _(r):
-            at = pl.ds(pl.multiple_of(r * chunk, chunk), chunk)
-            total = parts[slot, at, :].astype(jnp.float32)
-            for ref in others:
-                total = total + ref[at, :].astype(jnp.float32)
-            parts[slot, at, :] = total.astype(jnp.bfloat16)
-
-    def add_half(slot, ref, start):
-        @pl.loop(0, half_rows // chunk)
+        pause(3)
+
+    def add_in(held, start, size, others):
+        chunk = 32
+
+        @pl.loop(0, size // chunk)
         def _(r):
             at = pl.ds(pl.multiple_of(start + r * chunk, chunk), chunk)
             there = pl.ds(pl.multiple_of(r * chunk, chunk), chunk)
-            total = parts[slot, at, :].astype(jnp.float32) + ref[there, :].astype(jnp.float32)
-            parts[slot, at, :] = total.astype(jnp.bfloat16)
-
-    def free_core():
-        pl.semaphore_signal(
-            credit, inc=1, device_id=(links.peer(CORE_BIT), tp), device_id_type=MESH
-        )
+            total = parts[held, at, :].astype(jnp.float32)
+            for ref in others:
+                total = total + ref[there, :].astype(jnp.float32)
+            parts[held, at, :] = total.astype(jnp.bfloat16)
+
+    def to_core(s):
+        if s >= 2:
+            pl.semaphore_wait(credit, 1)
+        core[s][0].start()
+
+    def diagonal(s):
+        core[s][1].wait_recv()
+        add_in(2 + s % 3, 0, rows, [core_in.at[s % 2]])
+        if s < 2:
+            pl.semaphore_signal(
+                credit, inc=1, device_id=(links.peer(CORE_BIT), tp), device_id_type=MESH
+            )
+        for out, back in diag[s]:
+            out.start()
+
+    def sideways(s):
+        for h, (out, back) in enumerate(diag[s]):
+            back.wait_recv()
+            start = (2 - h) * quarter + h * (quarter // 2)
+            add_in(2 + s % 3, start, quarter // 2, [diag_in.at[s, h]])
+            side[s][h][0].start()
+
+    def finish(s):
+        held = 2 + s % 3
+        for out, back in side[s]:
+            back.wait_recv()
+        last = slice(3 * quarter, rows)
+        add_in(held, 3 * quarter, quarter, [side_in.at[s, 0], side_in.at[s, 1]])
+        if s == 0:
+            own_rows[...] = parts[held, last, :back_width].astype(jnp.float32)
+            parts[held, last, back_width:] = (
+                parts[held, last, back_width:].astype(jnp.float32) + residual_ref[...]
+            ).astype(jnp.bfloat16)
+        else:
+            rows_along[s - 1][0].start()
+        for out, back in cols_along[3 * s : 3 * s + 3]:
+            out.start()
+        start = pl.multiple_of(back_width + tp * out_width, 128)
+        own_cols[at_rows(links.along(QUARTERS - s), quarter), :] = parts[
+            held, last, pl.ds(start, out_width)
+        ].astype(jnp.float32)
+
+    def before_last():
+        core[1][0].wait_send()
+
+    def slot_free():
+        for out, back in diag[0] + side[0] + cols_along[:3]:
+            out.wait_send()
+
+    plan = {
+        (0, 0): [gathers[1].third, gathers[2].second],
+        (0, 1): [gathers[2].third],
+        (0, 2): [gathers[3].second],
+        (0, 3): [lambda: to_core(0), gathers[1].last],
+        (1, 0): [gathers[3].third],
+        (1, 3): [lambda: diagonal(0), gathers[2].last],
+        (2, 2): [lambda: sideways(0)],
+        (2, 3): [lambda: to_core(1)],
+        (3, 3): [lambda: diagonal(1), gathers[3].last],
+        (4, 2): [lambda: sideways(1)],
+        (4, 3): [lambda: to_core(2)],
+        (5, 0): [lambda: finish(0)],
+        (5, 3): [lambda: diagonal(2)],
+        (6, 2): [lambda: sideways(2)],
+        (6, 3): [lambda: to_core(3)],
+        (7, 0): [lambda: finish(1)],
+        (7, 3): [lambda: diagonal(3)],
+    }
+    before = {4: [core[0][0].wait_send], 6: [before_last], 7: [slot_free]}
+
+    gathers[0].second()
+    gathers[2].first()
+    gathers[0].third()
+    gathers[1].second()
+    gathers[3].first()
+    for load in loads:
+        load.wait()
+    gathers[0].last()
 
     @pl.loop(0, 8)
     def _(t):
-        pair = t // 2
-        second = t % 2
-        bits = 7 - 4 * pair + 6 * (pair // 2) - second
-        index = flip_by(fs, bits)
-        slot = second * (2 + pair - 3 * (pair // 3)) + (1 - second) * (pair % 2)
-
-        @pl.when(t == 4)
-        def _():
-            core_copies[0][0].wait_send()
-
-        @pl.when(t == 6)
-        def _():
-            core_copies[1][0].wait_send()
-
-        @pl.when(t == 7)
-        def _():
-            diag_y[0].wait_send()
-            diag_x[0].wait_send()
-
-        one_block(index, slot)
-        for i in range(4):
-
-            @pl.when(t == 2 * i)
-            def _(i=i):
-                if i >= 2:
-                    pl.semaphore_wait(credit, 1)
-                core_copies[i][0].start()
-
-        @pl.when(t == 1)
-        def _():
-            core_copies[0][1].wait_recv()
-            add_in(2, [core_in.at[0]])
-            free_core()
-            diag_y[0].start()
-            diag_x[0].start()
-
-        @pl.when(t == 3)
-        def _():
-            core_copies[1][1].wait_recv()
-            add_in(3, [core_in.at[1]])
-            free_core()
-            diag_y[1].wait_recv()
-            add_half(3, diag_in.at[0], 0)
-            side_x[0].start()
-
-        @pl.when(t == 5)
-        def _():
-            core_copies[2][1].wait_recv()
-            add_in(4, [core_in.at[0]])
-            diag_x[1].wait_recv()
-            add_half(4, diag_in.at[1], half_rows)
-            side_y[0].start()
-
-        @pl.when(t == 7)
-        def _():
-            core_copies[3][1].wait_recv()
-            add_in(2, [core_in.at[1]])
+        s = t // 2
+        slot_out = (1 - t % 2) * (s % 2) + (t % 2) * (2 + s % 3)
+        for at, steps in before.items():
+
+            @pl.when(t == at)
+            def _(steps=steps):
+                for step in steps:
+                    step()
+
+        def pause(point):
+            for (at, where), steps in plan.items():
+                if where == point:
+
+                    @pl.when(t == at)
+                    def _(steps=steps):
+                        for step in steps:
+                            step()
+
+        one_block(t, slot_out, pause)
 
     keeps = []
 
@@ -1096,43 +1370,16 @@
         keep.start()
         keeps.append(keep)
 
-    for g in range(E // 2):
+    for g in range(3):
         weight_grads(g)
-    side_x[1].wait_recv()
-    side_y[1].wait_recv()
-    add_in(2, [side_in.at[0], side_in.at[1]])
-    own = at_rows(tp, quarter)
-    parts[2, own, back_width:] = (
-        parts[2, own, back_width:].astype(jnp.float32) + residual_ref[...]
-    ).astype(jnp.bfloat16)
-    column = []
-    for step in range(1, QUARTERS):
-        peer = links.along(step)
-        column.append(
-            links.remote(
-                parts.at[2, at_rows(peer, quarter), pl.ds(0, back_width)],
-                rows_in.at[step - 1],
-                (fs, peer),
-                rows_in.at[step - 1],
-            )
-        )
-    for step in range(1, QUARTERS):
-        peer = links.along(step)
-        column.append(
-            links.remote(
-                parts.at[2, :, pl.ds(pl.multiple_of(back_width + peer * out_width, 128), out_width)],
-                cols_in.at[step - 1],
-                (fs, peer),
-                cols_in.at[step - 1],
-            )
-        )
-    for out, back in column:
-        out.start()
-    for g in range(E // 2, E):
+    sideways(3)
+    finish(2)
+    for g in range(3, E):
         weight_grads(g)
-    for out, back in column[:3]:
+    finish(3)
+    for out, back in rows_along:
         back.wait_recv()
-    total = parts[2, own, :back_width].astype(jnp.float32)
+    total = own_rows[...]
     for step in range(1, QUARTERS):
         total = total + rows_in[step - 1].astype(jnp.float32)
     dots = total[:, width : width + SMALL]
@@ -1155,11 +1402,12 @@
         gain = small_ref[b, 1:2, :].astype(jnp.float32)
         back_ref[:, at] = two_grad
         mean = mean + jnp.sum(two_grad * gain * normed, axis=1, keepdims=True)
-        grads = matmul_tn(logit_grad, two_all[fs, own, at])
-        sub = lax.broadcasted_iota(jnp.int32, (SMALL, block), 0)
+        grads = matmul_tn(logit_grad, two_all[1, 3 * quarter :, at])
+        line = lax.broadcasted_iota(jnp.int32, (SMALL, block), 0)
         gain_grad = jnp.sum(two_grad * normed, axis=0, keepdims=True)
-        small_grad_ref[:, at] = jnp.where(sub == 1, gain_grad, grads)
+        small_grad_ref[:, at] = jnp.where(line == 1, gain_grad, grads)
     mean = mean / width
+    own = at_rows(tp, quarter)
     for b in range(E):
         at = slice(b * block, (b + 1) * block)
         gain = small_ref[b, 1:2, :].astype(jnp.float32)
@@ -1169,25 +1417,30 @@
         )
         back_ref[:, at] = grad
         branch_ref[:, at] = grad.astype(jnp.bfloat16)
-    for out, back in column[3:]:
+    for out, back in cols_along:
         back.wait_recv()
-    start = pl.multiple_of(back_width + tp * out_width, 128)
-    total = parts[2, :, pl.ds(start, out_width)].astype(jnp.float32)
+    total = own_cols[...]
     for step in range(1, QUARTERS):
         total = total + cols_in[step - 1].astype(jnp.float32)
     output_ref[...] = total.astype(jnp.bfloat16)
-    for out, back in along + core_copies[2:] + [side_x, side_y] + column:
+    for out, back in core[2:] + rows_along + cols_along[3:]:
         out.wait_send()
+    for s in range(1, QUARTERS):
+        for out, back in diag[s] + side[s]:
+            out.wait_send()
+    for gather in gathers:
+        gather.sent()
     for keep in keeps[-2:]:
         keep.wait()
 
 
 def expert_call(
-    two_rows, router_rows, residual_rows, cotangent, cotangent_all, slabs, small_full, out_width, routed
+    two_rows, router_rows, residual_rows, cotangent, cotangent_all, cotangent_plane, slabs, small_full, out_width, routed
 ):
     quarter, width = residual_rows.shape
     rows = quarter * QUARTERS
     back_width = width + SIDE
+    whole = back_width + width
     block = width // E
     bf, f32 = jnp.bfloat16, jnp.float32
     sds = jax.ShapeDtypeStruct
@@ -1205,7 +1458,7 @@
         functools.partial(expert_kernel, routed),
         name="experts",
         out_shape=[o[0] for o in outs],
-        in_specs=[vmem, vmem, vmem, vmem, hbm, hbm, vmem],
+        in_specs=[hbm, vmem, vmem, vmem, hbm, hbm, hbm, vmem],
         out_specs=[o[1] for o in outs],
         scratch_shapes=[
             pltpu.VMEM((E, rows, back_width), bf),
@@ -1213,22 +1466,33 @@
             pltpu.VMEM((units, width), bf),
             pltpu.VMEM((units, E * rows), bf),
             pltpu.VMEM((units, rows), f32),
-            pltpu.VMEM((5, rows, back_width + width), bf),
-            pltpu.VMEM((2, rows, back_width + width), bf),
-            pltpu.VMEM((2, rows // 2, back_width + width), bf),
-            pltpu.VMEM((2, rows, back_width + width), bf),
+            pltpu.VMEM((5, rows, whole), bf),
+            pltpu.VMEM((2, rows, whole), bf),
+            pltpu.VMEM((QUARTERS, 2, quarter // 2, whole), bf),
+            pltpu.VMEM((QUARTERS, 2, quarter, whole), bf),
             pltpu.VMEM((QUARTERS - 1, quarter, back_width), bf),
             pltpu.VMEM((QUARTERS - 1, rows, out_width), bf),
+            pltpu.VMEM((quarter, back_width), f32),
+            pltpu.VMEM((rows, out_width), f32),
             pltpu.VMEM((2, units, block), bf),
-            pltpu.SemaphoreType.DMA((64,)),
-            pltpu.SemaphoreType.DMA((64,)),
-            pltpu.SemaphoreType.DMA((24,)),
+            pltpu.SemaphoreType.DMA((80,)),
+            pltpu.SemaphoreType.DMA((80,)),
+            pltpu.SemaphoreType.DMA((56,)),
             pltpu.SemaphoreType.REGULAR,
         ],
         compiler_params=pltpu.CompilerParams(
-            collective_id=2, has_side_effects=True, vmem_limit_bytes=62 * 2**20
+            collective_id=2, has_side_effects=True, vmem_limit_bytes=63 * 2**20
         ),
-    )(two_rows, router_rows, residual_rows, cotangent, cotangent_all, slabs, small_full)
+    )(
+        two_rows,
+        router_rows,
+        residual_rows,
+        cotangent,
+        cotangent_all,
+        cotangent_plane,
+        slabs,
+        small_full,
+    )
 
 
 class Scatter:
@@ -1325,7 +1589,10 @@
     qkv_own,
     out_own,
     small_own,
-    slabs_all,
+    up_all,
+    shared_up_all,
+    down_all,
+    shared_down_all,
     kv_full,
     qkv_full,
     out_full,
@@ -1380,16 +1647,33 @@
     for out, back in branch:
         out.start()
     branch_all[own, :] = branch_ref[...]
+    routed, shared = down_all.shape[1], shared_down_all.shape[0] // E
+
+    def slab(block_index, source):
+        units = pl.ds(pl.multiple_of(source * shared, 16), shared)
+        places = [
+            up_all.at[source],
+            shared_up_all.at[0, units],
+            shared_up_all.at[1, units],
+            down_all.at[source],
+            shared_down_all.at[units],
+        ]
+        placed, at = [], 0
+        for place, size in zip(places, (2 * routed, shared, shared, routed, shared), strict=True):
+            placed.append((slabs_ref.at[block_index, pl.ds(at, size)], place))
+            at += size
+        return placed
+
     slab_copies = []
-    for bits in (6, 7, 2, 3, 4, 5, 1):
+    for bits in (1, 6, 7, 2, 4, 3, 5):
         peer = links.peer(bits)
-        slab_copies.append(
-            links.remote(slabs_ref.at[peer], slabs_all.at[fs], (peer, tp), slabs_all.at[peer])
-        )
-    for out, back in slab_copies:
+        for (piece, place), (_, landing) in zip(slab(peer, fs), slab(peer, peer), strict=True):
+            slab_copies.append(links.remote(piece, place, (peer, tp), landing))
+    for out, back in slab_copies[:25]:
         out.start()
-    slab_own = links.inside(slabs_ref.at[fs], slabs_all.at[fs])
-    slab_own.start()
+    slab_own = [links.inside(piece, place) for piece, place in slab(fs, fs)]
+    for copy in slab_own:
+        copy.start()
     kv_load = links.inside(kv_ref, kv_full)
     kv_load.start()
     out_load = links.inside(out_ref, out_full)
@@ -1405,7 +1689,7 @@
     query_pos = fs * SEQ_DEV + lax.broadcasted_iota(jnp.int32, (SEQ_DEV, length), 0)
     for s in range(seqs):
         here = slice(s * SEQ_DEV, (s + 1) * SEQ_DEV)
-        allowed = (key_pos <= query_pos) & (key_pos >= start_ref[here, :])
+        allowed = (key_pos <= query_pos) & (key_pos >= as_column(start_ref[s : s + 1, :]))
         for h in range(heads):
             cols = slice(h * HD, (h + 1) * HD)
             keys = kv_full[:, here, cols].reshape(length, HD)
@@ -1463,6 +1747,8 @@
     out_sum.diagonal()
     qkv_load.wait()
     kv_sum.finish(kv_total)
+    for out, back in slab_copies[25:]:
+        out.start()
     projected[1] = turn(kv_total[:, :local_width], cos_ref[...], -sin_ref[...]).astype(jnp.bfloat16)
     projected[2] = kv_total[:, local_width:].astype(jnp.bfloat16)
     for b in range(E):
@@ -1555,8 +1841,8 @@
     small_own[...] = small_column[0] + small_column[1] + small_column[2] + small_column[3]
     for out, back in spread + slab_copies:
         back.wait_recv()
-    slab_own.wait()
-    keep.wait()
+    for copy in (*slab_own, keep):
+        copy.wait()
     for out, back in branch + slab_copies + column + spread + small_copies + small_spread:
         out.wait_send()
     for scatter in (kv_sum, out_sum, qkv_sum):
@@ -1579,11 +1865,13 @@
     sine,
     start,
     slabs,
+    routed,
 ):
     quarter, width = residual_grad.shape
     rows = quarter * QUARTERS
     block = width // E
     local_width = query_rows.shape[1]
+    shared = slabs.shape[1] // 3 - routed
     bf, f32 = jnp.bfloat16, jnp.float32
     sds = jax.ShapeDtypeStruct
     vmem = pl.BlockSpec(memory_space=pltpu.VMEM)
@@ -1593,7 +1881,10 @@
         (sds((3 * block, local_width), f32), vmem),
         (sds((local_width, block), f32), vmem),
         (sds((SMALL, block), f32), vmem),
-        (sds(slabs.shape, bf), hbm),
+        (sds((E, 2 * routed, block), bf), hbm),
+        (sds((2, E * shared, block), bf), hbm),
+        (sds((E, routed, block), bf), hbm),
+        (sds((E * shared, block), bf), hbm),
     ]
 
     def scatter_scratch(count, columns):
@@ -1628,8 +1919,8 @@
             pltpu.VMEM((E, SMALL, block), f32),
             pltpu.VMEM((E - 1, SMALL, block), f32),
             pltpu.VMEM((QUARTERS, SMALL, block), f32),
-            pltpu.SemaphoreType.DMA((64,)),
-            pltpu.SemaphoreType.DMA((64,)),
+            pltpu.SemaphoreType.DMA((96,)),
+            pltpu.SemaphoreType.DMA((96,)),
             pltpu.SemaphoreType.DMA((16,)),
         ],
         compiler_params=pltpu.CompilerParams(
@@ -1671,38 +1962,13 @@
 ):
     tok_rows, width = tokens.shape
     seq_count = tok_rows // SEQ_DEV
-    local_width = qkv_weight.shape[2]
-    quarter = tok_rows // QUARTERS
     fs_index = lax.axis_index("fs")
-    tp_index = lax.axis_index("tp")
-    fs_size = E
     query_pos = fs_index * SEQ_DEV + jnp.arange(SEQ_DEV, dtype=jnp.int32)
     positions = jnp.tile(query_pos, seq_count)
     half_cos, half_sin = rope_tables(positions)
     cosine = jnp.concatenate([half_cos, half_cos], axis=1)
     sine = jnp.concatenate([-half_sin, half_sin], axis=1)
-    small = jnp.concatenate(
-        [
-            norm_gains,
-            router_weight,
-            shared_gate[None],
-            jnp.zeros((SMALL - 3 - E, shared_gate.shape[0]), jnp.bfloat16),
-        ],
-        axis=0,
-    )
     routed_units = expert_down.shape[1]
-    shared_units = shared_down.shape[0] // fs_size
-    units = routed_units + shared_units
-    block = expert_down.shape[2]
-    expert_up_slabs = jnp.transpose(expert_gate_up, (0, 2, 3, 1))
-    shared_up_slabs = jnp.transpose(
-        shared_gate_up.reshape(block, 2, fs_size, shared_units), (2, 1, 3, 0)
-    )
-    up_slabs = jnp.concatenate([expert_up_slabs, shared_up_slabs], axis=2)
-    down_slabs = jnp.concatenate(
-        [expert_down, shared_down.reshape(fs_size, shared_units, block)], axis=1
-    )
-    slabs = jnp.concatenate([up_slabs, down_slabs[:, None]], axis=1)
     (
         two_rows,
         residual_rows,
@@ -1712,6 +1978,7 @@
         hidden_one,
         slabs,
         cotangent_all,
+        cotangent_plane,
         kv_all,
         qkv_full,
         out_full,
@@ -1721,12 +1988,17 @@
         cotangent,
         qkv_weight,
         out_weight,
-        small,
-        slabs.reshape(fs_size, 3 * units, block),
+        norm_gains,
+        router_weight,
+        shared_gate[None],
+        jnp.transpose(expert_gate_up, (0, 2, 3, 1)).reshape(E, 2 * routed_units, -1),
+        jnp.transpose(shared_gate_up, (1, 2, 0)),
+        expert_down,
+        shared_down,
         cosine,
         sine,
-        doc_start[:, None],
-        routes,
+        doc_start.reshape(seq_count, SEQ_DEV),
+        routes.T,
     )
     output, branch_rows, residual_grad, small_grad, grad_slabs = expert_call(
         two_rows,
@@ -1734,49 +2006,46 @@
         residual_rows,
         cotangent,
         cotangent_all,
+        cotangent_plane,
         slabs,
         small_full,
         width // QUARTERS,
         routed_units,
     )
-    input_grad, qkv_own, out_own, small_own, grad_slabs = backward_call(
-        branch_rows,
-        residual_grad,
-        small_grad,
-        attended,
-        query_rows,
-        hidden_one,
-        tokens,
-        kv_all,
-        qkv_full,
-        out_full,
-        small_full,
-        cosine,
-        sine,
-        doc_start[:, None],
-        grad_slabs,
-    )
-    input_grad = input_grad.astype(jnp.float32)
-    grad_slabs = grad_slabs.reshape(fs_size, 3, units, block)
-    own = grad_slabs.astype(jnp.float32)
-    expert_up_own = jnp.transpose(own[:, :2, :routed_units], (0, 3, 1, 2))
-    expert_down_own = own[:, 2, :routed_units]
-    shared_up_own = jnp.transpose(own[:, :2, routed_units:], (3, 1, 0, 2)).reshape(
-        shared_gate_up.shape
-    )
-    shared_down_own = own[:, 2, routed_units:].reshape(shared_down.shape)
+    input_grad, qkv_own, out_own, small_own, up_own, shared_up_own, down_own, shared_down_own = (
+        backward_call(
+            branch_rows,
+            residual_grad,
+            small_grad,
+            attended,
+            query_rows,
+            hidden_one,
+            tokens,
+            kv_all,
+            qkv_full,
+            out_full,
+            small_full,
+            cosine,
+            sine,
+            doc_start.reshape(seq_count, SEQ_DEV),
+            grad_slabs,
+            routed_units,
+        )
+    )
+    f32 = jnp.float32
+    up_own = up_own.reshape(E, 2, routed_units, -1)
     return (
         output,
-        input_grad,
+        input_grad.astype(f32),
         qkv_own.reshape(qkv_weight.shape),
         out_own,
         small_own[:2],
         small_own[2 : 2 + E],
         small_own[2 + E],
-        expert_up_own,
-        expert_down_own,
-        shared_up_own,
-        shared_down_own,
+        jnp.transpose(up_own, (0, 3, 1, 2)).astype(f32),
+        down_own.astype(f32),
+        jnp.transpose(shared_up_own, (2, 0, 1)).astype(f32),
+        shared_down_own.astype(f32),
     )
 
 

time: 569 us -> 480 us (0.84)
  Pallas kernels: 518 us -> 443 us
  local copies, waits for them, and re-layouts: 26.9 us -> 16.1 us
    pallas_call x1, Pallas kernels: 190 us -> 150 us  [expert_call(): pl.pallas_call(functools.partial(expert_kernel, routed), name='experts',...]
    pallas_call x1, Pallas kernels: 175 us -> 154 us  [forward_call(): pl.pallas_call(forward_kernel, name='attention_forward', out_shape=[o[0]...]
    pallas_call x1, Pallas kernels: 153 us -> 139 us  [backward_call(): pl.pallas_call(backward_kernel, name='attention_backward', out_shape=[o[0...]
where the time goes in v5:
time: 480 us; the launch traced here: 473 us
  Pallas kernels  443 us (92%)
  local copies, waits for them, and re-layouts  16.1 us (3%)
  other arithmetic  12.5 us (3%)
    pallas_call x1, Pallas kernels, forward_call(): pl.pallas_call(forward_kernel, name='attention_forward', out_shape=[o[0]...  154 us
    pallas_call x1, Pallas kernels, expert_call(): pl.pallas_call(functools.partial(expert_kernel, routed), name='experts',...  150 us
    pallas_call x1, Pallas kernels, backward_call(): pl.pallas_call(backward_kernel, name='attention_backward', out_shape=[o[0...  139 us
    unnamed x17, local copies, waits for them, and re-layouts  10.9 us

profile of v5, /device:TPU:0, one launch (start us, length us, event | category | flops | bytes accessed | tf_op | source)
XLA Modules:
  0.0 472.6 jit_solution(2998105550595958569)
XLA Ops:
  0.7 1.2 broadcast_in_dim.2.gate_ref
  1.9 0.5 fusion
  2.4 0.8 pad_maximum_fusion
  3.3 4.8 %copy.24 = bf16[256,2,1408]{0,2,1:T(8,128)(2,1)} copy(bf16[256,2,1408]{2,1,0:T(2,128)(2,1)} %param.22) | data formatting | bytes 2883584 | tf_op args[9]
  8.1 154.1 %attention_forward.1 = (bf16[4,64,2176]{2,1,0:T(8,128)(2,1)}, f32[64,2048]{1,0:T(8,128)}, f32[64,48]{1,0:T(8,128)}, bf16[256,512]{1,0:T(8,128)(2,1)}, bf16[256,5...) custom-call(bf16[256,2048]{1,0:T(8,128)(2,1)} %tokens_ref.3, ...), custom_call_target="tpu_custom_call" | custom-call | tf_op jit(solution)/shard_map/attention_forward/pallas_call | solution.py:959
  162.2 149.7 %experts.1 = (bf16[256,512]{1,0:T(8,128)(2,1)}, bf16[64,2048]{1,0:T(8,128)(2,1)}, f32[64,2048]{1,0:T(8,128)}, f32[16,2048]{1,0:T(8,128)}, bf16[8,1584,256]{2,1,0:T(8,128)(2,1)}) custom-call(bf16[4,64,2176]{2,1,0:T(8,128)(2,1)} %get-tuple-element.37.two_ref, f32[64,48]{1,0:T(8,128)} %get-tuple-element.38.router_ref, ...), custom_call_target="tpu_custom_call" | custom-call | tf_op jit(solution)/shard_map/experts/pallas_call | solution.py:1457
  311.9 139.0 %attention_backward.1 = (bf16[256,2048]{1,0:T(8,128)(2,1)}, f32[768,512]{1,0:T(8,128)}, f32[512,256]{1,0:T(8,128)}, f32[16,256]{1,0:T(8,128)}, bf16[8,704,256]{2...) custom-call(bf16[64,2048]{1,0:T(8,128)(2,1)} %get-tuple-element.45.branch, ...), custom_call_target="tpu_custom_call" | custom-call | tf_op jit(solution)/shard_map/attention_backward/pallas_call | solution.py:1898
  450.8 0.0 copy-start.3
  450.9 0.0 copy-start.2
  450.9 1.4 slice.11
  452.3 1.3 slice.9
  453.6 1.3 slice.10
  454.9 2.8 convert_element_type.37
  457.7 0.0 copy-done.3
  457.7 0.0 copy-start.1
  457.7 1.2 convert_element_type.44
  458.9 0.0 copy-done.2
  458.9 1.8 convert_element_type.41
  460.7 0.0 copy-done.1
  460.7 0.2 convert_bitcast_fusion.1
  460.9 3.4 copy.25
  464.4 0.0 copy-start.5
  464.4 0.0 copy-start
  464.4 5.1 %convert_bitcast_fusion = f32[8,256,2,352]{1,3,2,0:T(8,128)} fusion(bf16[8,2,352,256]{3,2,1,0:T(8,128)(2,1)} %bitcast.18), kind=kLoop, calls=%fused_computation | loop fusion | flops 1441792 | bytes 8650752 | tf_op jit(solution)/shard_map/convert_element_type | solution.py:2045
  469.5 0.0 copy-done.5
  469.5 0.0 copy-start.4
  469.5 0.7 copy.29
  470.2 0.0 copy-done
  470.2 1.1 copy.30
  471.3 0.0 copy-done.4
  471.3 0.8 copy.31
  (3 shorter events, 0.0 us)
Async XLA Ops:
  450.8 6.8 %copy-start.3 = (bf16[1408,256]{1,0:T(8,128)(2,1)S(1)}, bf16[1408,256]{1,0:T(8,128)(2,1)}, u32[]{:S(2)}) copy-start(bf16[1408,256]{1,0:T(8,128)(2,1)} %get-tuple-element.62) | copy-start | bytes 2162692
  450.9 8.0 %copy-start.2 = (bf16[8,352,256]{2,1,0:T(8,128)(2,1)S(1)}, bf16[8,352,256]{2,1,0:T(8,128)(2,1)}, u32[]{:S(2)}) copy-start(bf16[8,352,256]{2,1,0:T(8,128)(2,1)} %get-tuple-element.60) | copy-start | bytes 4325380
  457.7 3.1 copy-start.1
  464.4 5.1 %copy-start.5 = (bf16[256,512]{1,0:T(8,128)(2,1)S(1)}, bf16[256,512]{1,0:T(8,128)(2,1)}, u32[]{:S(2)}) copy-start(bf16[256,512]{1,0:T(8,128)(2,1)} %get-tuple-element.90) | copy-start | bytes 786436
  464.4 5.8 %copy-start = (f32[768,512]{1,0:T(8,128)S(1)}, f32[768,512]{1,0:T(8,128)}, u32[]{:S(2)}) copy-start(f32[768,512]{1,0:T(8,128)} %get-tuple-element.56) | copy-start | bytes 4718596
  469.5 1.9 copy-start.4

commit v6 on v5

--- a/solution.py
+++ b/solution.py
@@ -442,6 +442,7 @@
 X_BIT, Y_BIT, CORE_BIT = 2, 4, 1
 QUARTERS = 4
 SMALL = 16
+EARLY = (2, 4)
 CUT = 1536
 
 
@@ -630,6 +631,46 @@
             out.wait_send()
 
 
+def grad_shapes(routed, shared, block):
+    return (
+        (E, 2 * routed, block),
+        (2, E * shared, block),
+        (E, routed, block),
+        (E * shared, block),
+    )
+
+
+def grad_pieces(grads, results, index, source):
+    up_all, shared_up_all, down_all, shared_down_all = results
+    routed, shared = down_all.shape[1], shared_down_all.shape[0] // E
+    units = pl.ds(pl.multiple_of(source * shared, 16), shared)
+    places = [
+        up_all.at[source],
+        shared_up_all.at[0, units],
+        shared_up_all.at[1, units],
+        down_all.at[source],
+        shared_down_all.at[units],
+    ]
+    placed, at = [], 0
+    for place, size in zip(places, (2 * routed, shared, shared, routed, shared), strict=True):
+        placed.append((grads.at[index, pl.ds(at, size)], place))
+        at += size
+    return placed
+
+
+def grad_copies(links, grads, results, bits):
+    peer = links.peer(bits)
+    pairs = zip(
+        grad_pieces(grads, results, peer, links.fs),
+        grad_pieces(grads, results, peer, peer),
+        strict=True,
+    )
+    return [
+        links.remote(piece, place, (peer, links.tp), landing)
+        for (piece, place), (_, landing) in pairs
+    ]
+
+
 def turn(values, cosine, sine_signed):
     parts = []
     for h in range(values.shape[1] // HD):
@@ -659,8 +700,58 @@
     return lax.dot_general(a, b, (((0,), (0,)), ((), ())), preferred_element_type=jnp.float32)
 
 
-def forward_kernel(
-    tokens_ref,
+class RowGather:
+    def __init__(self, links, source, slot, half):
+        self.links = links
+
+        def to(bits, owner, h=None):
+            view = slot if h is None else lambda k: half(k, h)
+            start = source if owner == 0 and source is not None else view(owner)
+            return links.remote(
+                start, view(owner ^ bits), (links.peer(bits), links.tp), view(owner ^ bits)
+            )
+
+        x, y, c = X_BIT, Y_BIT, CORE_BIT
+        self.keep = None if source is None else links.inside(source, slot(0))
+        self.own = [to(x, 0), to(y, 0), to(c, 0)]
+        self.x_on = [to(y, x, 0), to(c, x)]
+        self.y_on = [to(x, y, 1), to(c, y)]
+        self.d_on = [to(c, x + y, 0), to(c, x + y, 1)]
+
+    def first(self):
+        for out, back in self.own:
+            out.start()
+        if self.keep is not None:
+            self.keep.start()
+
+    def second(self):
+        self.own[0][1].wait_recv()
+        for out, back in self.x_on:
+            out.start()
+        self.own[1][1].wait_recv()
+        for out, back in self.y_on:
+            out.start()
+
+    def third(self):
+        self.x_on[0][1].wait_recv()
+        self.d_on[0][0].start()
+        self.y_on[0][1].wait_recv()
+        self.d_on[1][0].start()
+
+    def last(self):
+        if self.keep is not None:
+            self.keep.wait()
+        for out, back in (self.own[2], self.x_on[1], self.y_on[1], *self.d_on):
+            back.wait_recv()
+
+    def sent(self):
+        for out, back in self.own + self.x_on + self.y_on + self.d_on:
+            out.wait_send()
+
+
+def layer_kernel(
+    routed,
+    tokens_hbm,
     cotangent_ref,
     qkv_ref,
     out_ref,
@@ -675,12 +766,18 @@
     sin_ref,
     start_ref,
     routes_ref,
-    two_out,
-    residual_ref,
-    scales_ref,
-    attended_ref,
-    query_ref,
-    hidden_buf,
+    output_ref,
+    branch_ref,
+    back_ref,
+    small_grad_ref,
+    grads_out,
+    up_all,
+    shared_up_all,
+    down_all,
+    shared_down_all,
+    attended_out,
+    query_out,
+    hidden_out,
     slabs_all,
     cotangent_all,
     cotangent_plane,
@@ -688,32 +785,41 @@
     qkv_out,
     out_out,
     small_out,
-    qkv_full,
-    out_full,
     small_full,
-    kv_own,
-    kv_full,
-    branch_buf,
     branch_in,
     two_ref,
     small_ref,
+    scales_ref,
+    residual_ref,
+    two_all,
+    core_in,
+    diag_in,
+    side_in,
+    rows_in,
+    cols_in,
     send,
     recv,
     local,
+    credit,
 ):
     links = Links(send, recv, local)
     fs, tp = links.fs, links.tp
-    rows, width = tokens_ref.shape
+    rows, width = tokens_hbm.shape
     block = width // E
     local_width = qkv_ref.shape[2]
     heads = local_width // HD
     seqs = rows // SEQ_DEV
     quarter = rows // QUARTERS
+    out_width = output_ref.shape[1]
+    back_width = width + SIDE
+    whole = back_width + width
+    slab_rows = slabs_all.shape[1]
+    count = slab_rows // 3
+    bf, f32 = jnp.bfloat16, jnp.float32
 
     def at_rows(index, size):
         return pl.ds(pl.multiple_of(index * size, size), size)
 
-    f32 = jnp.float32
     small_ref[...] = jnp.concatenate(
         [
             gains_ref[...].astype(f32),
@@ -724,21 +830,6 @@
         axis=0,
     ).astype(jnp.bfloat16)
     links.greet(range(1, 8), range(1, QUARTERS))
-    small = Gather(
-        links, small_ref, lambda f: small_full.at[f], lambda f, h: small_full.at[f, :, pl.ds(h * 128, 128)]
-    )
-    qkv = Gather(
-        links,
-        qkv_ref,
-        lambda f: qkv_full.at[:, at_rows(f, block)],
-        lambda f, h: qkv_full.at[:, pl.ds(pl.multiple_of(f * block + h * (block // 2), block // 2), block // 2)],
-    )
-    outs = Gather(
-        links,
-        out_ref,
-        lambda f: out_full.at[f],
-        lambda f, h: out_full.at[f, pl.ds(h * (local_width // 2), local_width // 2)],
-    )
     cut = cotangent_all.shape[2]
     cot = CrossGather(
         links, cotangent_ref.at[at_rows(tp, quarter), pl.ds(0, cut)], cotangent_all
@@ -749,45 +840,7 @@
         lambda f: cotangent_plane.at[f],
         lambda f, h: cotangent_plane.at[f, pl.ds(h * SEQ_DEV, SEQ_DEV)],
     )
-    small.first()
-    cot.first()
-    qkv.first()
-    small.second()
-    small.third()
-    small.last()
-    cot.second()
-    tokens = tokens_ref[...].astype(jnp.float32)
-    rstd_one = lax.rsqrt(jnp.mean(tokens * tokens, axis=1, keepdims=True) + NORM_EPS)
-    for b in range(E):
-        cols = slice(b * block, (b + 1) * block)
-        gain = small_full[b, 0:1, :].astype(jnp.float32)
-        hidden_buf[:, cols] = (tokens[:, cols] * rstd_one * gain).astype(jnp.bfloat16)
-    cot.third()
-    qkv.second()
-    qkv.third()
-    outs.first()
-    cot_plane.first()
-    qkv.last()
-    hidden = hidden_buf[...]
-    cosine, sine = cos_ref[...], sin_ref[...]
-    kv_own[:, :local_width] = turn(matmul(hidden, qkv_full[1]), cosine, sine).astype(jnp.bfloat16)
-    kv_own[:, local_width:] = matmul(hidden, qkv_full[2]).astype(jnp.bfloat16)
-    kv = Gather(
-        links,
-        kv_own,
-        lambda f: kv_full.at[f],
-        lambda f, h: kv_full.at[f, pl.ds(h * SEQ_DEV, SEQ_DEV)],
-    )
-    kv.first()
-    qkv_keep = links.inside(qkv_full, qkv_out)
-    qkv_keep.start()
-    query_ref[...] = turn(matmul(hidden, qkv_full[0]), cosine, sine).astype(jnp.bfloat16)
-    outs.second()
-    kv.second()
-    outs.third()
-    kv.third()
-    cot_plane.second()
-    routed, shared = down_ref.shape[1], shared_down_ref.shape[0] // E
+    shared = shared_down_ref.shape[0] // E
 
     def slab(peer, where):
         units = pl.ds(pl.multiple_of(peer * shared, 16), shared)
@@ -809,114 +862,594 @@
         peer = links.peer(bits)
         for (piece, place), (_, landing) in zip(slab(peer, fs), slab(peer, peer), strict=True):
             slab_copies.append(links.remote(piece, place, (peer, tp), landing))
-    for out, back in slab_copies:
-        out.start()
     slab_own = [links.inside(piece, place) for piece, place in slab(fs, fs)]
-    for copy in slab_own:
-        copy.start()
-    kv.last()
-    kv_keep = links.inside(kv_full, kv_out)
-    kv_keep.start()
-    length = E * SEQ_DEV
-    key_pos = lax.broadcasted_iota(jnp.int32, (SEQ_DEV, length), 1)
-    query_pos = fs * SEQ_DEV + lax.broadcasted_iota(jnp.int32, (SEQ_DEV, length), 0)
-    for s in range(seqs):
-        here = slice(s * SEQ_DEV, (s + 1) * SEQ_DEV)
-        allowed = (key_pos <= query_pos) & (key_pos >= as_column(start_ref[s : s + 1, :]))
-        for h in range(heads):
-            cols = slice(h * HD, (h + 1) * HD)
-            vcols = slice(local_width + h * HD, local_width + (h + 1) * HD)
-            keys = kv_full[:, here, cols].reshape(length, HD)
-            values = kv_full[:, here, vcols].reshape(length, HD)
-            scores = matmul_nt(query_ref[here, cols], keys) * (HD ** (-0.5))
-            scores = jnp.where(allowed, scores, NEG_FILL)
-            top = jnp.max(scores, axis=1, keepdims=True)
-            weights = jnp.exp(scores - top)
-            weights = weights / jnp.sum(weights, axis=1, keepdims=True)
-            attended_ref[here, cols] = matmul(weights.astype(jnp.bfloat16), values).astype(
+    def slot(s, k, h=None):
+        start = (3 - k // 2) * quarter
+        size = quarter
+        if h is not None:
+            size = quarter // 2
+            start = start + h * size
+        return two_all.at[2 * s + 1 - k % 2, pl.ds(start, size)]
+
+    along = []
+    for step in range(1, QUARTERS):
+        along.append(
+            links.remote(two_ref, slot(step, 0), (fs, links.along(step)), slot(step, 0))
+        )
+    gathers = []
+    for s in range(QUARTERS):
+        gathers.append(
+            RowGather(
+                links,
+                two_ref if s == 0 else None,
+                lambda k, s=s: slot(s, k),
+                lambda k, h, s=s: slot(s, k, h),
+            )
+        )
+
+    def attention(
+        tokens_ref,
+        hidden_buf,
+        attended_ref,
+        query_ref,
+        qkv_full,
+        out_full,
+        kv_own,
+        kv_full,
+        branch_buf,
+    ):
+        load = links.inside(tokens_hbm, tokens_ref)
+        load.start()
+        small = Gather(
+            links, small_ref, lambda f: small_full.at[f], lambda f, h: small_full.at[f, :, pl.ds(h * 128, 128)]
+        )
+        qkv = Gather(
+            links,
+            qkv_ref,
+            lambda f: qkv_out.at[:, at_rows(f, block)],
+            lambda f, h: qkv_out.at[:, pl.ds(pl.multiple_of(f * block + h * (block // 2), block // 2), block // 2)],
+        )
+        outs = Gather(
+            links,
+            out_ref,
+            lambda f: out_out.at[f],
+            lambda f, h: out_out.at[f, pl.ds(h * (local_width // 2), local_width // 2)],
+        )
+        small.first()
+        cot.first()
+        qkv.first()
+        small.second()
+        small.third()
+        small.last()
+        cot.second()
+        load.wait()
+        tokens = tokens_ref[...].astype(jnp.float32)
+        rstd_one = lax.rsqrt(jnp.mean(tokens * tokens, axis=1, keepdims=True) + NORM_EPS)
+        for b in range(E):
+            cols = slice(b * block, (b + 1) * block)
+            gain = small_full[b, 0:1, :].astype(jnp.float32)
+            hidden_buf[:, cols] = (tokens[:, cols] * rstd_one * gain).astype(jnp.bfloat16)
+        cot.third()
+        qkv.second()
+        qkv.third()
+        outs.first()
+        cot_plane.first()
+        qkv.last()
+        qkv_load = links.inside(qkv_out, qkv_full)
+        qkv_load.start()
+        qkv_load.wait()
+        hidden = hidden_buf[...]
+        cosine, sine = cos_ref[...], sin_ref[...]
+        kv_own[:, :local_width] = turn(matmul(hidden, qkv_full[1]), cosine, sine).astype(jnp.bfloat16)
+        kv_own[:, local_width:] = matmul(hidden, qkv_full[2]).astype(jnp.bfloat16)
+        kv = Gather(
+            links,
+            kv_own,
+            lambda f: kv_out.at[f],
+            lambda f, h: kv_out.at[f, pl.ds(h * SEQ_DEV, SEQ_DEV)],
+        )
+        kv.first()
+        query_ref[...] = turn(matmul(hidden, qkv_full[0]), cosine, sine).astype(jnp.bfloat16)
+        outs.second()
+        kv.second()
+        outs.third()
+        kv.third()
+        cot_plane.second()
+        for out, back in slab_copies:
+            out.start()
+        for copy in slab_own:
+            copy.start()
+        kv.last()
+        kv_load = links.inside(kv_out, kv_full)
+        kv_load.start()
+        kv_load.wait()
+        length = E * SEQ_DEV
+        key_pos = lax.broadcasted_iota(jnp.int32, (SEQ_DEV, length), 1)
+        query_pos = fs * SEQ_DEV + lax.broadcasted_iota(jnp.int32, (SEQ_DEV, length), 0)
+        for s in range(seqs):
+            here = slice(s * SEQ_DEV, (s + 1) * SEQ_DEV)
+            allowed = (key_pos <= query_pos) & (key_pos >= as_column(start_ref[s : s + 1, :]))
+            for h in range(heads):
+                cols = slice(h * HD, (h + 1) * HD)
+                vcols = slice(local_width + h * HD, local_width + (h + 1) * HD)
+                keys = kv_full[:, here, cols].reshape(length, HD)
+                values = kv_full[:, here, vcols].reshape(length, HD)
+                scores = matmul_nt(query_ref[here, cols], keys) * (HD ** (-0.5))
+                scores = jnp.where(allowed, scores, NEG_FILL)
+                top = jnp.max(scores, axis=1, keepdims=True)
+                weights = jnp.exp(scores - top)
+                weights = weights / jnp.sum(weights, axis=1, keepdims=True)
+                attended_ref[here, cols] = matmul(weights.astype(jnp.bfloat16), values).astype(
+                    jnp.bfloat16
+                )
+        outs.last()
+        cot_plane.third()
+        out_load = links.inside(out_out, out_full)
+        out_load.start()
+        small_keep = links.inside(small_full, small_out)
+        small_keep.start()
+        out_load.wait()
+        attended = attended_ref[...]
+        for b in range(E):
+            branch_buf[:, b * block : (b + 1) * block] = matmul(attended, out_full[b]).astype(
                 jnp.bfloat16
             )
-    outs.last()
-    cot_plane.third()
-    out_keep = links.inside(out_full, out_out)
-    out_keep.start()
-    small_keep = links.inside(small_full, small_out)
-    small_keep.start()
-    attended = attended_ref[...]
-    for b in range(E):
-        branch_buf[:, b * block : (b + 1) * block] = matmul(attended, out_full[b]).astype(
+        branch = []
+        for step in range(1, QUARTERS):
+            peer = links.along(step)
+            branch.append(
+                links.remote(
+                    branch_buf.at[at_rows(peer, quarter)],
+                    branch_in.at[step - 1],
+                    (fs, peer),
+                    branch_in.at[step - 1],
+                )
+            )
+        for out, back in branch:
+            out.start()
+        for out, back in branch:
+            back.wait_recv()
+        mine = at_rows(tp, quarter)
+        total = branch_buf[mine, :].astype(jnp.float32)
+        for step in range(1, QUARTERS):
+            total = total + branch_in[step - 1].astype(jnp.float32)
+        residual = tokens_ref[mine, :].astype(jnp.float32) + total
+        residual_ref[...] = residual
+        rstd_two = lax.rsqrt(jnp.mean(residual * residual, axis=1, keepdims=True) + NORM_EPS)
+        logits = jnp.zeros((quarter, SMALL), jnp.float32)
+        for b in range(E):
+            cols = slice(b * block, (b + 1) * block)
+            gain = small_full[b, 1:2, :].astype(jnp.float32)
+            part = (residual[:, cols] * rstd_two * gain).astype(jnp.bfloat16)
+            two_ref[:, cols] = part
+            logits = logits + matmul_nt(part, small_full[b])
+        lane = lax.broadcasted_iota(jnp.int32, (quarter, SMALL), 1)
+        real = (lane >= 2) & (lane < 2 + E)
+        masked = jnp.where(real, logits, NEG_FILL)
+        odds = jnp.exp(masked - jnp.max(masked, axis=1, keepdims=True))
+        odds = jnp.where(real, odds, 0.0)
+        probs = odds / jnp.sum(odds, axis=1, keepdims=True)
+        expert = lax.broadcasted_iota(jnp.int32, (SMALL, rows), 0) - 2
+        named = jnp.zeros((SMALL, rows), jnp.float32)
+        for k in range(routes_ref.shape[0]):
+            named = named + (routes_ref[k : k + 1, :] == expert).astype(jnp.float32)
+        pick = lax.broadcasted_iota(jnp.int32, (quarter, rows), 1) == (
+            tp * quarter + lax.broadcasted_iota(jnp.int32, (quarter, rows), 0)
+        )
+        chosen = matmul_nt(pick.astype(jnp.bfloat16), named.astype(jnp.bfloat16))
+        gate_value = 1.0 / (1.0 + jnp.exp(-logits))
+        scales = jnp.where(lane == 2 + E, gate_value, probs * chosen)
+        scales_ref[...] = jnp.concatenate([scales, probs, chosen], axis=1)
+        high = scales.astype(jnp.bfloat16)
+        low = (scales - high.astype(jnp.float32)).astype(jnp.bfloat16)
+        two_ref[:, width:] = jnp.concatenate(
+            [high, low, jnp.zeros((quarter, SIDE - 2 * SMALL), jnp.bfloat16)], axis=1
+        )
+        keeps = [
+            links.inside(attended_ref, attended_out),
+            links.inside(query_ref, query_out),
+            links.inside(hidden_buf, hidden_out),
+            small_keep,
+        ]
+        for keep in keeps[:3]:
+            keep.start()
+        for out, back in along:
+            out.start()
+        for out, back in branch:
+            out.wait_send()
+        for keep in keeps:
+            keep.wait()
+
+    pl.run_scoped(
+        attention,
+        pltpu.VMEM((rows, width), bf),
+        pltpu.VMEM((rows, width), bf),
+        pltpu.VMEM((rows, local_width), bf),
+        pltpu.VMEM((rows, local_width), bf),
+        pltpu.VMEM((3, width, local_width), bf),
+        pltpu.VMEM((E, local_width, block), bf),
+        pltpu.VMEM((rows, 2 * local_width), bf),
+        pltpu.VMEM((E, rows, 2 * local_width), bf),
+        pltpu.VMEM((rows, width), bf),
+    )
+
+    def experts(weights, cot_all, units, first, parts, own_rows, own_cols, staged, cot_rows):
+        loads = [
+            links.inside(slabs_all.at[g], weights.at[:, pl.ds(g * block, block)]) for g in range(E)
+        ]
+        loads.append(links.inside(cotangent_all, cot_all.at[:, :, pl.ds(0, cut)]))
+        for s in range(QUARTERS):
+            q = links.along(QUARTERS - s)
+            for k in range(E):
+                there = cot_all.at[
+                    2 * s + 1 - k % 2, pl.ds((3 - k // 2) * quarter, quarter), pl.ds(cut, width - cut)
+                ]
+                loads.append(
+                    links.inside(cotangent_plane.at[links.peer(k), at_rows(q, quarter)], there)
+                )
+        along[0][1].wait_recv()
+        gathers[1].first()
+        along[1][1].wait_recv()
+        gathers[2].first()
+        gathers[1].second()
+        along[2][1].wait_recv()
+        gathers[3].first()
+        gathers[0].first()
+        cot.last()
+        cot_plane.last()
+        for out, back in slab_copies:
+            back.wait_recv()
+        for copy in slab_own:
+            copy.wait()
+        for load in loads:
+            load.start()
+
+        cot_load = links.inside(cotangent_ref.at[at_rows(tp, quarter)], cot_rows)
+        cot_load.start()
+        core = [
+            links.remote(
+                parts.at[s % 2], core_in.at[s % 2], (links.peer(CORE_BIT), tp), core_in.at[s % 2]
+            )
+            for s in range(QUARTERS)
+        ]
+        diag, side, rows_along, cols_along = [], [], [], []
+        for s in range(QUARTERS):
+            held = parts.at[2 + s % 3]
+            diag.append(
+                [
+                    links.remote(
+                        held.at[pl.ds(h * (quarter // 2), quarter // 2)],
+                        diag_in.at[s, h],
+                        (links.peer(bits), tp),
+                        diag_in.at[s, h],
+                    )
+                    for h, bits in enumerate((Y_BIT, X_BIT))
+                ]
+            )
+            side.append(
+                [
+                    links.remote(
+                        held.at[pl.ds((3 - bits // 2) * quarter, quarter)],
+                        side_in.at[s, i],
+                        (links.peer(bits), tp),
+                        side_in.at[s, i],
+                    )
+                    for i, bits in enumerate((X_BIT, Y_BIT))
+                ]
+            )
+            last = pl.ds(3 * quarter, quarter)
+            if s < QUARTERS - 1:
+                rows_along.append(
+                    links.remote(
+                        held.at[last, pl.ds(0, back_width)],
+                        rows_in.at[s],
+                        (fs, links.along(QUARTERS - 1 - s)),
+                        rows_in.at[s],
+                    )
+                )
+            q = links.along(2 * QUARTERS - 1 - s)
+            for step in range(1, QUARTERS):
+                peer = links.along(step)
+                start = pl.multiple_of(back_width + peer * out_width, 128)
+                q_there = links.along(2 * QUARTERS - 1 - s - step)
+                cols_along.append(
+                    links.remote(
+                        held.at[last, pl.ds(start, out_width)],
+                        cols_in.at[step - 1, at_rows(q, quarter)],
+                        (fs, peer),
+                        cols_in.at[step - 1, at_rows(q_there, quarter)],
+                    )
+                )
+
+        sub = lax.broadcasted_iota(jnp.int32, (8, SIDE), 0)
+        lane = lax.broadcasted_iota(jnp.int32, (8, SIDE), 1)
+        mine, common = 2 + fs, 2 + E
+        pick_in = (
+            ((sub == 0) & ((lane == mine) | (lane == mine + SMALL)))
+            | ((sub == 1) & ((lane == common) | (lane == common + SMALL)))
+        ).astype(jnp.bfloat16)
+        pick_out = (((sub == 0) & (lane == mine)) | ((sub == 1) & (lane == common))).astype(
             jnp.bfloat16
         )
-    branch = []
-    for step in range(1, QUARTERS):
-        peer = links.along(step)
-        branch.append(
-            links.remote(
-                branch_buf.at[at_rows(peer, quarter)],
-                branch_in.at[step - 1],
-                (fs, peer),
-                branch_in.at[step - 1],
+
+        def one_block(t, index, slot_out, pause):
+            first[: 2 * count] = matmul_nt(weights[: 2 * count], two_all[index, :, :width])
+            pause(0)
+            first[2 * count :] = matmul_nt(weights[2 * count :], cot_all[index])
+            scale = matmul_nt(pick_in, two_all[index, :, width:])
+            cols = pl.ds(pl.multiple_of(index * rows, rows), rows)
+            dots = []
+            shared = count - routed
+            groups = ((0, 2 * count, routed), (2 * routed, 2 * count + routed, shared))
+            for group, (low, last, size) in enumerate(groups):
+                gate = first[low : low + size]
+                up = first[low + size : low + 2 * size]
+                grad = first[last : last + size]
+                by = scale[group : group + 1]
+                sigmoid = 1.0 / (1.0 + jnp.exp(-gate))
+                silu = gate * sigmoid
+                active = silu * up
+                units[last : last + size, cols] = (by * active).astype(jnp.bfloat16)
+                dots.append(jnp.sum(active * grad, axis=0, keepdims=True))
+                active_grad = by * grad
+                units[low : low + size, cols] = (
+                    active_grad * up * sigmoid * (1.0 + gate * (1.0 - sigmoid))
+                ).astype(jnp.bfloat16)
+                units[low + size : low + 2 * size, cols] = (active_grad * silu).astype(jnp.bfloat16)
+            both = jnp.concatenate([*dots, jnp.zeros((6, rows), jnp.float32)], axis=0)
+            pause(1)
+            tile = 512
+
+            def put(at, value, other):
+                if other is not None:
+                    value = value + other[:, at].astype(jnp.float32)
+                parts[slot_out, :, at] = value.astype(jnp.bfloat16)
+
+            def products(other):
+                put(
+                    slice(width, back_width), matmul_tn(both.astype(jnp.bfloat16), pick_out), other
+                )
+                for n in range(width // tile):
+                    at = slice(n * tile, (n + 1) * tile)
+                    put(at, matmul_tn(units[: 2 * count, cols], weights[: 2 * count, at]), other)
+                    beyond = slice(back_width + n * tile, back_width + (n + 1) * tile)
+                    put(beyond, matmul_tn(units[2 * count :, cols], weights[2 * count :, at]), other)
+
+            @pl.when(t % 2 == 0)
+            def _():
+                products(None)
+
+            @pl.when(t % 2 == 1)
+            def _():
+                products(core_in.at[(t // 2) % 2])
+
+            pause(3)
+
+        def add_in(held, start, size, others):
+            chunk = 32
+
+            @pl.loop(0, size // chunk)
+            def _(r):
+                at = pl.ds(pl.multiple_of(start + r * chunk, chunk), chunk)
+                there = pl.ds(pl.multiple_of(r * chunk, chunk), chunk)
+                total = parts[held, at, :].astype(jnp.float32)
+                for ref in others:
+                    total = total + ref[there, :].astype(jnp.float32)
+                parts[held, at, :] = total.astype(jnp.bfloat16)
+
+        def to_core(s):
+            if s >= 2:
+                pl.semaphore_wait(credit, 1)
+            core[s][0].start()
+
+        def diagonal(s):
+            if s < 2:
+                pl.semaphore_signal(
+                    credit, inc=1, device_id=(links.peer(CORE_BIT), tp), device_id_type=MESH
+                )
+            for out, back in diag[s]:
+                out.start()
+
+        def sideways(s):
+            for h, (out, back) in enumerate(diag[s]):
+                back.wait_recv()
+                start = (2 - h) * quarter + h * (quarter // 2)
+                add_in(2 + s % 3, start, quarter // 2, [diag_in.at[s, h]])
+                side[s][h][0].start()
+
+        def finish(s):
+            held = 2 + s % 3
+            for out, back in side[s]:
+                back.wait_recv()
+            last = slice(3 * quarter, rows)
+            add_in(held, 3 * quarter, quarter, [side_in.at[s, 0], side_in.at[s, 1]])
+            if s == QUARTERS - 1:
+                own_rows[...] = parts[held, last, :back_width].astype(jnp.float32)
+                parts[held, last, back_width:] = (
+                    parts[held, last, back_width:].astype(jnp.float32) + residual_ref[...]
+                ).astype(jnp.bfloat16)
+            else:
+                rows_along[s][0].start()
+            for out, back in cols_along[3 * s : 3 * s + 3]:
+                out.start()
+            start = pl.multiple_of(back_width + tp * out_width, 128)
+            own_cols[at_rows(links.along(2 * QUARTERS - 1 - s), quarter), :] = parts[
+                held, last, pl.ds(start, out_width)
+            ].astype(jnp.float32)
+
+        def before_last():
+            core[1][0].wait_send()
+
+        def slot_free():
+            for out, back in diag[0] + side[0] + cols_along[:3] + rows_along[:1]:
+                out.wait_send()
+
+        plan = {
+            (0, 0): [gathers[2].third, gathers[3].second],
+            (0, 1): [gathers[0].second, gathers[3].third],
+            (0, 3): [lambda: to_core(0), gathers[2].last],
+            (1, 0): [gathers[0].third],
+            (1, 1): [core[0][1].wait_recv],
+            (1, 3): [lambda: diagonal(0), gathers[3].last],
+            (2, 1): [lambda: sideways(0)],
+            (2, 3): [lambda: to_core(1)],
+            (3, 1): [core[1][1].wait_recv],
+            (3, 3): [lambda: diagonal(1)],
+            (4, 1): [lambda: sideways(1)],
+            (4, 3): [lambda: to_core(2)],
+            (5, 0): [lambda: finish(0)],
+            (5, 1): [core[2][1].wait_recv],
+            (5, 3): [lambda: diagonal(2), gathers[0].last],
+            (6, 1): [lambda: sideways(2)],
+            (6, 3): [lambda: to_core(3)],
+            (7, 0): [lambda: finish(1)],
+            (7, 1): [core[3][1].wait_recv],
+            (7, 3): [lambda: diagonal(3)],
+        }
+        before = {4: [core[0][0].wait_send], 6: [before_last], 7: [slot_free]}
+
+        gathers[1].third()
+        gathers[2].second()
+        for load in loads:
+            load.wait()
+        gathers[1].last()
+
+        @pl.loop(0, 8)
+        def _(t):
+            s = t // 2
+            slot_out = (1 - t % 2) * (s % 2) + (t % 2) * (2 + s % 3)
+            for at, steps in before.items():
+
+                @pl.when(t == at)
+                def _(steps=steps):
+                    for step in steps:
+                        step()
+
+            def pause(point):
+                for (at, where), steps in plan.items():
+                    if where == point:
+
+                        @pl.when(t == at)
+                        def _(steps=steps):
+                            for step in steps:
+                                step()
+
+            one_block(t, 2 * ((s + 1) % QUARTERS) + t % 2, slot_out, pause)
+
+        keeps = []
+
+        pending = [None, None]
+
+        def settle(place):
+            if pending[place] is not None:
+                pending[place].wait()
+            pending[place] = None
+
+        def weight_grads(bits):
+            g = links.peer(bits)
+            at = pl.ds(pl.multiple_of(g * block, block), block)
+            place = len(keeps) % 2
+            settle(place)
+            hidden_cols = two_all[:, :, at].reshape(E * rows, block)
+            staged[place, : 2 * count] = matmul(units[: 2 * count], hidden_cols).astype(
+                jnp.bfloat16
             )
-        )
-    for out, back in branch:
-        out.start()
-    for out, back in branch:
-        back.wait_recv()
-    mine = at_rows(tp, quarter)
-    total = branch_buf[mine, :].astype(jnp.float32)
-    for step in range(1, QUARTERS):
-        total = total + branch_in[step - 1].astype(jnp.float32)
-    residual = tokens_ref[mine, :].astype(jnp.float32) + total
-    residual_ref[...] = residual
-    rstd_two = lax.rsqrt(jnp.mean(residual * residual, axis=1, keepdims=True) + NORM_EPS)
-    logits = jnp.zeros((quarter, SMALL), jnp.float32)
-    for b in range(E):
-        cols = slice(b * block, (b + 1) * block)
-        gain = small_full[b, 1:2, :].astype(jnp.float32)
-        part = (residual[:, cols] * rstd_two * gain).astype(jnp.bfloat16)
-        two_ref[:, cols] = part
-        logits = logits + matmul_nt(part, small_full[b])
-    lane = lax.broadcasted_iota(jnp.int32, (quarter, SMALL), 1)
-    routed = (lane >= 2) & (lane < 2 + E)
-    masked = jnp.where(routed, logits, NEG_FILL)
-    odds = jnp.exp(masked - jnp.max(masked, axis=1, keepdims=True))
-    odds = jnp.where(routed, odds, 0.0)
-    probs = odds / jnp.sum(odds, axis=1, keepdims=True)
-    expert = lax.broadcasted_iota(jnp.int32, (SMALL, rows), 0) - 2
-    named = jnp.zeros((SMALL, rows), jnp.float32)
-    for k in range(routes_ref.shape[0]):
-        named = named + (routes_ref[k : k + 1, :] == expert).astype(jnp.float32)
-    pick = lax.broadcasted_iota(jnp.int32, (quarter, rows), 1) == (
-        tp * quarter + lax.broadcasted_iota(jnp.int32, (quarter, rows), 0)
-    )
-    chosen = matmul_nt(pick.astype(jnp.bfloat16), named.astype(jnp.bfloat16))
-    gate_value = 1.0 / (1.0 + jnp.exp(-logits))
-    scales = jnp.where(lane == 2 + E, gate_value, probs * chosen)
-    scales_ref[...] = jnp.concatenate([scales, probs, chosen], axis=1)
-    high = scales.astype(jnp.bfloat16)
-    low = (scales - high.astype(jnp.float32)).astype(jnp.bfloat16)
-    two_ref[:, width:] = jnp.concatenate(
-        [high, low, jnp.zeros((quarter, SIDE - 2 * SMALL), jnp.bfloat16)], axis=1
-    )
-    two_keep = links.inside(two_ref, two_out.at[0])
-    two_keep.start()
-    two_along = []
-    for step in range(1, QUARTERS):
-        there = two_out.at[step]
-        two_along.append(links.remote(two_ref, there, (fs, links.along(step)), there))
-    for out, back in two_along:
-        out.start()
-    cot_plane.last()
-    cot.last()
-    for out, back in slab_copies + two_along:
-        back.wait_recv()
-    for out, back in slab_copies + branch + two_along:
-        out.wait_send()
-    for copy in (*slab_own, two_keep, qkv_keep, kv_keep, out_keep, small_keep):
-        copy.wait()
-
-
-def forward_call(
+            cot_cols = cot_all[:, :, at].reshape(E * rows, block)
+            staged[place, 2 * count :] = matmul(units[2 * count :], cot_cols).astype(jnp.bfloat16)
+            keep = links.inside(staged.at[place], grads_out.at[g])
+            keep.start()
+            keeps.append(keep)
+            pending[place] = keep
+
+        results = (up_all, shared_up_all, down_all, shared_down_all)
+        early = [copy for bits in EARLY for copy in grad_copies(links, grads_out, results, bits)]
+        finish(2)
+        for bits in EARLY:
+            weight_grads(bits)
+        sideways(3)
+        settle(0)
+        settle(1)
+        for out, back in early:
+            out.start()
+        for bits in (6, 7, 3, 5, 1, 0):
+            weight_grads(bits)
+        finish(3)
+        for out, back in rows_along:
+            back.wait_recv()
+        total = own_rows[...]
+        for step in range(1, QUARTERS):
+            total = total + rows_in[step - 1].astype(jnp.float32)
+        dots = total[:, width : width + SMALL]
+        scales = scales_ref[:, :SMALL]
+        probs = scales_ref[:, SMALL : 2 * SMALL]
+        chosen = scales_ref[:, 2 * SMALL :]
+        chosen_grad = chosen * dots
+        logit_grad = probs * (chosen_grad - jnp.sum(probs * chosen_grad, axis=1, keepdims=True))
+        gate_lane = lax.broadcasted_iota(jnp.int32, (quarter, SMALL), 1) == 2 + E
+        logit_grad = jnp.where(gate_lane, dots * scales * (1.0 - scales), logit_grad).astype(
+            jnp.bfloat16
+        )
+        residual = residual_ref[...]
+        rstd = lax.rsqrt(jnp.mean(residual * residual, axis=1, keepdims=True) + NORM_EPS)
+        mean = jnp.zeros((quarter, 1), jnp.float32)
+        for b in range(E):
+            at = slice(b * block, (b + 1) * block)
+            two_grad = total[:, at] + matmul(logit_grad, small_full[b])
+            normed = residual[:, at] * rstd
+            gain = small_full[b, 1:2, :].astype(jnp.float32)
+            back_ref[:, at] = two_grad
+            mean = mean + jnp.sum(two_grad * gain * normed, axis=1, keepdims=True)
+            grads = matmul_tn(logit_grad, two_all[1, 3 * quarter :, at])
+            line = lax.broadcasted_iota(jnp.int32, (SMALL, block), 0)
+            gain_grad = jnp.sum(two_grad * normed, axis=0, keepdims=True)
+            small_grad_ref[:, at] = jnp.where(line == 1, gain_grad, grads)
+        mean = mean / width
+        cot_load.wait()
+        for b in range(E):
+            at = slice(b * block, (b + 1) * block)
+            gain = small_full[b, 1:2, :].astype(jnp.float32)
+            normed = residual[:, at] * rstd
+            grad = cot_rows[:, at].astype(jnp.float32) + rstd * (
+                back_ref[:, at] * gain - normed * mean
+            )
+            back_ref[:, at] = grad
+            branch_ref[:, at] = grad.astype(jnp.bfloat16)
+        for out, back in cols_along:
+            back.wait_recv()
+        total = own_cols[...]
+        for step in range(1, QUARTERS):
+            total = total + cols_in[step - 1].astype(jnp.float32)
+        output_ref[...] = total.astype(jnp.bfloat16)
+        for out, back in core[2:] + rows_along[1:] + cols_along[3:]:
+            out.wait_send()
+        for s in range(1, QUARTERS):
+            for out, back in diag[s] + side[s]:
+                out.wait_send()
+        for gather in gathers:
+            gather.sent()
+        for out, back in slab_copies + along:
+            out.wait_send()
+        settle(0)
+        settle(1)
+        for out, back in early:
+            back.wait_recv()
+            out.wait_send()
+
+    pl.run_scoped(
+        experts,
+        pltpu.VMEM((slab_rows, width), bf),
+        pltpu.VMEM((E, rows, width), bf),
+        pltpu.VMEM((slab_rows, E * rows), bf),
+        pltpu.VMEM((slab_rows, rows), f32),
+        pltpu.VMEM((5, rows, whole), bf),
+        pltpu.VMEM((quarter, back_width), f32),
+        pltpu.VMEM((rows, out_width), f32),
+        pltpu.VMEM((2, slab_rows, block), bf),
+        pltpu.VMEM((quarter, width), bf),
+    )
+
+
+def layer_call(
     tokens,
     cotangent,
     qkv_weight,
@@ -937,18 +1470,26 @@
     block = width // E
     local_width = qkv_weight.shape[2]
     quarter = rows // QUARTERS
+    out_width = width // QUARTERS
+    back_width = width + SIDE
+    whole = back_width + width
+    routed = down.shape[1]
+    slabs = (E, 3 * (routed + shared_down.shape[0] // E), block)
     bf, f32 = jnp.bfloat16, jnp.float32
     sds = jax.ShapeDtypeStruct
     vmem = pl.BlockSpec(memory_space=pltpu.VMEM)
     hbm = pl.BlockSpec(memory_space=pl.ANY)
     outs = [
-        (sds((QUARTERS, quarter, width + SIDE), bf), hbm),
+        (sds((rows, out_width), bf), vmem),
+        (sds((quarter, width), bf), vmem),
         (sds((quarter, width), f32), vmem),
-        (sds((quarter, 3 * SMALL), f32), vmem),
-        (sds((rows, local_width), bf), vmem),
-        (sds((rows, local_width), bf), vmem),
-        (sds((rows, width), bf), vmem),
-        (sds((E, 3 * (down.shape[1] + shared_down.shape[0] // E), block), bf), hbm),
+        (sds((SMALL, width), f32), vmem),
+        (sds(slabs, bf), hbm),
+        *((sds(shape, bf), hbm) for shape in grad_shapes(routed, shared_down.shape[0] // E, block)),
+        (sds((rows, local_width), bf), hbm),
+        (sds((rows, local_width), bf), hbm),
+        (sds((rows, width), bf), hbm),
+        (sds(slabs, bf), hbm),
         (sds((E, rows, CUT), bf), hbm),
         (sds((E, rows, width - CUT), bf), hbm),
         (sds((E, rows, 2 * local_width), bf), hbm),
@@ -957,27 +1498,31 @@
         (sds((E, SMALL, block), bf), hbm),
     ]
     return pl.pallas_call(
-        forward_kernel,
-        name="attention_forward",
+        functools.partial(layer_kernel, routed),
+        name="layer",
         out_shape=[o[0] for o in outs],
-        in_specs=[vmem, hbm, hbm, hbm, vmem, vmem, vmem, hbm, hbm, hbm, hbm, vmem, vmem, vmem, vmem],
+        in_specs=[hbm] * 4 + [vmem] * 3 + [hbm] * 4 + [vmem] * 4,
         out_specs=[o[1] for o in outs],
         scratch_shapes=[
-            pltpu.VMEM((3, width, local_width), bf),
-            pltpu.VMEM((E, local_width, block), bf),
             pltpu.VMEM((E, SMALL, block), bf),
-            pltpu.VMEM((rows, 2 * local_width), bf),
-            pltpu.VMEM((E, rows, 2 * local_width), bf),
-            pltpu.VMEM((rows, width), bf),
             pltpu.VMEM((QUARTERS - 1, quarter, width), bf),
-            pltpu.VMEM((quarter, width + SIDE), bf),
+            pltpu.VMEM((quarter, back_width), bf),
             pltpu.VMEM((SMALL, block), bf),
-            pltpu.SemaphoreType.DMA((128,)),
-            pltpu.SemaphoreType.DMA((128,)),
-            pltpu.SemaphoreType.DMA((32,)),
+            pltpu.VMEM((quarter, 3 * SMALL), f32),
+            pltpu.VMEM((quarter, width), f32),
+            pltpu.VMEM((E, rows, back_width), bf),
+            pltpu.VMEM((2, rows, whole), bf),
+            pltpu.VMEM((QUARTERS, 2, quarter // 2, whole), bf),
+            pltpu.VMEM((QUARTERS, 2, quarter, whole), bf),
+            pltpu.VMEM((QUARTERS - 1, quarter, back_width), bf),
+            pltpu.VMEM((QUARTERS - 1, rows, out_width), bf),
+            pltpu.SemaphoreType.DMA((192,)),
+            pltpu.SemaphoreType.DMA((192,)),
+            pltpu.SemaphoreType.DMA((96,)),
+            pltpu.SemaphoreType.REGULAR,
         ],
         compiler_params=pltpu.CompilerParams(
-            collective_id=1, has_side_effects=True, vmem_limit_bytes=56 * 2**20
+            collective_id=1, has_side_effects=True, vmem_limit_bytes=63 * 2**20
         ),
     )(
         tokens,
@@ -998,501 +1543,7 @@
     )
 
 
-class RowGather:
-    def __init__(self, links, source, slot, half):
-        self.links = links
-
-        def to(bits, owner, h=None):
-            view = slot if h is None else lambda k: half(k, h)
-            start = source if owner == 0 and source is not None else view(owner)
-            return links.remote(
-                start, view(owner ^ bits), (links.peer(bits), links.tp), view(owner ^ bits)
-            )
-
-        x, y, c = X_BIT, Y_BIT, CORE_BIT
-        self.keep = None if source is None else links.inside(source, slot(0))
-        self.own = [to(x, 0), to(y, 0), to(c, 0)]
-        self.x_on = [to(y, x, 0), to(c, x)]
-        self.y_on = [to(x, y, 1), to(c, y)]
-        self.d_on = [to(c, x + y, 0), to(c, x + y, 1)]
-
-    def first(self):
-        for out, back in self.own:
-            out.start()
-        if self.keep is not None:
-            self.keep.start()
-
-    def second(self):
-        self.own[0][1].wait_recv()
-        for out, back in self.x_on:
-            out.start()
-        self.own[1][1].wait_recv()
-        for out, back in self.y_on:
-            out.start()
-
-    def third(self):
-        self.x_on[0][1].wait_recv()
-        self.d_on[0][0].start()
-        self.y_on[0][1].wait_recv()
-        self.d_on[1][0].start()
-
-    def last(self):
-        if self.keep is not None:
-            self.keep.wait()
-        for out, back in (self.own[2], self.x_on[1], self.y_on[1], *self.d_on):
-            back.wait_recv()
-
-    def sent(self):
-        for out, back in self.own + self.x_on + self.y_on + self.d_on:
-            out.wait_send()
-
-
-def expert_kernel(
-    routed,
-    two_ref,
-    router_ref,
-    residual_ref,
-    cotangent_ref,
-    cotangent_all,
-    cotangent_plane,
-    slabs_ref,
-    small_ref,
-    output_ref,
-    branch_ref,
-    back_ref,
-    small_grad_ref,
-    grads_out,
-    two_all,
-    cot_all,
-    weights,
-    units,
-    first,
-    parts,
-    core_in,
-    diag_in,
-    side_in,
-    rows_in,
-    cols_in,
-    own_rows,
-    own_cols,
-    staged,
-    send,
-    recv,
-    local,
-    credit,
-):
-    links = Links(send, recv, local)
-    fs, tp = links.fs, links.tp
-    quarter, width = residual_ref.shape
-    rows = quarter * QUARTERS
-    block = width // E
-    count = weights.shape[0] // 3
-    out_width = output_ref.shape[1]
-    back_width = width + SIDE
-
-    def at_rows(index, size):
-        return pl.ds(pl.multiple_of(index * size, size), size)
-
-    links.greet(range(1, 8), range(1, QUARTERS))
-
-    def slot(s, k, h=None):
-        start = (3 - k // 2) * quarter
-        size = quarter
-        if h is not None:
-            size = quarter // 2
-            start = start + h * size
-        return two_all.at[2 * s + 1 - k % 2, pl.ds(start, size)]
-
-    gathers = []
-    for s in range(QUARTERS):
-        gathers.append(
-            RowGather(
-                links,
-                two_ref.at[s],
-                lambda k, s=s: slot(s, k),
-                lambda k, h, s=s: slot(s, k, h),
-            )
-        )
-    gathers[0].first()
-    gathers[1].first()
-    loads = [
-        links.inside(slabs_ref.at[g], weights.at[:, pl.ds(g * block, block)]) for g in range(E)
-    ]
-    cut = cotangent_all.shape[2]
-    loads.append(links.inside(cotangent_all, cot_all.at[:, :, pl.ds(0, cut)]))
-    for s in range(QUARTERS):
-        q = links.along(QUARTERS - s)
-        for k in range(E):
-            there = cot_all.at[
-                2 * s + 1 - k % 2, pl.ds((3 - k // 2) * quarter, quarter), pl.ds(cut, width - cut)
-            ]
-            loads.append(
-                links.inside(cotangent_plane.at[links.peer(k), at_rows(q, quarter)], there)
-            )
-    for load in loads:
-        load.start()
-
-    core = [
-        links.remote(
-            parts.at[s % 2], core_in.at[s % 2], (links.peer(CORE_BIT), tp), core_in.at[s % 2]
-        )
-        for s in range(QUARTERS)
-    ]
-    diag, side, rows_along, cols_along = [], [], [], []
-    for s in range(QUARTERS):
-        held = parts.at[2 + s % 3]
-        diag.append(
-            [
-                links.remote(
-                    held.at[pl.ds(h * (quarter // 2), quarter // 2)],
-                    diag_in.at[s, h],
-                    (links.peer(bits), tp),
-                    diag_in.at[s, h],
-                )
-                for h, bits in enumerate((Y_BIT, X_BIT))
-            ]
-        )
-        side.append(
-            [
-                links.remote(
-                    held.at[pl.ds((3 - bits // 2) * quarter, quarter)],
-                    side_in.at[s, i],
-                    (links.peer(bits), tp),
-                    side_in.at[s, i],
-                )
-                for i, bits in enumerate((X_BIT, Y_BIT))
-            ]
-        )
-        last = pl.ds(3 * quarter, quarter)
-        if s:
-            rows_along.append(
-                links.remote(
-                    held.at[last, pl.ds(0, back_width)],
-                    rows_in.at[s - 1],
-                    (fs, links.along(QUARTERS - s)),
-                    rows_in.at[s - 1],
-                )
-            )
-        q = links.along(QUARTERS - s)
-        for step in range(1, QUARTERS):
-            peer = links.along(step)
-            start = pl.multiple_of(back_width + peer * out_width, 128)
-            q_there = links.along(2 * QUARTERS - s - step)
-            cols_along.append(
-                links.remote(
-                    held.at[last, pl.ds(start, out_width)],
-                    cols_in.at[step - 1, at_rows(q, quarter)],
-                    (fs, peer),
-                    cols_in.at[step - 1, at_rows(q_there, quarter)],
-                )
-            )
-
-    sub = lax.broadcasted_iota(jnp.int32, (8, SIDE), 0)
-    lane = lax.broadcasted_iota(jnp.int32, (8, SIDE), 1)
-    mine, common = 2 + fs, 2 + E
-    pick_in = (
-        ((sub == 0) & ((lane == mine) | (lane == mine + SMALL)))
-        | ((sub == 1) & ((lane == common) | (lane == common + SMALL)))
-    ).astype(jnp.bfloat16)
-    pick_out = (((sub == 0) & (lane == mine)) | ((sub == 1) & (lane == common))).astype(
-        jnp.bfloat16
-    )
-
-    def one_block(t, slot_out, pause):
-        first[: 2 * count] = matmul_nt(weights[: 2 * count], two_all[t, :, :width])
-        pause(0)
-        first[2 * count :] = matmul_nt(weights[2 * count :], cot_all[t])
-        scale = matmul_nt(pick_in, two_all[t, :, width:])
-        cols = pl.ds(pl.multiple_of(t * rows, rows), rows)
-        dots = []
-        shared = count - routed
-        groups = ((0, 2 * count, routed), (2 * routed, 2 * count + routed, shared))
-        for group, (low, last, size) in enumerate(groups):
-            gate = first[low : low + size]
-            up = first[low + size : low + 2 * size]
-            grad = first[last : last + size]
-            by = scale[group : group + 1]
-            sigmoid = 1.0 / (1.0 + jnp.exp(-gate))
-            silu = gate * sigmoid
-            active = silu * up
-            units[last : last + size, cols] = (by * active).astype(jnp.bfloat16)
-            dots.append(jnp.sum(active * grad, axis=0, keepdims=True))
-            active_grad = by * grad
-            units[low : low + size, cols] = (
-                active_grad * up * sigmoid * (1.0 + gate * (1.0 - sigmoid))
-            ).astype(jnp.bfloat16)
-            units[low + size : low + 2 * size, cols] = (active_grad * silu).astype(jnp.bfloat16)
-        both = jnp.concatenate([*dots, jnp.zeros((6, rows), jnp.float32)], axis=0)
-        parts[slot_out, :, width:back_width] = matmul_tn(
-            both.astype(jnp.bfloat16), pick_out
-        ).astype(jnp.bfloat16)
-        pause(1)
-        tile = 512
-        for n in range(width // tile):
-            at = slice(n * tile, (n + 1) * tile)
-            parts[slot_out, :, at] = matmul_tn(
-                units[: 2 * count, cols], weights[: 2 * count, at]
-            ).astype(jnp.bfloat16)
-            if n == 1:
-                pause(2)
-        for n in range(width // tile):
-            at = slice(n * tile, (n + 1) * tile)
-            beyond = slice(back_width + n * tile, back_width + (n + 1) * tile)
-            parts[slot_out, :, beyond] = matmul_tn(
-                units[2 * count :, cols], weights[2 * count :, at]
-            ).astype(jnp.bfloat16)
-        pause(3)
-
-    def add_in(held, start, size, others):
-        chunk = 32
-
-        @pl.loop(0, size // chunk)
-        def _(r):
-            at = pl.ds(pl.multiple_of(start + r * chunk, chunk), chunk)
-            there = pl.ds(pl.multiple_of(r * chunk, chunk), chunk)
-            total = parts[held, at, :].astype(jnp.float32)
-            for ref in others:
-                total = total + ref[there, :].astype(jnp.float32)
-            parts[held, at, :] = total.astype(jnp.bfloat16)
-
-    def to_core(s):
-        if s >= 2:
-            pl.semaphore_wait(credit, 1)
-        core[s][0].start()
-
-    def diagonal(s):
-        core[s][1].wait_recv()
-        add_in(2 + s % 3, 0, rows, [core_in.at[s % 2]])
-        if s < 2:
-            pl.semaphore_signal(
-                credit, inc=1, device_id=(links.peer(CORE_BIT), tp), device_id_type=MESH
-            )
-        for out, back in diag[s]:
-            out.start()
-
-    def sideways(s):
-        for h, (out, back) in enumerate(diag[s]):
-            back.wait_recv()
-            start = (2 - h) * quarter + h * (quarter // 2)
-            add_in(2 + s % 3, start, quarter // 2, [diag_in.at[s, h]])
-            side[s][h][0].start()
-
-    def finish(s):
-        held = 2 + s % 3
-        for out, back in side[s]:
-            back.wait_recv()
-        last = slice(3 * quarter, rows)
-        add_in(held, 3 * quarter, quarter, [side_in.at[s, 0], side_in.at[s, 1]])
-        if s == 0:
-            own_rows[...] = parts[held, last, :back_width].astype(jnp.float32)
-            parts[held, last, back_width:] = (
-                parts[held, last, back_width:].astype(jnp.float32) + residual_ref[...]
-            ).astype(jnp.bfloat16)
-        else:
-            rows_along[s - 1][0].start()
-        for out, back in cols_along[3 * s : 3 * s + 3]:
-            out.start()
-        start = pl.multiple_of(back_width + tp * out_width, 128)
-        own_cols[at_rows(links.along(QUARTERS - s), quarter), :] = parts[
-            held, last, pl.ds(start, out_width)
-        ].astype(jnp.float32)
-
-    def before_last():
-        core[1][0].wait_send()
-
-    def slot_free():
-        for out, back in diag[0] + side[0] + cols_along[:3]:
-            out.wait_send()
-
-    plan = {
-        (0, 0): [gathers[1].third, gathers[2].second],
-        (0, 1): [gathers[2].third],
-        (0, 2): [gathers[3].second],
-        (0, 3): [lambda: to_core(0), gathers[1].last],
-        (1, 0): [gathers[3].third],
-        (1, 3): [lambda: diagonal(0), gathers[2].last],
-        (2, 2): [lambda: sideways(0)],
-        (2, 3): [lambda: to_core(1)],
-        (3, 3): [lambda: diagonal(1), gathers[3].last],
-        (4, 2): [lambda: sideways(1)],
-        (4, 3): [lambda: to_core(2)],
-        (5, 0): [lambda: finish(0)],
-        (5, 3): [lambda: diagonal(2)],
-        (6, 2): [lambda: sideways(2)],
-        (6, 3): [lambda: to_core(3)],
-        (7, 0): [lambda: finish(1)],
-        (7, 3): [lambda: diagonal(3)],
-    }
-    before = {4: [core[0][0].wait_send], 6: [before_last], 7: [slot_free]}
-
-    gathers[0].second()
-    gathers[2].first()
-    gathers[0].third()
-    gathers[1].second()
-    gathers[3].first()
-    for load in loads:
-        load.wait()
-    gathers[0].last()
-
-    @pl.loop(0, 8)
-    def _(t):
-        s = t // 2
-        slot_out = (1 - t % 2) * (s % 2) + (t % 2) * (2 + s % 3)
-        for at, steps in before.items():
-
-            @pl.when(t == at)
-            def _(steps=steps):
-                for step in steps:
-                    step()
-
-        def pause(point):
-            for (at, where), steps in plan.items():
-                if where == point:
-
-                    @pl.when(t == at)
-                    def _(steps=steps):
-                        for step in steps:
-                            step()
-
-        one_block(t, slot_out, pause)
-
-    keeps = []
-
-    def weight_grads(g):
-        at = pl.ds(g * block, block)
-        if g >= 2:
-            keeps[g - 2].wait()
-        hidden_cols = two_all[:, :, at].reshape(E * rows, block)
-        staged[g % 2, : 2 * count] = matmul(units[: 2 * count], hidden_cols).astype(jnp.bfloat16)
-        cot_cols = cot_all[:, :, at].reshape(E * rows, block)
-        staged[g % 2, 2 * count :] = matmul(units[2 * count :], cot_cols).astype(jnp.bfloat16)
-        keep = links.inside(staged.at[g % 2], grads_out.at[g])
-        keep.start()
-        keeps.append(keep)
-
-    for g in range(3):
-        weight_grads(g)
-    sideways(3)
-    finish(2)
-    for g in range(3, E):
-        weight_grads(g)
-    finish(3)
-    for out, back in rows_along:
-        back.wait_recv()
-    total = own_rows[...]
-    for step in range(1, QUARTERS):
-        total = total + rows_in[step - 1].astype(jnp.float32)
-    dots = total[:, width : width + SMALL]
-    scales = router_ref[:, :SMALL]
-    probs = router_ref[:, SMALL : 2 * SMALL]
-    chosen = router_ref[:, 2 * SMALL :]
-    chosen_grad = chosen * dots
-    logit_grad = probs * (chosen_grad - jnp.sum(probs * chosen_grad, axis=1, keepdims=True))
-    gate_lane = lax.broadcasted_iota(jnp.int32, (quarter, SMALL), 1) == 2 + E
-    logit_grad = jnp.where(gate_lane, dots * scales * (1.0 - scales), logit_grad).astype(
-        jnp.bfloat16
-    )
-    residual = residual_ref[...]
-    rstd = lax.rsqrt(jnp.mean(residual * residual, axis=1, keepdims=True) + NORM_EPS)
-    mean = jnp.zeros((quarter, 1), jnp.float32)
-    for b in range(E):
-        at = slice(b * block, (b + 1) * block)
-        two_grad = total[:, at] + matmul(logit_grad, small_ref[b])
-        normed = residual[:, at] * rstd
-        gain = small_ref[b, 1:2, :].astype(jnp.float32)
-        back_ref[:, at] = two_grad
-        mean = mean + jnp.sum(two_grad * gain * normed, axis=1, keepdims=True)
-        grads = matmul_tn(logit_grad, two_all[1, 3 * quarter :, at])
-        line = lax.broadcasted_iota(jnp.int32, (SMALL, block), 0)
-        gain_grad = jnp.sum(two_grad * normed, axis=0, keepdims=True)
-        small_grad_ref[:, at] = jnp.where(line == 1, gain_grad, grads)
-    mean = mean / width
-    own = at_rows(tp, quarter)
-    for b in range(E):
-        at = slice(b * block, (b + 1) * block)
-        gain = small_ref[b, 1:2, :].astype(jnp.float32)
-        normed = residual[:, at] * rstd
-        grad = cotangent_ref[own, at].astype(jnp.float32) + rstd * (
-            back_ref[:, at] * gain - normed * mean
-        )
-        back_ref[:, at] = grad
-        branch_ref[:, at] = grad.astype(jnp.bfloat16)
-    for out, back in cols_along:
-        back.wait_recv()
-    total = own_cols[...]
-    for step in range(1, QUARTERS):
-        total = total + cols_in[step - 1].astype(jnp.float32)
-    output_ref[...] = total.astype(jnp.bfloat16)
-    for out, back in core[2:] + rows_along + cols_along[3:]:
-        out.wait_send()
-    for s in range(1, QUARTERS):
-        for out, back in diag[s] + side[s]:
-            out.wait_send()
-    for gather in gathers:
-        gather.sent()
-    for keep in keeps[-2:]:
-        keep.wait()
-
-
-def expert_call(
-    two_rows, router_rows, residual_rows, cotangent, cotangent_all, cotangent_plane, slabs, small_full, out_width, routed
-):
-    quarter, width = residual_rows.shape
-    rows = quarter * QUARTERS
-    back_width = width + SIDE
-    whole = back_width + width
-    block = width // E
-    bf, f32 = jnp.bfloat16, jnp.float32
-    sds = jax.ShapeDtypeStruct
-    vmem = pl.BlockSpec(memory_space=pltpu.VMEM)
-    hbm = pl.BlockSpec(memory_space=pl.ANY)
-    outs = [
-        (sds((rows, out_width), bf), vmem),
-        (sds((quarter, width), bf), vmem),
-        (sds((quarter, width), f32), vmem),
-        (sds((SMALL, width), f32), vmem),
-        (sds(slabs.shape, bf), hbm),
-    ]
-    units = slabs.shape[1]
-    return pl.pallas_call(
-        functools.partial(expert_kernel, routed),
-        name="experts",
-        out_shape=[o[0] for o in outs],
-        in_specs=[hbm, vmem, vmem, vmem, hbm, hbm, hbm, vmem],
-        out_specs=[o[1] for o in outs],
-        scratch_shapes=[
-            pltpu.VMEM((E, rows, back_width), bf),
-            pltpu.VMEM((E, rows, width), bf),
-            pltpu.VMEM((units, width), bf),
-            pltpu.VMEM((units, E * rows), bf),
-            pltpu.VMEM((units, rows), f32),
-            pltpu.VMEM((5, rows, whole), bf),
-            pltpu.VMEM((2, rows, whole), bf),
-            pltpu.VMEM((QUARTERS, 2, quarter // 2, whole), bf),
-            pltpu.VMEM((QUARTERS, 2, quarter, whole), bf),
-            pltpu.VMEM((QUARTERS - 1, quarter, back_width), bf),
-            pltpu.VMEM((QUARTERS - 1, rows, out_width), bf),
-            pltpu.VMEM((quarter, back_width), f32),
-            pltpu.VMEM((rows, out_width), f32),
-            pltpu.VMEM((2, units, block), bf),
-            pltpu.SemaphoreType.DMA((80,)),
-            pltpu.SemaphoreType.DMA((80,)),
-            pltpu.SemaphoreType.DMA((56,)),
-            pltpu.SemaphoreType.REGULAR,
-        ],
-        compiler_params=pltpu.CompilerParams(
-            collective_id=2, has_side_effects=True, vmem_limit_bytes=63 * 2**20
-        ),
-    )(
-        two_rows,
-        router_rows,
-        residual_rows,
-        cotangent,
-        cotangent_all,
-        cotangent_plane,
-        slabs,
-        small_full,
-    )
+LATE = 20
 
 
 class Scatter:
@@ -1585,6 +1636,10 @@
     sin_ref,
     start_ref,
     slabs_ref,
+    up_in,
+    shared_up_in,
+    down_in,
+    shared_down_in,
     input_grad_ref,
     qkv_own,
     out_own,
@@ -1647,31 +1702,13 @@
     for out, back in branch:
         out.start()
     branch_all[own, :] = branch_ref[...]
-    routed, shared = down_all.shape[1], shared_down_all.shape[0] // E
-
-    def slab(block_index, source):
-        units = pl.ds(pl.multiple_of(source * shared, 16), shared)
-        places = [
-            up_all.at[source],
-            shared_up_all.at[0, units],
-            shared_up_all.at[1, units],
-            down_all.at[source],
-            shared_down_all.at[units],
-        ]
-        placed, at = [], 0
-        for place, size in zip(places, (2 * routed, shared, shared, routed, shared), strict=True):
-            placed.append((slabs_ref.at[block_index, pl.ds(at, size)], place))
-            at += size
-        return placed
-
+    results = (up_all, shared_up_all, down_all, shared_down_all)
     slab_copies = []
-    for bits in (1, 6, 7, 2, 4, 3, 5):
-        peer = links.peer(bits)
-        for (piece, place), (_, landing) in zip(slab(peer, fs), slab(peer, peer), strict=True):
-            slab_copies.append(links.remote(piece, place, (peer, tp), landing))
-    for out, back in slab_copies[:25]:
+    for bits in (1, 6, 3, 5, 7):
+        slab_copies += grad_copies(links, slabs_ref, results, bits)
+    for out, back in slab_copies[:LATE]:
         out.start()
-    slab_own = [links.inside(piece, place) for piece, place in slab(fs, fs)]
+    slab_own = [links.inside(*pair) for pair in grad_pieces(slabs_ref, results, fs, fs)]
     for copy in slab_own:
         copy.start()
     kv_load = links.inside(kv_ref, kv_full)
@@ -1747,7 +1784,7 @@
     out_sum.diagonal()
     qkv_load.wait()
     kv_sum.finish(kv_total)
-    for out, back in slab_copies[25:]:
+    for out, back in slab_copies[LATE:]:
         out.start()
     projected[1] = turn(kv_total[:, :local_width], cos_ref[...], -sin_ref[...]).astype(jnp.bfloat16)
     projected[2] = kv_total[:, local_width:].astype(jnp.bfloat16)
@@ -1865,13 +1902,12 @@
     sine,
     start,
     slabs,
-    routed,
+    *parts,
 ):
     quarter, width = residual_grad.shape
     rows = quarter * QUARTERS
     block = width // E
     local_width = query_rows.shape[1]
-    shared = slabs.shape[1] // 3 - routed
     bf, f32 = jnp.bfloat16, jnp.float32
     sds = jax.ShapeDtypeStruct
     vmem = pl.BlockSpec(memory_space=pltpu.VMEM)
@@ -1881,10 +1917,7 @@
         (sds((3 * block, local_width), f32), vmem),
         (sds((local_width, block), f32), vmem),
         (sds((SMALL, block), f32), vmem),
-        (sds((E, 2 * routed, block), bf), hbm),
-        (sds((2, E * shared, block), bf), hbm),
-        (sds((E, routed, block), bf), hbm),
-        (sds((E * shared, block), bf), hbm),
+        *((sds(part.shape, bf), hbm) for part in parts),
     ]
 
     def scatter_scratch(count, columns):
@@ -1899,8 +1932,9 @@
         backward_kernel,
         name="attention_backward",
         out_shape=[o[0] for o in outs],
-        in_specs=[vmem] * 7 + [hbm] * 3 + [vmem] * 4 + [hbm],
+        in_specs=[vmem] * 7 + [hbm] * 3 + [vmem] * 4 + [hbm] * 5,
         out_specs=[o[1] for o in outs],
+        input_output_aliases={15 + i: 4 + i for i in range(4)},
         scratch_shapes=[
             pltpu.VMEM((E, rows, 2 * local_width), bf),
             pltpu.VMEM((3, width, local_width), bf),
@@ -1942,7 +1976,50 @@
         sine,
         start,
         slabs,
-    )
+        *parts,
+    )
+
+
+def finish_kernel(
+    up_ref, down_ref, shared_ref, grad_ref, qkv_ref, out_ref, output_ref, small_ref,
+    up, down, shared, grad, qkv, out, output, gains, router, gate,
+):
+    up[...] = up_ref[...].astype(jnp.float32)
+    down[...] = down_ref[...].astype(jnp.float32)
+    shared[...] = shared_ref[...].astype(jnp.float32)
+    grad[...] = grad_ref[...].astype(jnp.float32)
+    qkv[...] = qkv_ref[...]
+    out[...] = out_ref[...]
+    output[...] = output_ref[...]
+    gains[...] = small_ref[0:2, :]
+    router[...] = small_ref[2 : 2 + E, :]
+    gate[...] = small_ref[2 + E : 3 + E, :]
+
+
+def finish_call(up, down, shared, grad, qkv, out, output, small):
+    f32 = jnp.float32
+    sds = jax.ShapeDtypeStruct
+    block = small.shape[1]
+    arrays = (up, down, shared, grad, qkv, out, output)
+
+    def split(array):
+        shape = (array.shape[0] // E, *array.shape[1:])
+        return pl.BlockSpec(shape, lambda i: (i,) + (0,) * (len(shape) - 1))
+
+    def once(shape):
+        return pl.BlockSpec(shape, lambda i: (0, 0))
+
+    specs = [split(array) for array in arrays]
+    types = (f32, f32, f32, f32, f32, f32, output.dtype)
+    return pl.pallas_call(
+        finish_kernel,
+        name="finish",
+        grid=(E,),
+        out_shape=[sds(a.shape, t) for a, t in zip(arrays, types, strict=True)]
+        + [sds((n, block), f32) for n in (2, E, 1)],
+        in_specs=[*specs, once(small.shape)],
+        out_specs=[*specs, *(once((n, block)) for n in (2, E, 1))],
+    )(*arrays, small)
 
 
 def shards_units(
@@ -1970,20 +2047,26 @@
     sine = jnp.concatenate([-half_sin, half_sin], axis=1)
     routed_units = expert_down.shape[1]
     (
-        two_rows,
-        residual_rows,
-        router_rows,
+        output,
+        branch_rows,
+        residual_grad,
+        small_grad,
+        grad_slabs,
+        up_part,
+        shared_up_part,
+        down_part,
+        shared_down_part,
         attended,
         query_rows,
         hidden_one,
-        slabs,
-        cotangent_all,
-        cotangent_plane,
+        _,
+        _,
+        _,
         kv_all,
         qkv_full,
         out_full,
         small_full,
-    ) = forward_call(
+    ) = layer_call(
         tokens,
         cotangent,
         qkv_weight,
@@ -1999,18 +2082,6 @@
         sine,
         doc_start.reshape(seq_count, SEQ_DEV),
         routes.T,
-    )
-    output, branch_rows, residual_grad, small_grad, grad_slabs = expert_call(
-        two_rows,
-        router_rows,
-        residual_rows,
-        cotangent,
-        cotangent_all,
-        cotangent_plane,
-        slabs,
-        small_full,
-        width // QUARTERS,
-        routed_units,
     )
     input_grad, qkv_own, out_own, small_own, up_own, shared_up_own, down_own, shared_down_own = (
         backward_call(
@@ -2029,23 +2100,30 @@
             sine,
             doc_start.reshape(seq_count, SEQ_DEV),
             grad_slabs,
-            routed_units,
-        )
-    )
-    f32 = jnp.float32
+            up_part,
+            shared_up_part,
+            down_part,
+            shared_down_part,
+        )
+    )
+    up_own, down_own, shared_down_own, input_grad, qkv_own, out_own, output, gains, router, gate = (
+        finish_call(
+            up_own, down_own, shared_down_own, input_grad, qkv_own, out_own, output, small_own
+        )
+    )
     up_own = up_own.reshape(E, 2, routed_units, -1)
     return (
         output,
-        input_grad.astype(f32),
+        input_grad,
         qkv_own.reshape(qkv_weight.shape),
         out_own,
-        small_own[:2],
-        small_own[2 : 2 + E],
-        small_own[2 + E],
-        jnp.transpose(up_own, (0, 3, 1, 2)).astype(f32),
-        down_own.astype(f32),
-        jnp.transpose(shared_up_own, (2, 0, 1)).astype(f32),
-        shared_down_own.astype(f32),
+        gains,
+        router,
+        gate[0],
+        jnp.transpose(up_own, (0, 3, 1, 2)),
+        down_own,
+        jnp.transpose(shared_up_own, (2, 0, 1)).astype(jnp.float32),
+        shared_down_own,
     )
 
 

time: 480 us -> 449 us (0.935)
  Pallas kernels: 443 us -> 429 us
  other arithmetic: 12.5 us -> 2.97 us
  local copies, waits for them, and re-layouts: 16.1 us -> 9.43 us
    pallas_call x1, Pallas kernels: 139 us -> 125 us  [backward_call(): pl.pallas_call(backward_kernel, name='attention_backward', out_shape=[o[0...]
    convert_element_type x5 -> x1, other arithmetic: 11.2 us -> 1.58 us  [shards_units(): jnp.transpose(shared_up_own, (2, 0, 1)).astype(jnp.float32)]
    unnamed x17 -> x2, local copies, waits for them, and re-layouts: 10.9 us -> 8.21 us
where the time goes in v6:
time: 449 us; the launch traced here: 443 us
  Pallas kernels  429 us (96%)
  local copies, waits for them, and re-layouts  9.43 us (2%)
    pallas_call x1, Pallas kernels, layer_call(): pl.pallas_call(functools.partial(layer_kernel, routed), name='layer', out...  294 us
    pallas_call x1, Pallas kernels, backward_call(): pl.pallas_call(backward_kernel, name='attention_backward', out_shape=[o[0...  125 us
    pallas_call x1, Pallas kernels, finish_call(): pl.pallas_call(finish_kernel, name='finish', grid=(E,), out_shape=[sds(a....  9.95 us

profile of v6, /device:TPU:0, one launch (start us, length us, event | category | flops | bytes accessed | tf_op | source)
XLA Modules:
  0.0 442.7 jit_solution(4687472185293989504)
XLA Ops:
  0.7 1.2 broadcast_in_dim.2.gate_ref
  1.9 0.5 fusion
  2.4 0.8 pad_maximum_fusion
  3.3 4.8 %copy.28 = bf16[256,2,1408]{0,2,1:T(8,128)(2,1)} copy(bf16[256,2,1408]{2,1,0:T(2,128)(2,1)} %param.22) | data formatting | bytes 2883584 | tf_op args[9]
  8.1 294.3 %layer.1 = (bf16[256,512]{1,0:T(8,128)(2,1)}, bf16[64,2048]{1,0:T(8,128)(2,1)}, f32[64,2048]{1,0:T(8,128)}, f32[16,2048]{1,0:T(8,128)}, bf16[8,1584,256]{2,1,0:T...) custom-call(bf16[256,2048]{1,0:T(8,128)(2,1)} %tokens_ref.1, ...), custom_call_target="tpu_custom_call" | custom-call | tf_op jit(solution)/shard_map/layer/pallas_call | solution.py:1500
  302.3 124.8 %attention_backward.1 = (bf16[256,2048]{1,0:T(8,128)(2,1)}, f32[768,512]{1,0:T(8,128)}, f32[512,256]{1,0:T(8,128)}, f32[16,256]{1,0:T(8,128)}, bf16[8,704,256]{2...) custom-call(bf16[64,2048]{1,0:T(8,128)(2,1)} %get-tuple-element.45.b, ...), custom_call_target="tpu_custom_call", output_to_operand_aliasing={{4}: (15, {}), {5}: (16, {}), {6}: (17, {}), {7}: (18, {})} | custom-call | tf_op jit(solution)/shard_map/attention_backward/pallas_call | solution.py:1931
  427.2 1.6 convert_bitcast_fusion
  428.8 3.4 copy.29
  432.2 9.9 %finish.1 = (f32[8,704,256]{2,1,0:T(8,128)}, f32[8,352,256]{2,1,0:T(8,128)}, f32[1408,256]{1,0:T(8,128)}, f32[256,2048]{1,0:T(8,128)}, f32[768,512]{1,0:T(8,128)...) custom-call(bf16[8,704,256]{2,1,0:T(8,128)(2,1)} %get-tuple-element., ...), custom_call_target="tpu_custom_call" | custom-call | tf_op jit(solution)/shard_map/finish/pallas_call | solution.py:2014
  (3 shorter events, 0.0 us)

commit v7 on v6

--- a/solution.py
+++ b/solution.py
@@ -759,7 +759,7 @@
     router_ref,
     gate_ref,
     up_ref,
-    shared_up_ref,
+    shared_raw,
     down_ref,
     shared_down_ref,
     cos_ref,
@@ -785,6 +785,7 @@
     qkv_out,
     out_out,
     small_out,
+    shared_up_ref,
     small_full,
     branch_in,
     two_ref,
@@ -897,9 +898,13 @@
         kv_own,
         kv_full,
         branch_buf,
+        raw,
+        by_unit,
     ):
         load = links.inside(tokens_hbm, tokens_ref)
         load.start()
+        raw_load = links.inside(shared_raw, raw)
+        raw_load.start()
         small = Gather(
             links, small_ref, lambda f: small_full.at[f], lambda f, h: small_full.at[f, :, pl.ds(h * 128, 128)]
         )
@@ -929,6 +934,11 @@
             cols = slice(b * block, (b + 1) * block)
             gain = small_full[b, 0:1, :].astype(jnp.float32)
             hidden_buf[:, cols] = (tokens[:, cols] * rstd_one * gain).astype(jnp.bfloat16)
+        raw_load.wait()
+        for k in range(2):
+            by_unit[k] = raw[:, k, :].astype(f32).T.astype(bf)
+        unit_keep = links.inside(by_unit, shared_up_ref)
+        unit_keep.start()
         cot.third()
         qkv.second()
         qkv.third()
@@ -955,6 +965,7 @@
         outs.third()
         kv.third()
         cot_plane.second()
+        unit_keep.wait()
         for out, back in slab_copies:
             out.start()
         for copy in slab_own:
@@ -1071,6 +1082,8 @@
         pltpu.VMEM((rows, 2 * local_width), bf),
         pltpu.VMEM((E, rows, 2 * local_width), bf),
         pltpu.VMEM((rows, width), bf),
+        pltpu.VMEM(shared_raw.shape, bf),
+        pltpu.VMEM(shared_up_ref.shape, bf),
     )
 
     def experts(weights, cot_all, units, first, parts, own_rows, own_cols, staged, cot_rows):
@@ -1496,6 +1509,7 @@
         (sds((3, width, local_width), bf), hbm),
         (sds((E, local_width, block), bf), hbm),
         (sds((E, SMALL, block), bf), hbm),
+        (sds((2, shared_down.shape[0], block), bf), hbm),
     ]
     return pl.pallas_call(
         functools.partial(layer_kernel, routed),
@@ -1660,10 +1674,14 @@
     kv_core,
     kv_diag,
     kv_side,
-    qkv_parts,
-    qkv_core,
-    qkv_diag,
-    qkv_side,
+    query_parts,
+    query_core,
+    query_diag,
+    query_side,
+    rest_parts,
+    rest_core,
+    rest_diag,
+    rest_side,
     out_parts,
     out_core,
     out_diag,
@@ -1718,7 +1736,8 @@
     qkv_load = links.inside(qkv_ref, qkv_full)
     qkv_load.start()
     kv_sum = Scatter(links, kv_parts, kv_core, kv_diag, kv_side)
-    qkv_sum = Scatter(links, qkv_parts, qkv_core, qkv_diag, qkv_side)
+    query_sum = Scatter(links, query_parts, query_core, query_diag, query_side)
+    rest_sum = Scatter(links, rest_parts, rest_core, rest_diag, rest_side)
     out_sum = Scatter(links, out_parts, out_core, out_diag, out_side)
 
     kv_load.wait()
@@ -1768,20 +1787,23 @@
     for b in range(E):
         cols = slice(b * block, (b + 1) * block)
         out_parts[b] = matmul_tn(attended, branch_all[:, cols]).astype(jnp.bfloat16)
-    kv_sum.diagonal()
-    out_sum.to_core()
-
     def weight_grad(j):
         for b in range(E):
             cols = slice(b * block, (b + 1) * block)
-            qkv_parts[b, j * block : (j + 1) * block] = matmul_tn(
-                hidden_ref[:, cols], projected[j]
-            ).astype(jnp.bfloat16)
-
+            part = matmul_tn(hidden_ref[:, cols], projected[j]).astype(jnp.bfloat16)
+            if j == 0:
+                query_parts[b] = part
+            else:
+                rest_parts[b, (j - 1) * block : j * block] = part
+
+    kv_sum.diagonal()
+    out_sum.to_core()
     weight_grad(0)
+    query_sum.to_core()
     kv_sum.sideways(0)
     kv_sum.sideways(1)
     out_sum.diagonal()
+    query_sum.diagonal()
     qkv_load.wait()
     kv_sum.finish(kv_total)
     for out, back in slab_copies[LATE:]:
@@ -1809,12 +1831,12 @@
         out.start()
     weight_grad(1)
     weight_grad(2)
-    qkv_sum.to_core()
+    rest_sum.to_core()
     out_sum.sideways(0)
     out_sum.sideways(1)
-    qkv_sum.diagonal()
-    qkv_sum.sideways(0)
-    qkv_sum.sideways(1)
+    query_sum.sideways(0)
+    query_sum.sideways(1)
+    rest_sum.diagonal()
     for out, back in column:
         back.wait_recv()
     tokens = tokens_ref[own, :].astype(jnp.float32)
@@ -1858,7 +1880,10 @@
         )
     for out, back in small_copies:
         out.start()
+    rest_sum.sideways(0)
+    rest_sum.sideways(1)
     out_sum.finish(out_own)
+    query_sum.finish(qkv_own.at[pl.ds(0, block)])
     for out, back in small_copies:
         back.wait_recv()
     small_total = small_parts[fs]
@@ -1872,7 +1897,7 @@
         small_spread.append(links.remote(here, here, (fs, links.along(step)), landing))
     for out, back in small_spread:
         out.start()
-    qkv_sum.finish(qkv_own)
+    rest_sum.finish(qkv_own.at[pl.ds(block, 2 * block)])
     for out, back in small_spread:
         back.wait_recv()
     small_own[...] = small_column[0] + small_column[1] + small_column[2] + small_column[3]
@@ -1882,7 +1907,7 @@
         copy.wait()
     for out, back in branch + slab_copies + column + spread + small_copies + small_spread:
         out.wait_send()
-    for scatter in (kv_sum, out_sum, qkv_sum):
+    for scatter in (kv_sum, out_sum, query_sum, rest_sum):
         scatter.sent()
 
 
@@ -1945,7 +1970,8 @@
             pltpu.VMEM((3, rows, local_width), bf),
             pltpu.VMEM((rows, 2 * local_width), f32),
             *scatter_scratch(rows, 2 * local_width),
-            *scatter_scratch(3 * block, local_width),
+            *scatter_scratch(block, local_width),
+            *scatter_scratch(2 * block, local_width),
             *scatter_scratch(local_width, block),
             pltpu.VMEM((rows, width), bf),
             pltpu.VMEM((QUARTERS - 1, quarter, width), bf),
@@ -1981,8 +2007,26 @@
 
 
 def finish_kernel(
-    up_ref, down_ref, shared_ref, grad_ref, qkv_ref, out_ref, output_ref, small_ref,
-    up, down, shared, grad, qkv, out, output, gains, router, gate,
+    up_ref,
+    down_ref,
+    shared_ref,
+    grad_ref,
+    qkv_ref,
+    out_ref,
+    output_ref,
+    shared_up_ref,
+    small_ref,
+    up,
+    down,
+    shared,
+    grad,
+    qkv,
+    out,
+    output,
+    shared_up,
+    gains,
+    router,
+    gate,
 ):
     up[...] = up_ref[...].astype(jnp.float32)
     down[...] = down_ref[...].astype(jnp.float32)
@@ -1991,35 +2035,42 @@
     qkv[...] = qkv_ref[...]
     out[...] = out_ref[...]
     output[...] = output_ref[...]
+    for k in range(2):
+        shared_up[:, k, :] = shared_up_ref[k].astype(jnp.float32).T
     gains[...] = small_ref[0:2, :]
     router[...] = small_ref[2 : 2 + E, :]
     gate[...] = small_ref[2 + E : 3 + E, :]
 
 
-def finish_call(up, down, shared, grad, qkv, out, output, small):
+def finish_call(up, down, shared, grad, qkv, out, output, shared_up, small):
+    steps = 2
     f32 = jnp.float32
     sds = jax.ShapeDtypeStruct
     block = small.shape[1]
     arrays = (up, down, shared, grad, qkv, out, output)
-
-    def split(array):
-        shape = (array.shape[0] // E, *array.shape[1:])
-        return pl.BlockSpec(shape, lambda i: (i,) + (0,) * (len(shape) - 1))
+    shared_shape = (block, 2, shared_up.shape[1])
+
+    def split(shape):
+        part = (shape[0] // steps, *shape[1:])
+        return pl.BlockSpec(part, lambda i: (i,) + (0,) * (len(part) - 1))
 
     def once(shape):
         return pl.BlockSpec(shape, lambda i: (0, 0))
 
-    specs = [split(array) for array in arrays]
+    specs = [split(array.shape) for array in arrays]
+    turned = pl.BlockSpec((*shared_up.shape[:2], block // steps), lambda i: (0, 0, i))
     types = (f32, f32, f32, f32, f32, f32, output.dtype)
     return pl.pallas_call(
         finish_kernel,
         name="finish",
-        grid=(E,),
+        grid=(steps,),
         out_shape=[sds(a.shape, t) for a, t in zip(arrays, types, strict=True)]
+        + [sds(shared_shape, f32)]
         + [sds((n, block), f32) for n in (2, E, 1)],
-        in_specs=[*specs, once(small.shape)],
-        out_specs=[*specs, *(once((n, block)) for n in (2, E, 1))],
-    )(*arrays, small)
+        in_specs=[*specs, turned, once(small.shape)],
+        out_specs=[*specs, split(shared_shape), *(once((n, block)) for n in (2, E, 1))],
+        compiler_params=pltpu.CompilerParams(vmem_limit_bytes=60 * 2**20),
+    )(*arrays, shared_up, small)
 
 
 def shards_units(
@@ -2066,6 +2117,7 @@
         qkv_full,
         out_full,
         small_full,
+        _,
     ) = layer_call(
         tokens,
         cotangent,
@@ -2075,7 +2127,7 @@
         router_weight,
         shared_gate[None],
         jnp.transpose(expert_gate_up, (0, 2, 3, 1)).reshape(E, 2 * routed_units, -1),
-        jnp.transpose(shared_gate_up, (1, 2, 0)),
+        shared_gate_up,
         expert_down,
         shared_down,
         cosine,
@@ -2106,10 +2158,28 @@
             shared_down_part,
         )
     )
-    up_own, down_own, shared_down_own, input_grad, qkv_own, out_own, output, gains, router, gate = (
-        finish_call(
-            up_own, down_own, shared_down_own, input_grad, qkv_own, out_own, output, small_own
-        )
+    (
+        up_own,
+        down_own,
+        shared_down_own,
+        input_grad,
+        qkv_own,
+        out_own,
+        output,
+        shared_up_own,
+        gains,
+        router,
+        gate,
+    ) = finish_call(
+        up_own,
+        down_own,
+        shared_down_own,
+        input_grad,
+        qkv_own,
+        out_own,
+        output,
+        shared_up_own,
+        small_own,
     )
     up_own = up_own.reshape(E, 2, routed_units, -1)
     return (
@@ -2122,7 +2192,7 @@
         gate[0],
         jnp.transpose(up_own, (0, 3, 1, 2)),
         down_own,
-        jnp.transpose(shared_up_own, (2, 0, 1)).astype(jnp.float32),
+        shared_up_own,
         shared_down_own,
     )
 

time: 449 us -> 432 us (0.962)
  local copies, waits for them, and re-layouts: 9.43 us -> 1.22 us
  Pallas kernels: 429 us -> 421 us
    unnamed x2 -> x0, local copies, waits for them, and re-layouts: 8.21 us -> none
    pallas_call x1, Pallas kernels: 125 us -> 117 us  [backward_call(): pl.pallas_call(backward_kernel, name='attention_backward', out_shape=[o[0...]
where the time goes in v7:
time: 432 us; the launch traced here: 425 us
  Pallas kernels  421 us (97%)
    pallas_call x1, Pallas kernels, layer_call(): pl.pallas_call(functools.partial(layer_kernel, routed), name='layer', out...  294 us
    pallas_call x1, Pallas kernels, backward_call(): pl.pallas_call(backward_kernel, name='attention_backward', out_shape=[o[0...  117 us
    pallas_call x1, Pallas kernels, finish_call(): pl.pallas_call(finish_kernel, name='finish', grid=(steps,), out_shape=[sd...  9.61 us

profile of v7, /device:TPU:0, one launch (start us, length us, event | category | flops | bytes accessed | tf_op | source)
XLA Modules:
  0.0 424.9 jit_solution(4256774015047800639)
XLA Ops:
  0.7 1.2 broadcast_in_dim.2.gate_ref
  1.9 0.5 fusion
  2.4 0.8 pad_maximum_fusion
  3.3 294.2 %layer.1 = (bf16[256,512]{1,0:T(8,128)(2,1)}, bf16[64,2048]{1,0:T(8,128)(2,1)}, f32[64,2048]{1,0:T(8,128)}, f32[16,2048]{1,0:T(8,128)}, bf16[8,1584,256]{2,1,0:T...) custom-call(bf16[256,2048]{1,0:T(8,128)(2,1)} %tokens_ref.1, ...), custom_call_target="tpu_custom_call" | custom-call | tf_op jit(solution)/shard_map/layer/pallas_call | solution.py:1514
  297.5 117.5 %attention_backward.1 = (bf16[256,2048]{1,0:T(8,128)(2,1)}, f32[768,512]{1,0:T(8,128)}, f32[512,256]{1,0:T(8,128)}, f32[16,256]{1,0:T(8,128)}, bf16[8,704,256]{2...) custom-call(bf16[64,2048]{1,0:T(8,128)(2,1)} %get-tuple-element.46.b, ...), custom_call_target="tpu_custom_call", output_to_operand_aliasing={{4}: (15, {}), {5}: (16, {}), {6}: (17, {}), {7}: (18, {})} | custom-call | tf_op jit(solution)/shard_map/attention_backward/pallas_call | solution.py:1956
  415.0 9.6 %finish.1 = (f32[8,704,256]{2,1,0:T(8,128)}, f32[8,352,256]{2,1,0:T(8,128)}, f32[1408,256]{1,0:T(8,128)}, f32[256,2048]{1,0:T(8,128)}, f32[768,512]{1,0:T(8,128)...) custom-call(bf16[8,704,256]{2,1,0:T(8,128)(2,1)} %get-tuple-element., ...), custom_call_target="tpu_custom_call" | custom-call | tf_op jit(solution)/shard_map/finish/pallas_call | solution.py:2063
  (3 shorter events, 0.0 us)

commit v8 on v7

--- a/solution.py
+++ b/solution.py
@@ -825,7 +825,7 @@
         [
             gains_ref[...].astype(f32),
             router_ref[...].astype(f32),
-            gate_ref[...].astype(f32),
+            jnp.concatenate([gate_ref[0:1], gate_ref[1:2]], axis=1).astype(f32),
             jnp.zeros((SMALL - 3 - E, block), f32),
         ],
         axis=0,
@@ -1107,7 +1107,6 @@
         gathers[1].second()
         along[2][1].wait_recv()
         gathers[3].first()
-        gathers[0].first()
         cot.last()
         cot_plane.last()
         for out, back in slab_copies:
@@ -1299,25 +1298,19 @@
 
         plan = {
             (0, 0): [gathers[2].third, gathers[3].second],
-            (0, 1): [gathers[0].second, gathers[3].third],
-            (0, 3): [lambda: to_core(0), gathers[2].last],
-            (1, 0): [gathers[0].third],
-            (1, 1): [core[0][1].wait_recv],
-            (1, 3): [lambda: diagonal(0), gathers[3].last],
-            (2, 1): [lambda: sideways(0)],
-            (2, 3): [lambda: to_core(1)],
+            (0, 1): [gathers[3].third],
+            (0, 3): [lambda: to_core(0), gathers[0].first, gathers[2].last],
+            (1, 1): [core[0][1].wait_recv, gathers[0].second],
+            (1, 3): [gathers[0].third, lambda: diagonal(0), gathers[3].last],
+            (2, 3): [lambda: to_core(1), lambda: sideways(0)],
             (3, 1): [core[1][1].wait_recv],
             (3, 3): [lambda: diagonal(1)],
-            (4, 1): [lambda: sideways(1)],
-            (4, 3): [lambda: to_core(2)],
-            (5, 0): [lambda: finish(0)],
+            (4, 3): [lambda: to_core(2), lambda: sideways(1)],
             (5, 1): [core[2][1].wait_recv],
-            (5, 3): [lambda: diagonal(2), gathers[0].last],
-            (6, 1): [lambda: sideways(2)],
-            (6, 3): [lambda: to_core(3)],
-            (7, 0): [lambda: finish(1)],
+            (5, 3): [lambda: diagonal(2), gathers[0].last, lambda: finish(0)],
+            (6, 3): [lambda: to_core(3), lambda: sideways(2)],
             (7, 1): [core[3][1].wait_recv],
-            (7, 3): [lambda: diagonal(3)],
+            (7, 3): [lambda: diagonal(3), lambda: finish(1)],
         }
         before = {4: [core[0][0].wait_send], 6: [before_last], 7: [slot_free]}
 
@@ -1636,12 +1629,12 @@
 
 def backward_kernel(
     branch_ref,
-    residual_ref,
-    small_grad_ref,
-    attended_ref,
+    residual_hbm,
+    small_grad_hbm,
+    attended_hbm,
     query_ref,
-    hidden_ref,
-    tokens_ref,
+    hidden_hbm,
+    tokens_hbm,
     kv_ref,
     qkv_ref,
     out_ref,
@@ -1692,6 +1685,11 @@
     small_parts,
     small_in,
     small_column,
+    residual_ref,
+    small_grad_ref,
+    attended_ref,
+    hidden_ref,
+    token_rows,
     send,
     recv,
     local,
@@ -1735,6 +1733,15 @@
     out_load.start()
     qkv_load = links.inside(qkv_ref, qkv_full)
     qkv_load.start()
+    operand_loads = [
+        links.inside(attended_hbm, attended_ref),
+        links.inside(hidden_hbm, hidden_ref),
+        links.inside(residual_hbm, residual_ref),
+        links.inside(small_grad_hbm, small_grad_ref),
+        links.inside(tokens_hbm.at[own], token_rows),
+    ]
+    for load in operand_loads:
+        load.start()
     kv_sum = Scatter(links, kv_parts, kv_core, kv_diag, kv_side)
     query_sum = Scatter(links, query_parts, query_core, query_diag, query_side)
     rest_sum = Scatter(links, rest_parts, rest_core, rest_diag, rest_side)
@@ -1783,6 +1790,8 @@
                 matmul(score_grad, keys) * scale, cos_ref[here, :], -sin_ref[here, :]
             ).astype(jnp.bfloat16)
     kv_sum.to_core()
+    for load in operand_loads:
+        load.wait()
     attended = attended_ref[...]
     for b in range(E):
         cols = slice(b * block, (b + 1) * block)
@@ -1839,7 +1848,7 @@
     rest_sum.diagonal()
     for out, back in column:
         back.wait_recv()
-    tokens = tokens_ref[own, :].astype(jnp.float32)
+    tokens = token_rows[...].astype(jnp.float32)
     rstd = lax.rsqrt(jnp.mean(tokens * tokens, axis=1, keepdims=True) + NORM_EPS)
     total = one_parts[own, :].astype(jnp.float32)
     for step in range(1, QUARTERS):
@@ -1957,7 +1966,7 @@
         backward_kernel,
         name="attention_backward",
         out_shape=[o[0] for o in outs],
-        in_specs=[vmem] * 7 + [hbm] * 3 + [vmem] * 4 + [hbm] * 5,
+        in_specs=[vmem] + [hbm] * 3 + [vmem] + [hbm] * 5 + [vmem] * 4 + [hbm] * 5,
         out_specs=[o[1] for o in outs],
         input_output_aliases={15 + i: 4 + i for i in range(4)},
         scratch_shapes=[
@@ -1979,6 +1988,11 @@
             pltpu.VMEM((E, SMALL, block), f32),
             pltpu.VMEM((E - 1, SMALL, block), f32),
             pltpu.VMEM((QUARTERS, SMALL, block), f32),
+            pltpu.VMEM((quarter, width), f32),
+            pltpu.VMEM((SMALL, width), f32),
+            pltpu.VMEM((rows, local_width), bf),
+            pltpu.VMEM((rows, width), bf),
+            pltpu.VMEM((quarter, width), bf),
             pltpu.SemaphoreType.DMA((96,)),
             pltpu.SemaphoreType.DMA((96,)),
             pltpu.SemaphoreType.DMA((16,)),
@@ -2125,7 +2139,7 @@
         out_weight,
         norm_gains,
         router_weight,
-        shared_gate[None],
+        shared_gate.reshape(2, -1),
         jnp.transpose(expert_gate_up, (0, 2, 3, 1)).reshape(E, 2 * routed_units, -1),
         shared_gate_up,
         expert_down,

time: 432 us -> 420 us (0.972)
  Pallas kernels: 421 us -> 411 us
    pallas_call x1, Pallas kernels: 294 us -> 286 us  [layer_call(): pl.pallas_call(functools.partial(layer_kernel, routed), name='layer', out...]
where the time goes in v8:
time: 420 us; the launch traced here: 414 us
  Pallas kernels  411 us (98%)
    pallas_call x1, Pallas kernels, layer_call(): pl.pallas_call(functools.partial(layer_kernel, routed), name='layer', out...  286 us
    pallas_call x1, Pallas kernels, backward_call(): pl.pallas_call(backward_kernel, name='attention_backward', out_shape=[o[0...  116 us
    pallas_call x1, Pallas kernels, finish_call(): pl.pallas_call(finish_kernel, name='finish', grid=(steps,), out_shape=[sd...  9.61 us

profile of v8, /device:TPU:0, one launch (start us, length us, event | category | flops | bytes accessed | tf_op | source)
XLA Modules:
  0.0 413.5 jit_solution(15153056272964417722)
XLA Ops:
  0.7 0.5 fusion
  1.2 0.8 pad_maximum_fusion
  2.1 285.6 %layer.1 = (bf16[256,512]{1,0:T(8,128)(2,1)}, bf16[64,2048]{1,0:T(8,128)(2,1)}, f32[64,2048]{1,0:T(8,128)}, f32[16,2048]{1,0:T(8,128)}, bf16[8,1584,256]{2,1,0:T...) custom-call(bf16[256,2048]{1,0:T(8,128)(2,1)} %tokens_hbm.3, ...), custom_call_target="tpu_custom_call" | custom-call | tf_op jit(solution)/shard_map/layer/pallas_call | solution.py:1507
  287.7 115.9 %attention_backward.1 = (bf16[256,2048]{1,0:T(8,128)(2,1)}, f32[768,512]{1,0:T(8,128)}, f32[512,256]{1,0:T(8,128)}, f32[16,256]{1,0:T(8,128)}, bf16[8,704,256]{2...) custom-call(bf16[64,2048]{1,0:T(8,128)(2,1)} %get-tuple-element.46.b, ...), custom_call_target="tpu_custom_call", output_to_operand_aliasing={{4}: (15, {}), {5}: (16, {}), {6}: (17, {}), {7}: (18, {})} | custom-call | tf_op jit(solution)/shard_map/attention_backward/pallas_call | solution.py:1965
  403.6 9.6 %finish.1 = (f32[8,704,256]{2,1,0:T(8,128)}, f32[8,352,256]{2,1,0:T(8,128)}, f32[1408,256]{1,0:T(8,128)}, f32[256,2048]{1,0:T(8,128)}, f32[768,512]{1,0:T(8,128)...) custom-call(bf16[8,704,256]{2,1,0:T(8,128)(2,1)} %get-tuple-element., ...), custom_call_target="tpu_custom_call" | custom-call | tf_op jit(solution)/shard_map/finish/pallas_call | solution.py:2077
  (3 shorter events, 0.0 us)

commit v9 on v8

--- a/solution.py
+++ b/solution.py
@@ -1109,11 +1109,13 @@
         gathers[3].first()
         cot.last()
         cot_plane.last()
+        for load in loads[E:]:
+            load.start()
         for out, back in slab_copies:
             back.wait_recv()
         for copy in slab_own:
             copy.wait()
-        for load in loads:
+        for load in loads[:E]:
             load.start()
 
         cot_load = links.inside(cotangent_ref.at[at_rows(tp, quarter)], cot_rows)

time: 420 us -> 420 us (level)
  no operation moved by 1% of the time
where the time goes in v9:
time: 420 us; the launch traced here: 413 us
  Pallas kernels  411 us (98%)
    pallas_call x1, Pallas kernels, layer_call(): pl.pallas_call(functools.partial(layer_kernel, routed), name='layer', out...  286 us
    pallas_call x1, Pallas kernels, backward_call(): pl.pallas_call(backward_kernel, name='attention_backward', out_shape=[o[0...  116 us
    pallas_call x1, Pallas kernels, finish_call(): pl.pallas_call(finish_kernel, name='finish', grid=(steps,), out_shape=[sd...  9.61 us

profile of v9, /device:TPU:0, one launch (start us, length us, event | category | flops | bytes accessed | tf_op | source)
XLA Modules:
  0.0 413.3 jit_solution(16241005699340796804)
XLA Ops:
  0.7 0.5 fusion
  1.2 0.8 pad_maximum_fusion
  2.1 285.6 %layer.1 = (bf16[256,512]{1,0:T(8,128)(2,1)}, bf16[64,2048]{1,0:T(8,128)(2,1)}, f32[64,2048]{1,0:T(8,128)}, f32[16,2048]{1,0:T(8,128)}, bf16[8,1584,256]{2,1,0:T...) custom-call(bf16[256,2048]{1,0:T(8,128)(2,1)} %tokens_hbm.3, ...), custom_call_target="tpu_custom_call" | custom-call | tf_op jit(solution)/shard_map/layer/pallas_call | solution.py:1509
  287.6 115.8 %attention_backward.1 = (bf16[256,2048]{1,0:T(8,128)(2,1)}, f32[768,512]{1,0:T(8,128)}, f32[512,256]{1,0:T(8,128)}, f32[16,256]{1,0:T(8,128)}, bf16[8,704,256]{2...) custom-call(bf16[64,2048]{1,0:T(8,128)(2,1)} %get-tuple-element.46.b, ...), custom_call_target="tpu_custom_call", output_to_operand_aliasing={{4}: (15, {}), {5}: (16, {}), {6}: (17, {}), {7}: (18, {})} | custom-call | tf_op jit(solution)/shard_map/attention_backward/pallas_call | solution.py:1967
  403.5 9.6 %finish.1 = (f32[8,704,256]{2,1,0:T(8,128)}, f32[8,352,256]{2,1,0:T(8,128)}, f32[1408,256]{1,0:T(8,128)}, f32[256,2048]{1,0:T(8,128)}, f32[768,512]{1,0:T(8,128)...) custom-call(bf16[8,704,256]{2,1,0:T(8,128)(2,1)} %get-tuple-element., ...), custom_call_target="tpu_custom_call" | custom-call | tf_op jit(solution)/shard_map/finish/pallas_call | solution.py:2079
  (3 shorter events, 0.0 us)
